TPU v7x, 32 devices: a whole 2x2x4 slice. The times are simulated.
32 devices in a mesh: weight: 2 (over y), context: 4 (over z), tensor: 4 (over x, core).
Axes of the slice: x: 2, y: 2, z: 4, core: 2. Of those that a mesh axis runs over, the one named last changes fastest.
Arguments:
- tokens: bfloat16 [2048, 768], P(('weight', 'context')), may hold values from -6 to 6
- segments: int32 [2048], P(('weight', 'context')), may hold values from 0 to 4, as said below
- query_key_value_weight: bfloat16 [1, 768, 3, 768], P(None, 'weight', None, 'tensor'), may hold values from -0.3125 to 0.3125
- input_bias: float32 [1, 2, 768], P(None, None, 'tensor'), may hold values from -3 to 3
- output_weight: bfloat16 [1, 768, 768], P(None, 'tensor', 'weight'), may hold values from -0.875 to 0.875
- row_bias: float32 [1, 2, 768], replicated, may hold values from -2 to 2
- norm_gain: float32 [1, 2, 768], replicated, may hold values from 0.5 to 1.5
- norm_bias: float32 [1, 2, 768], replicated, may hold values from -2 to 2
- up_weight: bfloat16 [1, 768, 3072], P(None, 'weight', 'tensor'), may hold values from -0.21875 to 0.21875
- up_bias: float32 [1, 3072], P(None, 'tensor'), may hold values from -3 to 3
- down_weight: bfloat16 [1, 3072, 768], P(None, 'tensor', 'weight'), may hold values from -0.109375 to 0.109375
- cotangent: bfloat16 [2048, 768], P(('weight', 'context')), may hold values from -6 to 6
Outputs:
- layer_output: bfloat16 [2048, 768], P(('weight', 'context'))
- grad_tokens: float32 [2048, 768], P(('weight', 'context'))
- grad_input_weight: float32 [1, 768, 3, 768], P(None, 'weight', None, 'tensor')
- grad_input_bias: float32 [1, 2, 768], P(None, None, 'tensor')
- grad_output_weight: float32 [1, 768, 768], P(None, 'tensor', 'weight')
- grad_row_bias: float32 [1, 2, 768], replicated
- grad_norm_gain: float32 [1, 2, 768], replicated
- grad_norm_bias: float32 [1, 2, 768], replicated
- grad_up_weight: float32 [1, 768, 3072], P(None, 'weight', 'tensor')
- grad_up_bias: float32 [1, 3072], P(None, 'tensor')
- grad_down_weight: float32 [1, 3072, 768], P(None, 'tensor', 'weight')
Inputs may be any that keep to these rules, and one draw needn't show every extreme that they name: `segments`: within each pack of 1024 tokens the numbers never fall and each of 0 to 4 occurs; number 2 holds tokens among the first 256 and among the last 256 of the pack. Only tokens of one pack with equal numbers attend to each other.
All inputs are finite; a program needn't handle non-finite values.
Results may differ from a plain program's by a relative error of at most 0.013.
The roundings to bfloat16 on the way count: a program that leaves them out, or rounds other values in their place, can miss the bound.
Values may be sent and summed in bfloat16 or wider, within the bound.
No kernel may reach another device: no remote copies, remote signals or barrier semaphores. Data moves between devices by JAX's collectives and lax.ppermute only.
A program may use at most 64 MiB of HBM per device.

v0:
```python
import jax
import jax.numpy as jnp
from jax import lax
from jax.sharding import PartitionSpec as P

HD = 64


EPSILON = 1e-05
NEG_FILL = -1e30
ROOT_HALF = 0.7071067811865476
DENSITY_FACTOR = 0.3989422804014327


def product(left, right):
    return jnp.dot(left, right, preferred_element_type=jnp.float32)


def product_left(left, right):
    return lax.dot_general(
        left, right, (((0,), (0,)), ((), ())), preferred_element_type=jnp.float32
    )


def product_right(left, right):
    return lax.dot_general(
        left, right, (((1,), (1,)), ((), ())), preferred_element_type=jnp.float32
    )


def tensor_total(partial_rows):
    return lax.psum(partial_rows, "tensor")


def reduce_heads(partial_rows):
    return tensor_total(partial_rows)


def normalize(summed, gain_vector, shift_vector):
    center = summed - jnp.mean(summed, axis=-1, keepdims=True)
    inverse = lax.rsqrt(jnp.mean(center * center, axis=-1, keepdims=True) + EPSILON)
    normed = center * inverse
    return (normed * gain_vector + shift_vector, normed, inverse)


def normalize_back(grad_output, normed, inverse, gain_vector):
    scaled = grad_output * gain_vector
    grad_summed = inverse * (
        scaled
        - jnp.mean(scaled, axis=-1, keepdims=True)
        - normed * jnp.mean(scaled * normed, axis=-1, keepdims=True)
    )
    return (grad_summed, jnp.sum(grad_output * normed, axis=0), jnp.sum(grad_output, axis=0))


def attention_scores(query_heads, key_heads, segments, key_segments):
    scores = jnp.einsum(
        "qhe,khe->hqk", query_heads, key_heads, preferred_element_type=jnp.float32
    ) * HD ** (-0.5)
    same_doc = segments[:, None] == key_segments[None, :]
    return jnp.where(same_doc[None], scores, NEG_FILL)


def forward_layer(
    hidden_state,
    hidden_low,
    segments,
    pieces,
    bias_pair,
    row_pair,
    gain_pair,
    shift_pair,
    hidden_bias,
):
    input_full, output_full, up_full, down_full = pieces
    model_width, shard_width = (input_full.shape[0], input_full.shape[2])
    local_heads = shard_width // HD
    count_of_rows = hidden_low.shape[0]
    projected_rows = product(hidden_low, input_full.reshape(model_width, 3 * shard_width))
    queries = (projected_rows[:, :shard_width] + bias_pair[0]).astype(jnp.bfloat16)
    key_value_rows = jnp.concatenate(
        [
            projected_rows[:, shard_width : 2 * shard_width],
            projected_rows[:, 2 * shard_width :] + bias_pair[1],
        ],
        axis=1,
    ).astype(jnp.bfloat16)
    gathered_rows, key_segments = (
        lax.all_gather(key_value_rows, "context", axis=0, tiled=True),
        lax.all_gather(segments, "context", axis=0, tiled=True),
    )
    key_count = gathered_rows.shape[0]
    query_heads = queries.reshape(count_of_rows, local_heads, HD)
    key_heads = gathered_rows[:, :shard_width].reshape(key_count, local_heads, HD)
    value_heads = gathered_rows[:, shard_width:].reshape(key_count, local_heads, HD)
    scores = attention_scores(query_heads, key_heads, segments, key_segments)
    row_max = jnp.max(scores, axis=-1, keepdims=True)
    exponent = jnp.exp(scores - row_max)
    row_total = jnp.sum(exponent, axis=-1, keepdims=True)
    probability = (exponent / row_total).astype(jnp.bfloat16)
    log_total = row_max + jnp.log(row_total)
    context = jnp.einsum(
        "hqk,khe->qhe", probability, value_heads, preferred_element_type=jnp.float32
    )
    context = context.reshape(count_of_rows, shard_width).astype(jnp.bfloat16)
    attended = reduce_heads(product(context, output_full)) + row_pair[0]
    first_norm, normed_one, inverse_one = normalize(
        hidden_state + attended, gain_pair[0], shift_pair[0]
    )
    first_low = first_norm.astype(jnp.bfloat16)
    preactivation = product(first_low, up_full) + hidden_bias
    cumulative = 0.5 * (1.0 + lax.erf(preactivation * ROOT_HALF))
    activated_low = (preactivation * cumulative).astype(jnp.bfloat16)
    activation_slope = cumulative + preactivation * DENSITY_FACTOR * jnp.exp(
        -0.5 * preactivation * preactivation
    )
    feed_output = reduce_heads(product(activated_low, down_full)) + row_pair[1]
    result, normed_two, inverse_two = normalize(
        first_norm + feed_output, gain_pair[1], shift_pair[1]
    )
    saved_state = (
        hidden_low,
        queries,
        gathered_rows,
        key_segments,
        log_total,
        context,
        normed_one,
        inverse_one,
        first_low,
        activation_slope,
        activated_low,
        normed_two,
        inverse_two,
    )
    return (result, saved_state)


def backward_layer(grad_output, saved_state, segments, pieces, gain_pair):
    (
        hidden_low,
        queries,
        gathered_rows,
        key_segments,
        log_total,
        context,
        normed_one,
        inverse_one,
        first_low,
        activation_slope,
        activated_low,
        normed_two,
        inverse_two,
    ) = saved_state
    input_full, output_full, up_full, down_full = pieces
    model_width, shard_width = (input_full.shape[0], input_full.shape[2])
    local_heads = shard_width // HD
    count_of_rows = queries.shape[0]
    key_count = gathered_rows.shape[0]
    scale_factor = HD ** (-0.5)
    grad_two, gain_two, shift_two = normalize_back(
        grad_output, normed_two, inverse_two, gain_pair[1]
    )
    grad_two_low = grad_two.astype(jnp.bfloat16)
    grad_down = product_left(activated_low, grad_two_low)
    grad_pre = product_right(grad_two_low, down_full) * activation_slope
    grad_pre_low = grad_pre.astype(jnp.bfloat16)
    grad_up = product_left(first_low, grad_pre_low)
    grad_first = grad_two + reduce_heads(product_right(grad_pre_low, up_full))
    grad_one, gain_one, shift_one = normalize_back(
        grad_first, normed_one, inverse_one, gain_pair[0]
    )
    grad_one_low = grad_one.astype(jnp.bfloat16)
    grad_output_w = product_left(context, grad_one_low)
    grad_context = product_right(grad_one_low, output_full).astype(jnp.bfloat16)
    query_heads = queries.reshape(count_of_rows, local_heads, HD)
    key_heads = gathered_rows[:, :shard_width].reshape(key_count, local_heads, HD)
    value_heads = gathered_rows[:, shard_width:].reshape(key_count, local_heads, HD)
    scores = attention_scores(query_heads, key_heads, segments, key_segments)
    probability = jnp.exp(scores - log_total)
    context_heads = grad_context.reshape(count_of_rows, local_heads, HD)
    grad_probability = jnp.einsum(
        "qhe,khe->hqk", context_heads, value_heads, preferred_element_type=jnp.float32
    )
    grad_values = jnp.einsum(
        "hqk,qhe->khe",
        probability.astype(jnp.bfloat16),
        context_heads,
        preferred_element_type=jnp.float32,
    )
    row_dot = jnp.sum(probability * grad_probability, axis=-1, keepdims=True)
    grad_scores = (probability * (grad_probability - row_dot)).astype(jnp.bfloat16)
    grad_query = (
        jnp.einsum(
            "hqk,khe->qhe", grad_scores, key_heads, preferred_element_type=jnp.float32
        ).reshape(count_of_rows, shard_width)
        * scale_factor
    )
    grad_keys = (
        jnp.einsum(
            "hqk,qhe->khe", grad_scores, query_heads, preferred_element_type=jnp.float32
        ).reshape(key_count, shard_width)
        * scale_factor
    )
    grad_pair = lax.psum_scatter(
        jnp.concatenate([grad_keys, grad_values.reshape(key_count, shard_width)], axis=1),
        "context",
        scatter_dimension=0,
        tiled=True,
    )
    grad_projected = jnp.concatenate([grad_query, grad_pair], axis=1).astype(jnp.bfloat16)
    grad_input_w = product_left(hidden_low, grad_projected).reshape(model_width, 3, shard_width)
    grad_hidden = grad_one + reduce_heads(
        product_right(grad_projected, input_full.reshape(model_width, 3 * shard_width))
    )
    bias_grads = jnp.stack(
        [jnp.sum(grad_query, axis=0), jnp.sum(grad_pair[:, shard_width:], axis=0)]
    )
    small_grads = (
        bias_grads,
        jnp.sum(grad_pre, axis=0),
        jnp.stack([jnp.sum(grad_one, axis=0), jnp.sum(grad_two, axis=0)]),
        jnp.stack([gain_one, gain_two]),
        jnp.stack([shift_one, shift_two]),
    )
    return (grad_hidden, (grad_input_w, grad_output_w, grad_up, grad_down), small_grads)


def shards(
    tokens,
    segments,
    query_key_value_weight,
    input_bias,
    output_weight,
    row_bias,
    norm_gain,
    norm_bias,
    up_weight,
    up_bias,
    down_weight,
    cotangent,
):
    layers = query_key_value_weight.shape[0]
    tokens_wide = tokens.astype(jnp.float32)
    cotangent_wide = cotangent.astype(jnp.float32)
    hidden_state = tokens_wide
    grad_hidden = cotangent_wide
    hidden_low = tokens
    gathered = []
    layer_index = 0
    pieces = (
        lax.all_gather(query_key_value_weight[layer_index], "weight", axis=0, tiled=True),
        lax.all_gather(output_weight[layer_index], "weight", axis=1, tiled=True),
        lax.all_gather(up_weight[layer_index], "weight", axis=0, tiled=True),
        lax.all_gather(down_weight[layer_index], "weight", axis=1, tiled=True),
    )
    gathered.append(pieces)
    hidden_state, saved_state = forward_layer(
        hidden_state,
        hidden_low,
        segments,
        pieces,
        input_bias[layer_index],
        row_bias[layer_index],
        norm_gain[layer_index],
        norm_bias[layer_index],
        up_bias[layer_index],
    )
    records = [saved_state]
    hidden_low = hidden_state.astype(jnp.bfloat16)
    weight_parts = [None] * layers
    small_parts = [None] * layers
    for layer_index in reversed(range(layers)):
        pieces = (
            lax.all_gather(query_key_value_weight[layer_index], "weight", axis=0, tiled=True),
            lax.all_gather(output_weight[layer_index], "weight", axis=1, tiled=True),
            lax.all_gather(up_weight[layer_index], "weight", axis=0, tiled=True),
            lax.all_gather(down_weight[layer_index], "weight", axis=1, tiled=True),
        )
        grad_hidden, weight_grads, small_grads = backward_layer(
            grad_hidden, records[layer_index], segments, pieces, norm_gain[layer_index]
        )
        shares = (
            lax.psum_scatter(weight_grads[0], "weight", scatter_dimension=0, tiled=True),
            lax.psum_scatter(weight_grads[1], "weight", scatter_dimension=1, tiled=True),
            lax.psum_scatter(weight_grads[2], "weight", scatter_dimension=0, tiled=True),
            lax.psum_scatter(weight_grads[3], "weight", scatter_dimension=1, tiled=True),
        )
        shares = lax.psum((shares[0], shares[1], shares[2], shares[3]), "context")
        weight_parts[layer_index] = shares
        small_parts[layer_index] = small_grads
    stacked_small = tuple((jnp.stack([small_parts[0][member]]) for member in range(5)))
    summed_small = lax.psum(
        (stacked_small[0], stacked_small[1], stacked_small[2], stacked_small[3], stacked_small[4]),
        ("weight", "context"),
    )
    stacked_weights = [jnp.stack([weight_parts[0][member]]) for member in range(4)]
    return (
        hidden_low,
        grad_hidden,
        stacked_weights[0],
        summed_small[0],
        stacked_weights[1],
        summed_small[2],
        summed_small[3],
        summed_small[4],
        stacked_weights[2],
        summed_small[1],
        stacked_weights[3],
    )


def solution(mesh):
    placed = (
        P(("weight", "context"), None),
        P(("weight", "context")),
        P(None, "weight", None, "tensor"),
        P(None, None, "tensor"),
        P(None, "tensor", "weight"),
        P(),
        P(),
        P(),
        P(None, "weight", "tensor"),
        P(None, "tensor"),
        P(None, "tensor", "weight"),
        P(("weight", "context"), None),
    )
    return jax.shard_map(
        shards,
        mesh=mesh,
        in_specs=placed,
        out_specs=(
            P(("weight", "context"), None),
            P(("weight", "context"), None),
            P(None, "weight", None, "tensor"),
            P(None, None, "tensor"),
            P(None, "tensor", "weight"),
            P(),
            P(),
            P(),
            P(None, "weight", "tensor"),
            P(None, "tensor"),
            P(None, "tensor", "weight"),
        ),
        check_vma=False,
    )
```

profile of v0, /device:TPU:4, one launch (start us, length us, event | category | flops | bytes accessed | tf_op | source)
XLA Modules:
  0.0 546.9 jit_solution(15553507549658719792)
XLA Ops:
  8.1 12.8 %all-gather = bf16[1,768,3,192]{1,3,2,0:T(8,128)(2,1)S(1)} all-gather(bf16[1,384,3,192]{1,3,2,0:T(8,128)(2,1)} %param.14), channel_id=2, replica_groups=mesh['weight'=2,'context'=4,'tensor'=4] {'weight'}, dimensions={1}, use_global_device_ids=true | all-gather | bytes 1327104 | tf_op jit(solution)/shard_map/all_gather | solution.py:252
  21.8 1.4 fusion.54
  23.4 20.0 %all_gather.23 = bf16[1024,384]{0,1:T(8,128)(2,1)S(1)} all-gather(bf16[256,384]{0,1:T(8,128)(2,1)S(1)} %pad_maximum_fusion.2), channel_id=1, replica_groups=mesh['weight'=2,'context'=4,'tensor'=4] {'context'}, dimensions={0}, use_global_device_ids=true | all-gather | bytes 983040 | tf_op jit(solution)/shard_map/all_gather | solution.py:89
  43.5 9.2 %all-gather.4 = s32[4,1,256]{2,1,0:T(1,128)S(1)} all-gather(s32[1,1,256]{2,1,0:T(1,128)S(1)} %bitcast.94), channel_id=1, replica_groups=mesh['weight'=2,'context'=4,'tensor'=4] {'context'}, dimensions={0}, use_global_device_ids=true | all-gather | bytes 5120 | tf_op jit(solution)/shard_map/all_gather | solution.py:90
  53.0 5.8 %all-gather.1 = bf16[1,192,768]{2,1,0:T(8,128)(2,1)S(1)} all-gather(bf16[1,192,384]{2,1,0:T(8,128)(2,1)S(1)} %copy-done.31), channel_id=3, replica_groups=mesh['weight'=2,'context'=4,'tensor'=4] {'weight'}, dimensions={2}, use_global_device_ids=true | all-gather | bytes 442368 | tf_op jit(solution)/shard_map/all_gather | solution.py:253
  58.8 0.8 fusion.52
  59.7 0.9 fusion
  62.0 1.2 fusion.25
  64.4 1.4 slice_reduce_fusion.1
  65.8 1.4 slice_reduce_fusion.3
  67.2 1.3 reduce.5
  68.5 27.7 %all-reduce.8.cloned.1.call-done = f32[256,768]{1,0:T(8,128)} async-done(((f32[256,768]{1,0:T(8,128)}), f32[256,768]{1,0:T(8,128)}) %all-reduce.8.cloned.1.call-update) | async-done | bytes 786448 | tf_op jit(solution)/shard_map/psum | solution.py:32
  96.2 1.3 fusion.48
  97.5 0.9 copy-done
  99.2 3.0 convolution_add_fusion
  102.1 6.9 %all-gather.10.cloned.1.call-done = bf16[1,768,768]{2,1,0:T(8,128)(2,1)} async-done(((bf16[1,768,384]{2,1,0:T(8,128)(2,1)}), bf16[1,768,768]{2,1,0:T(8,128)(2,1)}) %all-gather.10.cloned.1.call-update) | async-done | bytes 1179664 | tf_op jit(solution)/shard_map/all_gather | solution.py:255
  109.0 2.9 fusion.7
  112.0 35.9 %all-reduce.10.cloned.1.call-done = f32[256,768]{1,0:T(8,128)} async-done(((f32[256,768]{1,0:T(8,128)}), f32[256,768]{1,0:T(8,128)}) %all-reduce.10.cloned.1.call-update) | async-done | bytes 786448 | tf_op jit(solution)/shard_map/psum | solution.py:32
  147.9 1.8 fusion.47
  149.9 0.9 fusion.19
  150.9 1.7 fusion.45
  152.6 0.9 copy-done.9
  153.5 1.2 fusion.53
  155.4 1.4 fusion.9
  157.6 34.1 %all-reduce.12.cloned.1.call-done = f32[256,768]{1,0:T(8,128)} async-done(((f32[256,768]{1,0:T(8,128)}), f32[256,768]{1,0:T(8,128)}) %all-reduce.12.cloned.1.call-update) | async-done | bytes 786448 | tf_op jit(solution)/shard_map/psum | solution.py:32
  191.7 2.8 multiply_reduce_fusion.1
  194.5 1.6 fusion.44
  197.0 0.9 multiply_reduce_fusion
  200.7 1.3 pad_maximum_fusion
  202.1 1.1 fusion.29
  203.3 2.1 fusion.32
  205.7 3.2 fusion.35
  209.0 0.9 copy-done.13
  210.6 26.9 %reduce-scatter.6.cloned.1.call-done = f32[256,384]{0,1:T(8,128)} async-done(((f32[1024,384]{0,1:T(8,128)}), f32[256,384]{0,1:T(8,128)}) %reduce-scatter.6.cloned.1.call-update) | async-done | bytes 393232 | tf_op jit(solution)/shard_map/reduce_scatter | solution.py:205
  237.5 1.0 convert.18
  238.5 1.6 fusion.38
  240.2 1.4 fusion.39
  241.7 11.0 %reduce-scatter.10.cloned.1.call-done = f32[192,384]{1,0:T(8,128)} async-done(((f32[192,768]{1,0:T(8,128)}), f32[192,384]{1,0:T(8,128)}) %reduce-scatter.10.cloned.1.call-update) | async-done | bytes 294928 | tf_op jit(solution)/shard_map/reduce_scatter | solution.py:285
  252.7 36.9 %reduce-scatter.12.cloned.1.call-done = f32[384,768]{1,0:T(8,128)} async-done(((f32[768,768]{1,0:T(8,128)}), f32[384,768]{1,0:T(8,128)}) %reduce-scatter.12.cloned.1.call-update) | async-done | bytes 1179664 | tf_op jit(solution)/shard_map/reduce_scatter | solution.py:286
  289.6 37.0 %reduce-scatter.14.cloned.1.call-done = f32[768,384]{1,0:T(8,128)} async-done(((f32[768,768]{1,0:T(8,128)}), f32[768,384]{1,0:T(8,128)}) %reduce-scatter.14.cloned.1.call-update) | async-done | bytes 1179664 | tf_op jit(solution)/shard_map/reduce_scatter | solution.py:287
  326.6 30.6 %reduce-scatter.8.cloned.1.call-done = f32[384,3,192]{0,2,1:T(8,128)} async-done(((f32[768,3,192]{0,2,1:T(8,128)}), f32[384,3,192]{0,2,1:T(8,128)}) %reduce-scatter.8.cloned.1.call-update) | async-done | bytes 884752 | tf_op jit(solution)/shard_map/reduce_scatter | solution.py:284
  357.7 38.1 %all-reduce = (f32[1,2,192]{2,1,0:T(2,128)}, f32[1,2,768]{2,1,0:T(2,128)}, f32[1,2,768]{2,1,0:T(2,128)}, f32[1,2,768]{2,1,0:T(2,128)}, f32[1,768]{1,0:T(1,128)}) all-reduce(f32[1,2,192]{2,1,0:T(2,128)S(1)} %maximum_bitcast_fusion.3, ...), channel_id=1, replica_groups=mesh['weight'=2,'context'=4,'tensor'=4] {'weight','context'}, use_global_device_ids=true, to_apply=%region_20.21 | all-reduce | flops 5760 | bytes 46080 | tf_op jit(solution)/shard_map/psum | solution.py:293
  396.0 2.1 add.181
  398.1 135.3 %all-reduce.16.cloned.1.call-done = (f32[1,384,3,192]{1,3,2,0:T(8,128)}, f32[1,192,384]{2,1,0:T(8,128)}, f32[1,384,768]{2,1,0:T(8,128)}, f32[1,768,384]{2,1,0:T(8,128)}) async-done(((f32[1,384,3,192]{1,3,2,0:T(8,128)}, f32[1,192,384]{2,1,0:T(8,128)}, f32[1,384,768]{2,1,0:T(8,128)}, f32[1,768,384]{2,1,0:T(8,128)}), (f32[1,384,3,192]{1,3,2,0:T(8,128)}, f32[1,192,384]{2,1,0:T(8,128)}, ...) | async-done | bytes 3538960 | tf_op jit(solution)/shard_map/psum | solution.py:289
  533.4 2.3 copy.31
  535.7 1.7 copy.32
  537.4 1.0 copy.33
  538.4 1.0 copy.34
  (147 shorter events, 12.2 us)
Async XLA Ops:
  8.0 88.1 %all-reduce.8.cloned.1.call-start = ((), (), s32[]{:S(2)}) async-start(), calls=%async_computation.5 | async-start | bytes 1572864 | tf_op jit(solution)/shard_map/psum | solution.py:32
  21.8 21.8 %copy-start.42 = (s32[256]{0:T(256)S(1)}, s32[256]{0:T(256)}, u32[]{:S(2)}) copy-start(s32[256]{0:T(256)} %param.13) | copy-start | bytes 3076
  23.2 29.8 %copy-start.31 = (bf16[1,192,384]{2,1,0:T(8,128)(2,1)S(1)}, bf16[1,192,384]{2,1,0:T(8,128)(2,1)}, u32[]{:S(2)}) copy-start(bf16[1,192,384]{2,1,0:T(8,128)(2,1)} %param.16) | copy-start | bytes 442372
  23.4 36.3 %copy-start.26 = (bf16[256,192]{0,1:T(8,128)(2,1)}, bf16[256,192]{0,1:T(8,128)(2,1)S(1)}, u32[]{:S(2)}) copy-start(bf16[256,192]{0,1:T(8,128)(2,1)S(1)} %get-tuple-element.46) | copy-start | bytes 294916
  43.5 15.3 %copy-start.12 = (bf16[1024,192]{0,1:T(8,128)(2,1)}, bf16[1024,192]{0,1:T(8,128)(2,1)S(1)}, u32[]{:S(2)}) copy-start(bf16[1024,192]{0,1:T(8,128)(2,1)S(1)} %get-tuple-element.44) | copy-start | bytes 1179652
  43.5 17.0 %copy-start.20 = (bf16[1024,192]{0,1:T(8,128)(2,1)}, bf16[1024,192]{0,1:T(8,128)(2,1)S(1)}, u32[]{:S(2)}) copy-start(bf16[1024,192]{0,1:T(8,128)(2,1)S(1)} %get-tuple-element.45) | copy-start | bytes 1179652
  58.8 2.6 copy-start.15
  59.7 1.7 copy-start.32
  61.4 34.8 %copy-start.11 = (bf16[256,768]{1,0:T(8,128)(2,1)S(1)}, bf16[256,768]{1,0:T(8,128)(2,1)}, u32[]{:S(2)}) copy-start(bf16[256,768]{1,0:T(8,128)(2,1)} %param.12) | copy-start | bytes 1179652
  63.2 36.0 %all-gather.8.cloned.1.call-start = ((), (), s32[]{:S(2)}) async-start(), calls=%async_computation.14 | async-start | bytes 1769472 | tf_op jit(solution)/shard_map/all_gather | solution.py:254
  63.8 45.3 %all-gather.10.cloned.1.call-start = ((), (), s32[]{:S(2)}) async-start(), calls=%async_computation.15 | async-start | bytes 1769472 | tf_op jit(solution)/shard_map/all_gather | solution.py:255
  64.4 83.5 %all-reduce.10.cloned.1.call-start = ((), (), s32[]{:S(2)}) async-start(), calls=%async_computation.6 | async-start | bytes 1572864 | tf_op jit(solution)/shard_map/psum | solution.py:32
  112.0 79.7 %all-reduce.12.cloned.1.call-start = ((), (), s32[]{:S(2)}) async-start(), calls=%async_computation.7 | async-start | bytes 1572864 | tf_op jit(solution)/shard_map/psum | solution.py:32
  147.9 2.1 copy-start.19
  147.9 3.0 copy-start.35
  149.7 3.8 copy-start.14
  149.7 3.8 copy-start.25
  152.6 2.9 copy-start.22
  156.9 80.6 %reduce-scatter.6.cloned.1.call-start = ((), (), s32[]{:S(2)}) async-start(), calls=%async_computation.8 | async-start | bytes 1966080 | tf_op jit(solution)/shard_map/reduce_scatter | solution.py:205
  191.7 2.8 copy-start.1
  191.7 4.4 copy-start.16
  194.5 2.5 copy-start.21
  199.5 1.1 copy-start.3
  200.6 1.4 copy-start.6
  200.6 1.5 copy-start.30
  201.9 1.4 copy-start.2
  201.9 1.4 copy-start.18
  201.9 1.4 copy-start.33
  202.0 50.7 %reduce-scatter.10.cloned.1.call-start = ((), (), s32[]{:S(2)}) async-start(), calls=%async_computation.11 | async-start | bytes 884736 | tf_op jit(solution)/shard_map/reduce_scatter | solution.py:285
  203.2 2.4 copy-start.10
  203.2 86.4 %reduce-scatter.12.cloned.1.call-start = ((), (), s32[]{:S(2)}) async-start(), calls=%async_computation.12 | async-start | bytes 3538944 | tf_op jit(solution)/shard_map/reduce_scatter | solution.py:286
  205.4 3.6 copy-start.4
  205.4 121.2 %reduce-scatter.14.cloned.1.call-start = ((), (), s32[]{:S(2)}) async-start(), calls=%async_computation.13 | async-start | bytes 3538944 | tf_op jit(solution)/shard_map/reduce_scatter | solution.py:287
  208.9 1.0 copy-start.13
  208.9 148.3 %reduce-scatter.8.cloned.1.call-start = ((), (), s32[]{:S(2)}) async-start(), calls=%async_computation.10 | async-start | bytes 2654208 | tf_op jit(solution)/shard_map/reduce_scatter | solution.py:284
  210.6 29.6 %copy-start.8 = (bf16[1,768,3,192]{1,3,2,0:T(8,128)(2,1)S(1)}, bf16[1,768,3,192]{1,3,2,0:T(8,128)(2,1)}, u32[]{:S(2)}) copy-start(bf16[1,768,3,192]{1,3,2,0:T(8,128)(2,1)} %copy-done.7) | copy-start | bytes 2654212
  240.1 155.9 %all-reduce.14.cloned.1.call-start = ((), (), s32[]{:S(2)}) async-start(), calls=%async_computation.9 | async-start | bytes 1572864 | tf_op jit(solution)/shard_map/psum | solution.py:32
  241.6 115.7 %copy-start.38 = (f32[768]{0:T(1024)S(1)}, f32[768]{0:T(1024)}, u32[]{:S(2)}) copy-start(f32[768]{0:T(1024)} %get-tuple-element.36) | copy-start | bytes 9220
  241.6 115.7 %copy-start.37 = (f32[768]{0:T(1024)S(1)}, f32[768]{0:T(1024)}, u32[]{:S(2)}) copy-start(f32[768]{0:T(1024)} %get-tuple-element.13) | copy-start | bytes 9220
  241.6 115.7 %copy-start.36 = (f32[768]{0:T(1024)S(1)}, f32[768]{0:T(1024)}, u32[]{:S(2)}) copy-start(f32[768]{0:T(1024)} %get-tuple-element.18) | copy-start | bytes 9220
  241.6 115.7 %copy-start.43 = (f32[768]{0:T(1024)S(1)}, f32[768]{0:T(1024)}, u32[]{:S(2)}) copy-start(f32[768]{0:T(1024)} %get-tuple-element.57) | copy-start | bytes 9220
  241.6 115.8 %copy-start.41 = (f32[768]{0:T(1024)S(1)}, f32[768]{0:T(1024)}, u32[]{:S(2)}) copy-start(f32[768]{0:T(1024)} %get-tuple-element.34) | copy-start | bytes 9220
  241.6 115.8 %copy-start.40 = (f32[768]{0:T(1024)S(1)}, f32[768]{0:T(1024)}, u32[]{:S(2)}) copy-start(f32[768]{0:T(1024)} %get-tuple-element.11) | copy-start | bytes 9220
  241.6 115.8 %copy-start.39 = (f32[768]{0:T(1024)S(1)}, f32[768]{0:T(1024)}, u32[]{:S(2)}) copy-start(f32[768]{0:T(1024)} %get-tuple-element.16) | copy-start | bytes 9220
  241.6 115.9 %copy-start.28 = (f32[256,384]{0,1:T(8,128)S(1)}, f32[256,384]{0,1:T(8,128)}, u32[]{:S(2)}) copy-start(f32[256,384]{0,1:T(8,128)} %reduce-scatter.6.cloned.1.call-done) | copy-start | bytes 1179652
  241.6 291.8 %all-reduce.16.cloned.1.call-start = ((), (), s32[]{:S(2)}) async-start(), calls=%async_computation.16 | async-start | bytes 7077888 | tf_op jit(solution)/shard_map/psum | solution.py:289
  533.4 4.0 copy-start.24
  533.4 5.0 copy-start.23
  (8 other events, 6.7 us)
Sparse Core Ops, SparseCore 0:
  63.3 32.7 all-reduce.7
  112.1 35.7 all-reduce.9
  157.0 34.6 all-reduce.11
  202.1 35.3 reduce-scatter.5
  239.6 13.0 reduce-scatter.9
  254.9 34.6 reduce-scatter.11
  291.9 34.7 reduce-scatter.13
  329.0 28.2 reduce-scatter.7
  360.2 35.7 all-reduce.13
  398.5 134.8 all-reduce.15
Sparse Core Ops, SparseCore 1:
  65.2 19.7 all-gather.7
  86.3 22.6 all-gather.9
where the time goes:
time: 549 us; the launch traced here: 547 us
  waiting for transfers between devices  384 us (70%)
  blocking collectives  86 us (16%)
  matrix products  25.1 us (5%)
  other arithmetic  19.6 us (4%)
  between operations  16.2 us (3%)
  local copies, waits for them, and re-layouts  15.7 us (3%)
    psum x1, waiting for transfers between devices, shards(): shares = lax.psum((shares[0], shares[1], shares[2], shares[3]), 'context')  135 us
    psum x4, waiting for transfers between devices, tensor_total(): return lax.psum(partial_rows, 'tensor')  97.9 us
    psum x1, blocking collectives, shards(): lax.psum((stacked_small[0], stacked_small[1], stacked_small[2], stacked_s...  38.1 us
    reduce_scatter x1, waiting for transfers between devices, shards(): lax.psum_scatter(weight_grads[3], 'weight', scatter_dimension=1, tiled=True)  37 us
    reduce_scatter x1, waiting for transfers between devices, shards(): lax.psum_scatter(weight_grads[2], 'weight', scatter_dimension=0, tiled=True)  36.9 us
    reduce_scatter x1, waiting for transfers between devices, shards(): lax.psum_scatter(weight_grads[0], 'weight', scatter_dimension=0, tiled=True)  30.6 us
    reduce_scatter x1, waiting for transfers between devices, backward_layer(): lax.psum_scatter(jnp.concatenate([grad_keys, grad_values.reshape(key_coun...  26.9 us
    all_gather x1, blocking collectives, forward_layer(): lax.all_gather(key_value_rows, 'context', axis=0, tiled=True)  20 us
  transfers between devices with their start and end apart: 12, of which 11 were waited for; matrix products, arithmetic and copies ran while one was open for 4% of the time, Pallas kernels for 0%

commit v1 on v0

v1 whole, which is shorter than its diff:
```python
import jax
import jax.numpy as jnp
from jax import lax
from jax.sharding import PartitionSpec as P

HD = 64
EPSILON = 1e-05
NEG_FILL = -1e30
ROOT_HALF = 0.7071067811865476
DENSITY_FACTOR = 0.3989422804014327
BF = jnp.bfloat16
F32 = jnp.float32


def product(left, right):
    return jnp.dot(left, right, preferred_element_type=F32)


def product_left(left, right):
    return lax.dot_general(left, right, (((0,), (0,)), ((), ())), preferred_element_type=F32)


def product_right(left, right):
    return lax.dot_general(left, right, (((1,), (1,)), ((), ())), preferred_element_type=F32)


def normalize(summed):
    center = summed - jnp.mean(summed, axis=-1, keepdims=True)
    inverse = lax.rsqrt(jnp.mean(center * center, axis=-1, keepdims=True) + EPSILON)
    return center * inverse, inverse


def normalize_back(grad_output, normed, inverse, gain_vector):
    scaled = grad_output * gain_vector
    return inverse * (
        scaled
        - jnp.mean(scaled, axis=-1, keepdims=True)
        - normed * jnp.mean(scaled * normed, axis=-1, keepdims=True)
    )


def build(mesh):
    count = dict(mesh.shape)
    paired = count["weight"] == 2

    def flip(value, axis, bit):
        return lax.ppermute(value, axis, [(i, i ^ bit) for i in range(count[axis])])

    def bits(axis):
        bit, found = 1, []
        while bit < count[axis]:
            found.append(bit)
            bit *= 2
        return found

    def shards(
        tokens,
        segments,
        query_key_value_weight,
        input_bias,
        output_weight,
        row_bias,
        norm_gain,
        norm_bias,
        up_weight,
        up_bias,
        down_weight,
        cotangent,
    ):
        weight_at = lax.axis_index("weight")
        context_at = lax.axis_index("context")
        core_at = lax.axis_index("tensor") % 2
        rows, width = tokens.shape
        half = rows // 2
        shard_width = input_bias.shape[2]
        heads = shard_width // HD
        packs = count["context"]

        def columns(value):
            if not paired:
                return value
            middle = value.shape[-1] // 2
            swapped = jnp.concatenate([value[..., middle:], value[..., :middle]], axis=-1)
            return jnp.where(weight_at == 0, value, swapped)

        def own_rows(value):
            middle = value.shape[0] // 2
            swapped = jnp.concatenate([value[middle:], value[:middle]], axis=0)
            return jnp.where(core_at == 0, value, swapped)

        def gather_weight(value, axis):
            if paired:
                return [value, flip(value, "weight", 1)]
            return [lax.all_gather(value, "weight", axis=axis, tiled=True)]

        def contract(value, groups):
            step = width // len(groups)
            total = product(value[:, :step], groups[0])
            for number in range(1, len(groups)):
                total = total + product(
                    value[:, number * step : (number + 1) * step], groups[number]
                )
            return total

        def expand(value, groups):
            parts = [product(value, group) for group in groups]
            return parts[0] if len(parts) == 1 else jnp.concatenate(parts, axis=1)

        def contract_right(value, groups):
            step = width // len(groups)
            total = product_right(value[:, :step], groups[0])
            for number in range(1, len(groups)):
                total = total + product_right(
                    value[:, number * step : (number + 1) * step], groups[number]
                )
            return total

        def expand_right(value, groups):
            parts = [product_right(value, group) for group in groups]
            return parts[0] if len(parts) == 1 else jnp.concatenate(parts, axis=1)

        def row_total(partial):
            mine, theirs = partial[:half], partial[half:].astype(BF)
            total = mine + flip(theirs, "tensor", 1).astype(F32)
            for bit in bits("tensor")[1:]:
                low = total.astype(BF)
                total = low.astype(F32) + flip(low, "tensor", bit).astype(F32)
            return total

        def both_halves(value):
            return jnp.concatenate([value, flip(value, "tensor", 1)], axis=0)

        def take_half(value, which):
            middle = value.shape[0] // 2
            return lax.dynamic_slice_in_dim(value, which * middle, middle, axis=0)

        def context_total(value):
            for bit in bits("context"):
                which = (context_at // bit) % 2
                own, other = take_half(value, which), take_half(value, 1 - which)
                value = own + flip(other.astype(BF), "context", bit).astype(F32)
            value = value.astype(BF)
            for bit in reversed(bits("context")):
                which = (context_at // bit) % 2
                other = flip(value, "context", bit)
                value = jnp.where(
                    which == 0,
                    jnp.concatenate([value, other], axis=0),
                    jnp.concatenate([other, value], axis=0),
                )
            return value.astype(F32)

        def context_blocks(value):
            blocks = [value] + [flip(value, "context", j) for j in range(1, packs)]
            return blocks

        def in_order(blocks):
            placed = []
            for at in range(packs):
                chosen = blocks[0]
                for j in range(1, packs):
                    chosen = jnp.where(context_at == (at ^ j), blocks[j], chosen)
                placed.append(chosen)
            return jnp.concatenate(placed, axis=0)

        projection = query_key_value_weight[0].reshape(-1, 3 * shard_width)
        input_groups = gather_weight(projection, 0)
        output_groups = gather_weight(output_weight[0], 1)
        up_groups = gather_weight(up_weight[0], 0)
        down_groups = gather_weight(down_weight[0], 1)

        gains, shifts, row_pair = columns(norm_gain[0]), columns(norm_bias[0]), columns(row_bias[0])
        low_rows = own_rows(columns(tokens))
        cotangent_rows = own_rows(columns(cotangent))[:half].astype(F32)
        segment_rows = own_rows(segments)

        own_blocks = [low_rows[:half]] + [
            flip(low_rows[:half], "context", j) for j in range(1, packs)
        ]
        blocks = [low_rows] + [both_halves(block) for block in own_blocks[1:]]
        pack_rows = in_order(blocks)
        pack_segments = in_order(context_blocks(segment_rows))

        bias_pair = input_bias[0]
        projected = contract(pack_rows, input_groups)
        pack_queries = (projected[:, :shard_width] + bias_pair[0]).astype(BF)
        pack_keys = projected[:, shard_width : 2 * shard_width].astype(BF)
        pack_values = (projected[:, 2 * shard_width :] + bias_pair[1]).astype(BF)
        length = pack_rows.shape[0]
        key_heads = pack_keys.reshape(length, heads, HD)
        value_heads = pack_values.reshape(length, heads, HD)
        query_heads = lax.dynamic_slice_in_dim(pack_queries, context_at * rows, rows, 0).reshape(
            rows, heads, HD
        )

        scale = HD ** (-0.5)

        def attention_scores(queries, query_segments):
            scores = (
                jnp.einsum("qhe,khe->hqk", queries, key_heads, preferred_element_type=F32) * scale
            )
            same = query_segments[:, None] == pack_segments[None, :]
            return jnp.where(same[None], scores, NEG_FILL)

        scores = attention_scores(query_heads, segment_rows)
        row_max = jnp.max(scores, axis=-1, keepdims=True)
        exponent = jnp.exp(scores - row_max)
        total = jnp.sum(exponent, axis=-1, keepdims=True)
        probability = (exponent / total).astype(BF)
        log_total = (row_max + jnp.log(total))[..., 0]
        context = jnp.einsum("hqk,khe->qhe", probability, value_heads, preferred_element_type=F32)
        context = context.reshape(rows, shard_width).astype(BF)
        pack_log = in_order(context_blocks(log_total.T)).T

        hidden_half = low_rows[:half].astype(F32)
        attended = row_total(expand(context, output_groups)) + row_pair[0]
        normed_one, inverse_one = normalize(hidden_half + attended)
        first_norm = normed_one * gains[0] + shifts[0]
        first_low = both_halves(first_norm.astype(BF))

        preactivation = contract(first_low, up_groups) + up_bias[0]
        cumulative = 0.5 * (1.0 + lax.erf(preactivation * ROOT_HALF))
        activated = (preactivation * cumulative).astype(BF)
        slope = cumulative + preactivation * DENSITY_FACTOR * jnp.exp(
            -0.5 * preactivation * preactivation
        )
        feed = row_total(expand(activated, down_groups)) + row_pair[1]
        normed_two, inverse_two = normalize(first_norm + feed)
        result = (normed_two * gains[1] + shifts[1]).astype(BF)
        layer_output = columns(own_rows(both_halves(result)))

        grad_two = normalize_back(cotangent_rows, normed_two, inverse_two, gains[1])
        grad_two_low = both_halves(grad_two.astype(BF))

        def owner_total(left, right, axis):
            if paired:
                step = width // 2
                if axis == 0:
                    mine = product_left(left[:, :step], right)
                    theirs = product_left(left[:, step:], right)
                else:
                    mine = product_left(left, right[:, :step])
                    theirs = product_left(left, right[:, step:])
                return mine + flip(theirs.astype(BF), "weight", 1).astype(F32)
            return lax.psum_scatter(
                product_left(left, right).astype(BF), "weight", scatter_dimension=axis, tiled=True
            ).astype(F32)

        grad_down = context_total(owner_total(activated, grad_two_low, 1))
        grad_pre = contract_right(grad_two_low, down_groups) * slope
        grad_pre_low = grad_pre.astype(BF)
        grad_first = grad_two + row_total(expand_right(grad_pre_low, up_groups))
        grad_up = context_total(owner_total(first_low, grad_pre_low, 0))
        grad_one = normalize_back(grad_first, normed_one, inverse_one, gains[0])
        grad_one_low = both_halves(grad_one.astype(BF))
        grad_context = contract_right(grad_one_low, output_groups).astype(BF)
        pack_context = in_order(context_blocks(grad_context))
        grad_out = context_total(owner_total(context, grad_one_low, 1))

        all_queries = pack_queries.reshape(length, heads, HD)
        all_context = pack_context.reshape(length, heads, HD)
        probability = jnp.exp(
            attention_scores(all_queries, pack_segments) - pack_log[:, :, None]
        )
        grad_probability = jnp.einsum(
            "qhe,khe->hqk", all_context, value_heads, preferred_element_type=F32
        )
        grad_values = jnp.einsum(
            "hqk,qhe->khe", probability.astype(BF), all_context, preferred_element_type=F32
        ).reshape(length, shard_width)
        row_dot = jnp.sum(probability * grad_probability, axis=-1, keepdims=True)
        grad_scores = (probability * (grad_probability - row_dot)).astype(BF)
        grad_query = (
            jnp.einsum("hqk,khe->qhe", grad_scores, key_heads, preferred_element_type=F32).reshape(
                length, shard_width
            )
            * scale
        )
        grad_keys = (
            jnp.einsum("hqk,qhe->khe", grad_scores, all_queries, preferred_element_type=F32).reshape(
                length, shard_width
            )
            * scale
        )
        pack_projected = jnp.concatenate([grad_query, grad_keys, grad_values], axis=1).astype(BF)
        grad_input = owner_total(pack_rows, pack_projected, 0)
        own_projected = lax.dynamic_slice_in_dim(pack_projected, context_at * rows, rows, 0)
        grad_half = grad_one + row_total(expand_right(own_projected, input_groups))
        grad_tokens = columns(own_rows(both_halves(grad_half)))

        def sums(value):
            return jnp.sum(value, axis=0)

        small = jnp.stack(
            [
                sums(grad_one),
                sums(grad_two),
                sums(grad_first * normed_one),
                sums(cotangent_rows * normed_two),
                sums(grad_first),
                sums(cotangent_rows),
            ]
        )
        small = columns(small)
        small = small + flip(small, "tensor", 1)
        hidden_sum = sums(grad_pre)
        joined = jnp.concatenate([small.reshape(-1), hidden_sum])
        for bit in bits("context"):
            joined = joined + flip(joined, "context", bit)
        joined = weight_total(joined)
        small = joined[: 6 * width].reshape(3, 2, width)
        bias_grads = weight_total(jnp.stack([sums(grad_query), sums(grad_values)]))
        return (
            layer_output,
            grad_tokens,
            grad_input.reshape(1, -1, 3, shard_width),
            bias_grads[None],
            grad_out[None],
            small[0][None],
            small[1][None],
            small[2][None],
            grad_up[None],
            joined[6 * width :][None],
            grad_down[None],
        )

    def weight_total(value):
        if paired:
            return value + flip(value, "weight", 1)
        return lax.psum(value, "weight")

    return shards


def solution(mesh):
    token_rows = P(("weight", "context"), None)
    input_spec = P(None, "weight", None, "tensor")
    out_spec = P(None, "tensor", "weight")
    placed = (
        token_rows,
        P(("weight", "context")),
        input_spec,
        P(None, None, "tensor"),
        out_spec,
        P(),
        P(),
        P(),
        P(None, "weight", "tensor"),
        P(None, "tensor"),
        out_spec,
        token_rows,
    )
    return jax.shard_map(
        build(mesh),
        mesh=mesh,
        in_specs=placed,
        out_specs=(
            token_rows,
            token_rows,
            input_spec,
            P(None, None, "tensor"),
            out_spec,
            P(),
            P(),
            P(),
            P(None, "weight", "tensor"),
            P(None, "tensor"),
            out_spec,
        ),
        check_vma=False,
    )
```

time: 549 us -> 245 us (0.45)
  waiting for transfers between devices: 384 us -> 91.6 us
  blocking collectives: 86 us -> 0 us
  starting transfers between devices: 0.68 us -> 60.2 us
  matrix products: 25.1 us -> 51.4 us
  between operations: 16.2 us -> 1.95 us
  other arithmetic: 19.6 us -> 25.4 us
    psum x5 -> x0, waiting for transfers between devices: 233 us -> none  [the longest x1 135 us: shards(): shares = lax.psum((shares[0], shares[1], shares[2], shares[3]), 'context')]
    reduce_scatter x5 -> x0, waiting for transfers between devices: 142 us -> none  [the longest x1 37 us: shards(): lax.psum_scatter(weight_grads[3], 'weight', scatter_dimension=1, tiled=True)]
    ppermute x0 -> x53, waiting for transfers between devices: none -> 91.6 us  [flip(): return lax.ppermute(value, axis, [(i, i ^ bit) for i in range(count[axis])])]
    ppermute x0 -> x53, starting transfers between devices: none -> 60.2 us  [flip(): return lax.ppermute(value, axis, [(i, i ^ bit) for i in range(count[axis])])]
    all_gather x4 -> x0, blocking collectives: 47.9 us -> none  [the longest x1 20 us: forward_layer(): lax.all_gather(key_value_rows, 'context', axis=0, tiled=True)]
    psum x1 -> x0, blocking collectives: 38.1 us -> none  [shards(): lax.psum((stacked_small[0], stacked_small[1], stacked_small[2], stacked_s...]
    dot_general x10 -> x15, matrix products: 12.8 us -> 31.2 us  [the longest x2 7.21 us: attention_scores(): jnp.einsum('qhe,khe->hqk', queries, key_heads, preferred_element_type=F32)]
    convert_element_type x2 -> x15, other arithmetic: 0.79 us -> 12.1 us  [the longest x1 6.99 us: shards(): grad_scores = (probability * (grad_probability - row_dot)).astype(BF)]
  transfers between devices with their start and end apart: 12 -> 53, of which waited for: 11 -> 25; matrix products, arithmetic and copies ran while one was open for 4% -> 35% of each run, Pallas kernels for 0% -> 0%
where the time goes in v1:
time: 245 us; the launch traced here: 243 us
  waiting for transfers between devices  91.6 us (37%)
  starting transfers between devices  60.2 us (25%)
  matrix products  51.4 us (21%)
  other arithmetic  25.4 us (10%)
  local copies, waits for them, and re-layouts  12.1 us (5%)
    ppermute x53, waiting for transfers between devices, flip(): return lax.ppermute(value, axis, [(i, i ^ bit) for i in range(count[axis])])  91.6 us
    ppermute x53, starting transfers between devices, flip(): return lax.ppermute(value, axis, [(i, i ^ bit) for i in range(count[axis])])  60.2 us
    dot_general x8, matrix products, product_left(): lax.dot_general(left, right, (((0,), (0,)), ((), ())), preferred_element_...  13.8 us
    dot_general x2, matrix products, attention_scores(): jnp.einsum('qhe,khe->hqk', queries, key_heads, preferred_element_type=F32)  7.21 us
    dot_general x1, matrix products, shards(): jnp.einsum('qhe,khe->hqk', all_context, value_heads, preferred_element_ty...  7.19 us
    convert_element_type x1, other arithmetic, shards(): grad_scores = (probability * (grad_probability - row_dot)).astype(BF)  6.99 us
    dot_general x1, matrix products, shards(): jnp.einsum('hqk,qhe->khe', probability.astype(BF), all_context, preferred...  6.73 us
    dot_general x8, matrix products, product_right(): lax.dot_general(left, right, (((1,), (1,)), ((), ())), preferred_element_...  6.33 us
  transfers between devices with their start and end apart: 53, of which 25 were waited for; matrix products, arithmetic and copies ran while one was open for 35% of the time, Pallas kernels for 0%

profile of v1, /device:TPU:4, one launch (start us, length us, event | category | flops | bytes accessed | tf_op | source)
XLA Modules:
  0.0 242.7 jit_solution(910822437048500488)
XLA Ops:
  2.2 3.7 %collective-permute-start = (bf16[128,768]{1,0:T(8,128)(2,1)S(1)}, bf16[128,768]{1,0:T(8,128)(2,1)S(1)}, u32[]{:S(2)}, u32[]{:S(2)}) collective-permute-start(bf16[128,768]{1,0:T(8,128)(2,1)S(1)} %slice.264), channel_id=1, source_target_pairs={{0,12},{4,8},{8,4},{12,0},{1,13},{5,9},{9,5},{13,1},{2,14},{6,10},... | collective-permute-start | bytes 589832 | tf_op jit(solution)/shard_map/ppermute | solution.py:47
  5.9 2.0 collective-permute-start.7
  10.6 4.5 %collective-permute-done.7 = s32[256]{0:T(256)S(1)} collective-permute-done((s32[256]{0:T(256)S(1)}, s32[256]{0:T(256)S(1)}, u32[]{:S(2)}, u32[]{:S(2)}) %collective-permute-start.7) | collective-permute-done | bytes 1056 | tf_op jit(solution)/shard_map/ppermute | solution.py:47
  15.1 8.1 %collective-permute-start.4 = (bf16[128,768]{1,0:T(8,128)(2,1)S(1)}, bf16[128,768]{1,0:T(8,128)(2,1)S(1)}, u32[]{:S(2)}, u32[]{:S(2)}) collective-permute-start(bf16[128,768]{1,0:T(8,128)(2,1)S(1)} %slice.264), channel_id=1, source_target_pairs={{0,4},{4,0},{8,12},{12,8},{1,5},{5,1},{9,13},{13,9},{2,6},{6,2},{1... | collective-permute-start | bytes 589832 | tf_op jit(solution)/shard_map/ppermute | solution.py:47
  23.2 1.5 collective-permute-start.14
  25.5 1.6 collective-permute-start.10
  31.2 17.8 %collective-permute-done.6 = bf16[384,576]{0,1:T(8,128)(2,1)S(1)} collective-permute-done((bf16[384,576]{0,1:T(8,128)(2,1)S(1)}, bf16[384,576]{0,1:T(8,128)(2,1)S(1)}, u32[]{:S(2)}, u32[]{:S(2)}) %collective-permute-start.6) | collective-permute-done | bytes 442400 | tf_op jit(solution)/shard_map/ppermute | solution.py:47
  56.3 1.6 collective-permute-start.12
  57.9 5.3 %collective-permute-done.12 = bf16[128,768]{1,0:T(8,128)(2,1)S(1)} collective-permute-done((bf16[128,768]{1,0:T(8,128)(2,1)S(1)}, bf16[128,768]{1,0:T(8,128)(2,1)S(1)}, u32[]{:S(2)}, u32[]{:S(2)}) %collective-permute-start.12) | collective-permute-done | bytes 196640 | tf_op jit(solution)/shard_map/ppermute | solution.py:47
  69.6 1.6 collective-permute-start.17
  71.1 2.5 %collective-permute-start.22 = (f32[256,3]{0,1:T(4,128)S(1)}, f32[256,3]{0,1:T(4,128)S(1)}, u32[]{:S(2)}, u32[]{:S(2)}) collective-permute-start(f32[256,3]{0,1:T(4,128)S(1)} %add_bitcast_fusion), channel_id=1, source_target_pairs={{0,12},{4,8},{8,4},{12,0},{1,13},{5,9},{9,5},{13,1},{2,14},{6,10},... | collective-permute-start | bytes 9224 | tf_op jit(solution)/shard_map/ppermute | solution.py:47
  73.6 1.9 collective-permute-start.24
  78.3 6.4 %fusion.119 = f32[3,1024,1024]{1,2,0:T(8,128)} fusion(bf16[1024,3,64]{0,2,1:T(8,128)(2,1)S(1)} %bitcast.97, bf16[1024,3,64]{0,2,1:T(8,128)(2,1)S(1)} %bitcast.95), kind=kOutput, calls=%fused_computation.249 | convolution fusion | flops 402653184 | bytes 13369344 | tf_op jit(solution)/shard_map/qhe,khe->hqk/dot_general | solution.py:200
  85.3 1.6 fusion.100
  89.7 1.6 collective-permute-start.21
  92.4 1.5 collective-permute-start.43
  93.9 3.1 %collective-permute-done.21 = bf16[128,768]{1,0:T(8,128)(2,1)S(1)} collective-permute-done((bf16[128,768]{1,0:T(8,128)(2,1)S(1)}, bf16[128,768]{1,0:T(8,128)(2,1)S(1)}, u32[]{:S(2)}, u32[]{:S(2)}) %collective-permute-start.21) | collective-permute-done | bytes 196640 | tf_op jit(solution)/shard_map/ppermute | solution.py:47
  100.9 2.2 convolution_convert_fusion
  105.8 2.5 %collective-permute-done.40 = f32[5376]{0:T(1024)S(1)} collective-permute-done((f32[5376]{0:T(1024)S(1)}, f32[5376]{0:T(1024)S(1)}, u32[]{:S(2)}, u32[]{:S(2)}) %collective-permute-start.40) | collective-permute-done | bytes 21536 | tf_op jit(solution)/shard_map/ppermute | solution.py:47
  109.4 1.6 collective-permute-start.48
  111.0 2.1 collective-permute-done.41
  113.0 1.5 collective-permute-start.42
  116.1 9.1 %collective-permute-done.42 = f32[5376]{0:T(1024)S(1)} collective-permute-done((f32[5376]{0:T(1024)S(1)}, f32[5376]{0:T(1024)S(1)}, u32[]{:S(2)}, u32[]{:S(2)}) %collective-permute-start.42) | collective-permute-done | bytes 21536 | tf_op jit(solution)/shard_map/ppermute | solution.py:47
  127.6 1.6 convolution_add_fusion.2
  130.0 1.7 collective-permute-start.44
  136.9 1.5 collective-permute-start.26
  138.5 1.7 collective-permute-start.27
  141.4 1.8 convolution_convert_fusion.3
  143.2 6.3 %collective-permute-done.26 = bf16[256,192]{0,1:T(8,128)(2,1)S(1)} collective-permute-done((bf16[256,192]{0,1:T(8,128)(2,1)S(1)}, bf16[256,192]{0,1:T(8,128)(2,1)S(1)}, u32[]{:S(2)}, u32[]{:S(2)}) %collective-permute-start.26) | collective-permute-done | bytes 98336 | tf_op jit(solution)/shard_map/ppermute | solution.py:47
  149.5 1.5 collective-permute-start.34
  151.1 6.7 %fusion.102 = (f32[3,64]{1,0:T(4,128)S(1)}, bf16[1024,3,64]{0,2,1:T(8,128)(2,1)S(1)}) fusion(bf16[1024,3,64]{0,2,1:T(8,128)(2,1)S(1)} %bitcast.100, f32[3,1024,1024]{1,2,0:T(8,128)} %fusion.119, f32[3,1024]{1,0:T(4,128)S(1)} %maximum_bitcast_fusion, pred[1024,1024]{0,1:T(8,128)(4,1)S(1)} %broadcast_compare_fusion), kind=kOutput, calls=%fused_computation.232 | convolution fusion | flops 415629120 | bytes 14430976 | tf_op jit(solution)/shard_map/hqk,qhe->khe/dot_general | solution.py:268
  158.2 7.2 %multiply_reduce_fusion = (f32[3,1024]{1,0:T(4,128)S(1)}, f32[3,1024,1024]{1,2,0:T(8,128)}) fusion(f32[3,1024,1024]{1,2,0:T(8,128)S(1)} %bitcast.93, f32[3,1024]{1,0:T(4,128)S(1)} %maximum_bitcast_fusion, pred[1024,1024]{0,1:T(8,128)(4,1)S(1)} %broadcast_compare_fusion, bf16[1024,3,64]{0,2,1:T(8,128)(2,1)S(1)} %bitcast.101, ...), kind=kOutput, calls=%fused_computation.1 | convolution fusion | flops 418378752 | bytes 27025408 | tf_op jit(solution)/shard_map/qhe,khe->hqk/dot_general | solution.py:265
  165.4 7.0 %multiply_convert_fusion = bf16[3,1024,1024]{1,2,0:T(8,128)(2,1)S(1)} fusion(f32[3,1024,1024]{1,2,0:T(8,128)} %get-tuple-element.94, f32[3,1024,1024]{1,2,0:T(8,128)S(1)} %bitcast.93, f32[3,1024]{1,0:T(4,128)S(1)} %get-tuple-element.93, f32[3,1024]{1,0:T(4,128)S(1)} %maximum_bitcast_fusion, pred[1024,1024]{0,1:T(8,128)(4,1)S(1)} %broadcast_compare_fusion), kind=kLoop, calls=%fused_computation | loop fusion | flops 18874368 | bytes 32530432 | tf_op jit(solution)/shard_map/convert_element_type | solution.py:272
  172.4 2.0 fusion.12
  178.4 1.5 convolution_convert_fusion.2
  182.7 1.6 collective-permute-start.35
  184.2 2.9 %collective-permute-done.35 = bf16[96,384]{1,0:T(8,128)(2,1)S(1)} collective-permute-done((bf16[96,384]{1,0:T(8,128)(2,1)S(1)}, bf16[96,384]{1,0:T(8,128)(2,1)S(1)}, u32[]{:S(2)}, u32[]{:S(2)}) %collective-permute-start.35) | collective-permute-done | bytes 73760 | tf_op jit(solution)/shard_map/ppermute | solution.py:47
  188.0 4.8 %collective-permute-done.33 = f32[2,192]{1,0:T(2,128)S(1)} collective-permute-done((f32[2,192]{1,0:T(2,128)S(1)}, f32[2,192]{1,0:T(2,128)S(1)}, u32[]{:S(2)}, u32[]{:S(2)}) %collective-permute-start.33) | collective-permute-done | bytes 1568 | tf_op jit(solution)/shard_map/ppermute | solution.py:47
  194.5 3.2 %collective-permute-done.36 = bf16[48,384]{1,0:T(8,128)(2,1)S(1)} collective-permute-done((bf16[48,384]{1,0:T(8,128)(2,1)S(1)}, bf16[48,384]{1,0:T(8,128)(2,1)S(1)}, u32[]{:S(2)}, u32[]{:S(2)}) %collective-permute-start.36) | collective-permute-done | bytes 36896 | tf_op jit(solution)/shard_map/ppermute | solution.py:47
  199.9 1.9 collective-permute-start.45
  205.1 1.7 collective-permute-start.38
  210.5 2.4 collective-permute-done.45
  212.9 3.1 %collective-permute-start.46 = (bf16[96,768]{1,0:T(8,128)(2,1)S(1)}, bf16[96,768]{1,0:T(8,128)(2,1)S(1)}, u32[]{:S(2)}, u32[]{:S(2)}) collective-permute-start(bf16[96,768]{1,0:T(8,128)(2,1)S(1)} %add_convert_fusion.2), channel_id=1, source_target_pairs={{0,8},{4,12},{8,0},{12,4},{1,9},{5,13},{9,1},{13,5},{2,10},{6,14},... | collective-permute-start | bytes 442376 | tf_op jit(solution)/shard_map/ppermute | solution.py:47
  217.3 8.3 %collective-permute-done.46 = bf16[96,768]{1,0:T(8,128)(2,1)S(1)} collective-permute-done((bf16[96,768]{1,0:T(8,128)(2,1)S(1)}, bf16[96,768]{1,0:T(8,128)(2,1)S(1)}, u32[]{:S(2)}, u32[]{:S(2)}) %collective-permute-start.46) | collective-permute-done | bytes 147488 | tf_op jit(solution)/shard_map/ppermute | solution.py:47
  225.7 2.3 collective-permute-done.51
  228.2 2.7 %convert_add_fusion = f32[384,576]{0,1:T(8,128)} fusion(bf16[384,576]{0,1:T(8,128)(2,1)} %collective-permute-done.32, bf16[1024,768]{1,0:T(8,128)(2,1)S(1)} %pad_maximum_fusion, bf16[1024,192]{0,1:T(8,128)(2,1)S(1)} %bitcast.121, bf16[1024,192]{0,1:T(8,128)(2,1)S(1)} %bitcast.109, bf16[1024,192]{0,1:T(8,128)(2,1)S(1)} %bitcast.116), kind=kOutput, calls=%fused_computation.35 | convolution fusion | flops 456966144 | bytes 3293184 | tf_op jit(solution)/shard_map/dot_general | solution.py:20
  230.9 4.7 %collective-permute-done.47 = bf16[192,768]{1,0:T(8,128)(2,1)S(1)} collective-permute-done((bf16[192,768]{1,0:T(8,128)(2,1)S(1)}, bf16[192,768]{1,0:T(8,128)(2,1)S(1)}, u32[]{:S(2)}, u32[]{:S(2)}) %collective-permute-start.47) | collective-permute-done | bytes 294944 | tf_op jit(solution)/shard_map/ppermute | solution.py:47
  236.7 3.8 %collective-permute-done.52 = bf16[384,384]{1,0:T(8,128)(2,1)S(1)} collective-permute-done((bf16[384,384]{1,0:T(8,128)(2,1)S(1)}, bf16[384,384]{1,0:T(8,128)(2,1)S(1)}, u32[]{:S(2)}, u32[]{:S(2)}) %collective-permute-start.52) | collective-permute-done | bytes 294944 | tf_op jit(solution)/shard_map/ppermute | solution.py:47
  (294 shorter events, 71.9 us)
Async XLA Ops:
  2.2 23.3 %collective-permute-start = (bf16[128,768]{1,0:T(8,128)(2,1)S(1)}, bf16[128,768]{1,0:T(8,128)(2,1)S(1)}, u32[]{:S(2)}, u32[]{:S(2)}) collective-permute-start(bf16[128,768]{1,0:T(8,128)(2,1)S(1)} %slice.264), channel_id=1, source_target_pairs={{0,12},{4,8},{8,4},{12,0},{1,13},{5,9},{9,5},{13,1},{2,14},{6,10},... | collective-permute-start | bytes 589832 | tf_op jit(solution)/shard_map/ppermute | solution.py:47
  5.8 21.2 %collective-permute-start.2 = (bf16[128,768]{1,0:T(8,128)(2,1)S(1)}, bf16[128,768]{1,0:T(8,128)(2,1)S(1)}, u32[]{:S(2)}, u32[]{:S(2)}) collective-permute-start(bf16[128,768]{1,0:T(8,128)(2,1)S(1)} %slice.264), channel_id=1, source_target_pairs={{0,8},{4,12},{8,0},{12,4},{1,9},{5,13},{9,1},{13,5},{2,10},{6,14},... | collective-permute-start | bytes 589832 | tf_op jit(solution)/shard_map/ppermute | solution.py:47
  5.9 9.2 %collective-permute-start.7 = (s32[256]{0:T(256)S(1)}, s32[256]{0:T(256)S(1)}, u32[]{:S(2)}, u32[]{:S(2)}) collective-permute-start(s32[256]{0:T(256)S(1)} %add_select_fusion), channel_id=1, source_target_pairs={{0,12},{4,8},{8,4},{12,0},{1,13},{5,9},{9,5},{13,1},{2,14},{6,10},... | collective-permute-start | bytes 3080 | tf_op jit(solution)/shard_map/ppermute | solution.py:47
  7.8 15.3 %collective-permute-start.8 = (s32[256]{0:T(256)S(1)}, s32[256]{0:T(256)S(1)}, u32[]{:S(2)}, u32[]{:S(2)}) collective-permute-start(s32[256]{0:T(256)S(1)} %add_select_fusion), channel_id=1, source_target_pairs={{0,8},{4,12},{8,0},{12,4},{1,9},{5,13},{9,1},{13,5},{2,10},{6,14},... | collective-permute-start | bytes 3080 | tf_op jit(solution)/shard_map/ppermute | solution.py:47
  8.9 15.8 %collective-permute-start.9 = (s32[256]{0:T(256)S(1)}, s32[256]{0:T(256)S(1)}, u32[]{:S(2)}, u32[]{:S(2)}) collective-permute-start(s32[256]{0:T(256)S(1)} %add_select_fusion), channel_id=1, source_target_pairs={{0,4},{4,0},{8,12},{12,8},{1,5},{5,1},{9,13},{13,9},{2,6},{6,2},{1... | collective-permute-start | bytes 3080 | tf_op jit(solution)/shard_map/ppermute | solution.py:47
  15.1 12.1 %collective-permute-start.4 = (bf16[128,768]{1,0:T(8,128)(2,1)S(1)}, bf16[128,768]{1,0:T(8,128)(2,1)S(1)}, u32[]{:S(2)}, u32[]{:S(2)}) collective-permute-start(bf16[128,768]{1,0:T(8,128)(2,1)S(1)} %slice.264), channel_id=1, source_target_pairs={{0,4},{4,0},{8,12},{12,8},{1,5},{5,1},{9,13},{13,9},{2,6},{6,2},{1... | collective-permute-start | bytes 589832 | tf_op jit(solution)/shard_map/ppermute | solution.py:47
  23.2 40.8 %collective-permute-start.14 = (bf16[384,768]{1,0:T(8,128)(2,1)S(1)}, bf16[384,768]{1,0:T(8,128)(2,1)S(1)}, u32[]{:S(2)}, u32[]{:S(2)}) collective-permute-start(bf16[384,768]{1,0:T(8,128)(2,1)S(1)} %bitcast.99), channel_id=1, source_target_pairs={{0,16},{16,0},{1,17},{17,1},{2,18},{18,2},{3,19},{19,3},{4,20},{20... | collective-permute-start | bytes 1769480 | tf_op jit(solution)/shard_map/ppermute | solution.py:47
  24.7 24.2 %collective-permute-start.6 = (bf16[384,576]{0,1:T(8,128)(2,1)S(1)}, bf16[384,576]{0,1:T(8,128)(2,1)S(1)}, u32[]{:S(2)}, u32[]{:S(2)}) collective-permute-start(bf16[384,576]{0,1:T(8,128)(2,1)S(1)} %bitcast.104), channel_id=1, source_target_pairs={{0,16},{16,0},{1,17},{17,1},{2,18},{18,2},{3,19},{19,3},{4,20},{20... | collective-permute-start | bytes 1327112 | tf_op jit(solution)/shard_map/ppermute | solution.py:47
  25.5 28.6 %collective-permute-start.10 = (bf16[192,384]{1,0:T(8,128)(2,1)}, bf16[192,384]{1,0:T(8,128)(2,1)S(1)}, u32[]{:S(2)}, u32[]{:S(2)}) collective-permute-start(bf16[192,384]{1,0:T(8,128)(2,1)} %bitcast.8), channel_id=1, source_target_pairs={{0,16},{16,0},{1,17},{17,1},{2,18},{18,2},{3,19},{19,3},{4,20},{20... | collective-permute-start | bytes 442376 | tf_op jit(solution)/shard_map/ppermute | solution.py:47
  27.2 1.7 collective-permute-start.3
  28.9 38.7 %collective-permute-start.15 = (bf16[768,384]{1,0:T(8,128)(2,1)}, bf16[768,384]{1,0:T(8,128)(2,1)S(1)}, u32[]{:S(2)}, u32[]{:S(2)}) collective-permute-start(bf16[768,384]{1,0:T(8,128)(2,1)} %bitcast.14), channel_id=1, source_target_pairs={{0,16},{16,0},{1,17},{17,1},{2,18},{18,2},{3,19},{19,3},{4,20},{20... | collective-permute-start | bytes 1769480 | tf_op jit(solution)/shard_map/ppermute | solution.py:47
  56.3 7.0 %collective-permute-start.12 = (bf16[128,768]{1,0:T(8,128)(2,1)S(1)}, bf16[128,768]{1,0:T(8,128)(2,1)S(1)}, u32[]{:S(2)}, u32[]{:S(2)}) collective-permute-start(bf16[128,768]{1,0:T(8,128)(2,1)S(1)} %fusion.48), channel_id=1, source_target_pairs={{0,2},{1,3},{2,0},{3,1},{4,6},{5,7},{6,4},{7,5},{8,10},{9,11},{10,... | collective-permute-start | bytes 589832 | tf_op jit(solution)/shard_map/ppermute | solution.py:47
  69.6 7.0 %collective-permute-start.17 = (bf16[128,768]{1,0:T(8,128)(2,1)S(1)}, bf16[128,768]{1,0:T(8,128)(2,1)S(1)}, u32[]{:S(2)}, u32[]{:S(2)}) collective-permute-start(bf16[128,768]{1,0:T(8,128)(2,1)S(1)} %fusion.45), channel_id=1, source_target_pairs={{0,2},{1,3},{2,0},{3,1},{4,6},{5,7},{6,4},{7,5},{8,10},{9,11},{10,... | collective-permute-start | bytes 589832 | tf_op jit(solution)/shard_map/ppermute | solution.py:47
  71.1 17.2 %collective-permute-start.22 = (f32[256,3]{0,1:T(4,128)S(1)}, f32[256,3]{0,1:T(4,128)S(1)}, u32[]{:S(2)}, u32[]{:S(2)}) collective-permute-start(f32[256,3]{0,1:T(4,128)S(1)} %add_bitcast_fusion), channel_id=1, source_target_pairs={{0,12},{4,8},{8,4},{12,0},{1,13},{5,9},{9,5},{13,1},{2,14},{6,10},... | collective-permute-start | bytes 9224 | tf_op jit(solution)/shard_map/ppermute | solution.py:47
  73.6 14.8 %collective-permute-start.23 = (f32[256,3]{0,1:T(4,128)S(1)}, f32[256,3]{0,1:T(4,128)S(1)}, u32[]{:S(2)}, u32[]{:S(2)}) collective-permute-start(f32[256,3]{0,1:T(4,128)S(1)} %add_bitcast_fusion), channel_id=1, source_target_pairs={{0,8},{4,12},{8,0},{12,4},{1,9},{5,13},{9,1},{13,5},{2,10},{6,14},... | collective-permute-start | bytes 9224 | tf_op jit(solution)/shard_map/ppermute | solution.py:47
  73.6 14.8 %collective-permute-start.24 = (f32[256,3]{0,1:T(4,128)S(1)}, f32[256,3]{0,1:T(4,128)S(1)}, u32[]{:S(2)}, u32[]{:S(2)}) collective-permute-start(f32[256,3]{0,1:T(4,128)S(1)} %add_bitcast_fusion), channel_id=1, source_target_pairs={{0,4},{4,0},{8,12},{12,8},{1,5},{5,1},{9,13},{13,9},{2,6},{6,2},{1... | collective-permute-start | bytes 9224 | tf_op jit(solution)/shard_map/ppermute | solution.py:47
  78.2 6.5 %collective-permute-start.19 = (bf16[128,768]{1,0:T(8,128)(2,1)S(1)}, bf16[128,768]{1,0:T(8,128)(2,1)S(1)}, u32[]{:S(2)}, u32[]{:S(2)}) collective-permute-start(bf16[128,768]{1,0:T(8,128)(2,1)S(1)} %convert_element_type.225), channel_id=1, source_target_pairs={{0,1},{1,0},{2,3},{3,2},{4,5},{5,4},{6,7},{7,6},{8,9},{9,8},{10,11... | collective-permute-start | bytes 589832 | tf_op jit(solution)/shard_map/ppermute | solution.py:47
  87.8 1.9 collective-permute-start.20
  88.4 16.2 %collective-permute-start.18 = (bf16[128,768]{1,0:T(8,128)(2,1)}, bf16[128,768]{1,0:T(8,128)(2,1)}, u32[]{:S(2)}, u32[]{:S(2)}) collective-permute-start(bf16[128,768]{1,0:T(8,128)(2,1)} %get-tuple-element.49), channel_id=1, source_target_pairs={{0,1},{1,0},{2,3},{3,2},{4,5},{5,4},{6,7},{7,6},{8,9},{9,8},{10,11... | collective-permute-start | bytes 589832 | tf_op jit(solution)/shard_map/ppermute | solution.py:47
  89.7 7.3 %collective-permute-start.21 = (bf16[128,768]{1,0:T(8,128)(2,1)S(1)}, bf16[128,768]{1,0:T(8,128)(2,1)S(1)}, u32[]{:S(2)}, u32[]{:S(2)}) collective-permute-start(bf16[128,768]{1,0:T(8,128)(2,1)S(1)} %fusion.42), channel_id=1, source_target_pairs={{0,2},{1,3},{2,0},{3,1},{4,6},{5,7},{6,4},{7,5},{8,10},{9,11},{10,... | collective-permute-start | bytes 589832 | tf_op jit(solution)/shard_map/ppermute | solution.py:47
  92.4 35.1 %collective-permute-start.43 = (bf16[384,768]{1,0:T(8,128)(2,1)}, bf16[384,768]{1,0:T(8,128)(2,1)}, u32[]{:S(2)}, u32[]{:S(2)}) collective-permute-start(bf16[384,768]{1,0:T(8,128)(2,1)} %convolution_convert_fusion.1), channel_id=1, source_target_pairs={{0,16},{16,0},{1,17},{17,1},{2,18},{18,2},{3,19},{19,3},{4,20},{20... | collective-permute-start | bytes 1769480 | tf_op jit(solution)/shard_map/ppermute | solution.py:47
  100.8 2.2 collective-permute-start.39
  104.4 3.9 %collective-permute-start.40 = (f32[5376]{0:T(1024)S(1)}, f32[5376]{0:T(1024)S(1)}, u32[]{:S(2)}, u32[]{:S(2)}) collective-permute-start(f32[5376]{0:T(1024)S(1)} %pad_maximum_fusion.17), channel_id=1, source_target_pairs={{0,4},{4,0},{8,12},{12,8},{1,5},{5,1},{9,13},{13,9},{2,6},{6,2},{1... | collective-permute-start | bytes 64520 | tf_op jit(solution)/shard_map/ppermute | solution.py:47
  108.3 4.7 %collective-permute-start.41 = (f32[5376]{0:T(1024)S(1)}, f32[5376]{0:T(1024)S(1)}, u32[]{:S(2)}, u32[]{:S(2)}) collective-permute-start(f32[5376]{0:T(1024)S(1)} %fusion.87), channel_id=1, source_target_pairs={{0,8},{4,12},{8,0},{12,4},{1,9},{5,13},{9,1},{13,5},{2,10},{6,14},... | collective-permute-start | bytes 64520 | tf_op jit(solution)/shard_map/ppermute | solution.py:47
  109.4 22.3 %collective-permute-start.48 = (bf16[768,384]{1,0:T(8,128)(2,1)}, bf16[768,384]{1,0:T(8,128)(2,1)}, u32[]{:S(2)}, u32[]{:S(2)}) collective-permute-start(bf16[768,384]{1,0:T(8,128)(2,1)} %convolution_convert_fusion), channel_id=1, source_target_pairs={{0,16},{16,0},{1,17},{17,1},{2,18},{18,2},{3,19},{19,3},{4,20},{20... | collective-permute-start | bytes 1769480 | tf_op jit(solution)/shard_map/ppermute | solution.py:47
  113.0 12.1 %collective-permute-start.42 = (f32[5376]{0:T(1024)S(1)}, f32[5376]{0:T(1024)S(1)}, u32[]{:S(2)}, u32[]{:S(2)}) collective-permute-start(f32[5376]{0:T(1024)S(1)} %add.319), channel_id=1, source_target_pairs={{0,16},{16,0},{1,17},{17,1},{2,18},{18,2},{3,19},{19,3},{4,20},{20... | collective-permute-start | bytes 64520 | tf_op jit(solution)/shard_map/ppermute | solution.py:47
  116.1 18.2 %collective-permute-start.25 = (bf16[128,768]{1,0:T(8,128)(2,1)}, bf16[128,768]{1,0:T(8,128)(2,1)}, u32[]{:S(2)}, u32[]{:S(2)}) collective-permute-start(bf16[128,768]{1,0:T(8,128)(2,1)} %convert_element_type.231), channel_id=1, source_target_pairs={{0,1},{1,0},{2,3},{3,2},{4,5},{5,4},{6,7},{7,6},{8,9},{9,8},{10,11... | collective-permute-start | bytes 589832 | tf_op jit(solution)/shard_map/ppermute | solution.py:47
  130.0 68.9 %collective-permute-start.44 = (bf16[192,768]{1,0:T(8,128)(2,1)}, bf16[192,768]{1,0:T(8,128)(2,1)}, u32[]{:S(2)}, u32[]{:S(2)}) collective-permute-start(bf16[192,768]{1,0:T(8,128)(2,1)} %dynamic-slice_convert_fusion.1), channel_id=1, source_target_pairs={{0,4},{4,0},{8,12},{12,8},{1,5},{5,1},{9,13},{13,9},{2,6},{6,2},{1... | collective-permute-start | bytes 884744 | tf_op jit(solution)/shard_map/ppermute | solution.py:47
  134.0 67.8 %collective-permute-start.49 = (bf16[384,384]{1,0:T(8,128)(2,1)}, bf16[384,384]{1,0:T(8,128)(2,1)}, u32[]{:S(2)}, u32[]{:S(2)}) collective-permute-start(bf16[384,384]{1,0:T(8,128)(2,1)} %dynamic-slice_convert_fusion), channel_id=1, source_target_pairs={{0,4},{4,0},{8,12},{12,8},{1,5},{5,1},{9,13},{13,9},{2,6},{6,2},{1... | collective-permute-start | bytes 884744 | tf_op jit(solution)/shard_map/ppermute | solution.py:47
  136.9 12.5 %collective-permute-start.26 = (bf16[256,192]{0,1:T(8,128)(2,1)S(1)}, bf16[256,192]{0,1:T(8,128)(2,1)S(1)}, u32[]{:S(2)}, u32[]{:S(2)}) collective-permute-start(bf16[256,192]{0,1:T(8,128)(2,1)S(1)} %fusion.13), channel_id=1, source_target_pairs={{0,12},{4,8},{8,4},{12,0},{1,13},{5,9},{9,5},{13,1},{2,14},{6,10},... | collective-permute-start | bytes 294920 | tf_op jit(solution)/shard_map/ppermute | solution.py:47
  138.5 12.5 %collective-permute-start.27 = (bf16[256,192]{0,1:T(8,128)(2,1)S(1)}, bf16[256,192]{0,1:T(8,128)(2,1)S(1)}, u32[]{:S(2)}, u32[]{:S(2)}) collective-permute-start(bf16[256,192]{0,1:T(8,128)(2,1)S(1)} %fusion.13), channel_id=1, source_target_pairs={{0,8},{4,12},{8,0},{12,4},{1,9},{5,13},{9,1},{13,5},{2,10},{6,14},... | collective-permute-start | bytes 294920 | tf_op jit(solution)/shard_map/ppermute | solution.py:47
  140.2 10.8 %collective-permute-start.28 = (bf16[256,192]{0,1:T(8,128)(2,1)S(1)}, bf16[256,192]{0,1:T(8,128)(2,1)S(1)}, u32[]{:S(2)}, u32[]{:S(2)}) collective-permute-start(bf16[256,192]{0,1:T(8,128)(2,1)S(1)} %fusion.13), channel_id=1, source_target_pairs={{0,4},{4,0},{8,12},{12,8},{1,5},{5,1},{9,13},{13,9},{2,6},{6,2},{1... | collective-permute-start | bytes 294920 | tf_op jit(solution)/shard_map/ppermute | solution.py:47
  149.5 31.8 %collective-permute-start.34 = (bf16[192,384]{1,0:T(8,128)(2,1)}, bf16[192,384]{1,0:T(8,128)(2,1)}, u32[]{:S(2)}, u32[]{:S(2)}) collective-permute-start(bf16[192,384]{1,0:T(8,128)(2,1)} %convolution_convert_fusion.3), channel_id=1, source_target_pairs={{0,16},{16,0},{1,17},{17,1},{2,18},{18,2},{3,19},{19,3},{4,20},{20... | collective-permute-start | bytes 442376 | tf_op jit(solution)/shard_map/ppermute | solution.py:47
  178.4 28.5 %collective-permute-start.29 = (bf16[128,768]{1,0:T(8,128)(2,1)}, bf16[128,768]{1,0:T(8,128)(2,1)}, u32[]{:S(2)}, u32[]{:S(2)}) collective-permute-start(bf16[128,768]{1,0:T(8,128)(2,1)} %fusion.49), channel_id=1, source_target_pairs={{0,1},{1,0},{2,3},{3,2},{4,5},{5,4},{6,7},{7,6},{8,9},{9,8},{10,11... | collective-permute-start | bytes 589832 | tf_op jit(solution)/shard_map/ppermute | solution.py:47
  180.0 48.2 %collective-permute-start.32 = (bf16[384,576]{0,1:T(8,128)(2,1)}, bf16[384,576]{0,1:T(8,128)(2,1)}, u32[]{:S(2)}, u32[]{:S(2)}) collective-permute-start(bf16[384,576]{0,1:T(8,128)(2,1)} %convolution_convert_fusion.2), channel_id=1, source_target_pairs={{0,16},{16,0},{1,17},{17,1},{2,18},{18,2},{3,19},{19,3},{4,20},{20... | collective-permute-start | bytes 1327112 | tf_op jit(solution)/shard_map/ppermute | solution.py:47
  182.7 4.5 %collective-permute-start.35 = (bf16[96,384]{1,0:T(8,128)(2,1)S(1)}, bf16[96,384]{1,0:T(8,128)(2,1)S(1)}, u32[]{:S(2)}, u32[]{:S(2)}) collective-permute-start(bf16[96,384]{1,0:T(8,128)(2,1)S(1)} %dynamic-slice_convert_fusion.4), channel_id=1, source_target_pairs={{0,4},{4,0},{8,12},{12,8},{1,5},{5,1},{9,13},{13,9},{2,6},{6,2},{1... | collective-permute-start | bytes 221192 | tf_op jit(solution)/shard_map/ppermute | solution.py:47
  187.1 5.8 %collective-permute-start.33 = (f32[2,192]{1,0:T(2,128)S(1)}, f32[2,192]{1,0:T(2,128)S(1)}, u32[]{:S(2)}, u32[]{:S(2)}) collective-permute-start(f32[2,192]{1,0:T(2,128)S(1)} %pad_maximum_fusion.18), channel_id=1, source_target_pairs={{0,16},{16,0},{1,17},{17,1},{2,18},{18,2},{3,19},{19,3},{4,20},{20... | collective-permute-start | bytes 4616 | tf_op jit(solution)/shard_map/ppermute | solution.py:47
  192.9 4.9 %collective-permute-start.36 = (bf16[48,384]{1,0:T(8,128)(2,1)S(1)}, bf16[48,384]{1,0:T(8,128)(2,1)S(1)}, u32[]{:S(2)}, u32[]{:S(2)}) collective-permute-start(bf16[48,384]{1,0:T(8,128)(2,1)S(1)} %dynamic-slice_convert_fusion.5), channel_id=1, source_target_pairs={{0,8},{4,12},{8,0},{12,4},{1,9},{5,13},{9,1},{13,5},{2,10},{6,14},... | collective-permute-start | bytes 110600 | tf_op jit(solution)/shard_map/ppermute | solution.py:47
  197.7 7.3 %collective-permute-start.37 = (bf16[48,384]{1,0:T(8,128)(2,1)S(1)}, bf16[48,384]{1,0:T(8,128)(2,1)S(1)}, u32[]{:S(2)}, u32[]{:S(2)}) collective-permute-start(bf16[48,384]{1,0:T(8,128)(2,1)S(1)} %add_convert_fusion.3), channel_id=1, source_target_pairs={{0,8},{4,12},{8,0},{12,4},{1,9},{5,13},{9,1},{13,5},{2,10},{6,14},... | collective-permute-start | bytes 110600 | tf_op jit(solution)/shard_map/ppermute | solution.py:47
  199.9 12.9 %collective-permute-start.45 = (bf16[96,768]{1,0:T(8,128)(2,1)S(1)}, bf16[96,768]{1,0:T(8,128)(2,1)S(1)}, u32[]{:S(2)}, u32[]{:S(2)}) collective-permute-start(bf16[96,768]{1,0:T(8,128)(2,1)S(1)} %dynamic-slice_convert_fusion.3), channel_id=1, source_target_pairs={{0,8},{4,12},{8,0},{12,4},{1,9},{5,13},{9,1},{13,5},{2,10},{6,14},... | collective-permute-start | bytes 442376 | tf_op jit(solution)/shard_map/ppermute | solution.py:47
  202.9 14.0 %collective-permute-start.50 = (bf16[192,384]{1,0:T(8,128)(2,1)S(1)}, bf16[192,384]{1,0:T(8,128)(2,1)S(1)}, u32[]{:S(2)}, u32[]{:S(2)}) collective-permute-start(bf16[192,384]{1,0:T(8,128)(2,1)S(1)} %dynamic-slice_convert_fusion.2), channel_id=1, source_target_pairs={{0,8},{4,12},{8,0},{12,4},{1,9},{5,13},{9,1},{13,5},{2,10},{6,14},... | collective-permute-start | bytes 442376 | tf_op jit(solution)/shard_map/ppermute | solution.py:47
  205.1 4.6 %collective-permute-start.38 = (bf16[96,384]{1,0:T(8,128)(2,1)S(1)}, bf16[96,384]{1,0:T(8,128)(2,1)S(1)}, u32[]{:S(2)}, u32[]{:S(2)}) collective-permute-start(bf16[96,384]{1,0:T(8,128)(2,1)S(1)} %maximum_select_fusion.12), channel_id=1, source_target_pairs={{0,4},{4,0},{8,12},{12,8},{1,5},{5,1},{9,13},{13,9},{2,6},{6,2},{1... | collective-permute-start | bytes 221192 | tf_op jit(solution)/shard_map/ppermute | solution.py:47
  207.8 9.3 %collective-permute-start.30 = (bf16[128,768]{1,0:T(8,128)(2,1)S(1)}, bf16[128,768]{1,0:T(8,128)(2,1)S(1)}, u32[]{:S(2)}, u32[]{:S(2)}) collective-permute-start(bf16[128,768]{1,0:T(8,128)(2,1)S(1)} %fusion.39), channel_id=1, source_target_pairs={{0,2},{1,3},{2,0},{3,1},{4,6},{5,7},{6,4},{7,5},{8,10},{9,11},{10,... | collective-permute-start | bytes 589832 | tf_op jit(solution)/shard_map/ppermute | solution.py:47
  212.9 12.6 %collective-permute-start.46 = (bf16[96,768]{1,0:T(8,128)(2,1)S(1)}, bf16[96,768]{1,0:T(8,128)(2,1)S(1)}, u32[]{:S(2)}, u32[]{:S(2)}) collective-permute-start(bf16[96,768]{1,0:T(8,128)(2,1)S(1)} %add_convert_fusion.2), channel_id=1, source_target_pairs={{0,8},{4,12},{8,0},{12,4},{1,9},{5,13},{9,1},{13,5},{2,10},{6,14},... | collective-permute-start | bytes 442376 | tf_op jit(solution)/shard_map/ppermute | solution.py:47
  217.0 11.0 %collective-permute-start.51 = (bf16[192,384]{1,0:T(8,128)(2,1)S(1)}, bf16[192,384]{1,0:T(8,128)(2,1)S(1)}, u32[]{:S(2)}, u32[]{:S(2)}) collective-permute-start(bf16[192,384]{1,0:T(8,128)(2,1)S(1)} %add_convert_fusion.1), channel_id=1, source_target_pairs={{0,8},{4,12},{8,0},{12,4},{1,9},{5,13},{9,1},{13,5},{2,10},{6,14},... | collective-permute-start | bytes 442376 | tf_op jit(solution)/shard_map/ppermute | solution.py:47
  217.2 24.5 %collective-permute-start.31 = (f32[128,768]{1,0:T(8,128)S(1)}, f32[128,768]{1,0:T(8,128)S(1)}, u32[]{:S(2)}, u32[]{:S(2)}) collective-permute-start(f32[128,768]{1,0:T(8,128)S(1)} %add_add_fusion), channel_id=1, source_target_pairs={{0,1},{1,0},{2,3},{3,2},{4,5},{5,4},{6,7},{7,6},{8,9},{9,8},{10,11... | collective-permute-start | bytes 1179656 | tf_op jit(solution)/shard_map/ppermute | solution.py:47
  225.6 10.0 %collective-permute-start.47 = (bf16[192,768]{1,0:T(8,128)(2,1)S(1)}, bf16[192,768]{1,0:T(8,128)(2,1)S(1)}, u32[]{:S(2)}, u32[]{:S(2)}) collective-permute-start(bf16[192,768]{1,0:T(8,128)(2,1)S(1)} %maximum_select_fusion.9), channel_id=1, source_target_pairs={{0,4},{4,0},{8,12},{12,8},{1,5},{5,1},{9,13},{13,9},{2,6},{6,2},{1... | collective-permute-start | bytes 884744 | tf_op jit(solution)/shard_map/ppermute | solution.py:47
  228.1 12.4 %collective-permute-start.52 = (bf16[384,384]{1,0:T(8,128)(2,1)S(1)}, bf16[384,384]{1,0:T(8,128)(2,1)S(1)}, u32[]{:S(2)}, u32[]{:S(2)}) collective-permute-start(bf16[384,384]{1,0:T(8,128)(2,1)S(1)} %maximum_select_fusion.10), channel_id=1, source_target_pairs={{0,4},{4,0},{8,12},{12,8},{1,5},{5,1},{9,13},{13,9},{2,6},{6,2},{1... | collective-permute-start | bytes 884744 | tf_op jit(solution)/shard_map/ppermute | solution.py:47
  (47 other events, 551.6 us)

commit v2 on v1

v2 whole, which is shorter than its diff:
```python
import functools

import jax
import jax.experimental.pallas as pl
import jax.experimental.pallas.tpu as pltpu
import jax.numpy as jnp
from jax import lax
from jax.sharding import PartitionSpec as P

HD = 64
EPSILON = 1e-05
NEG_FILL = -1e30
ROOT_HALF = 0.7071067811865476
DENSITY_FACTOR = 0.3989422804014327
BF = jnp.bfloat16
F32 = jnp.float32


def product(left, right):
    return jnp.dot(left, right, preferred_element_type=F32)


def product_left(left, right):
    return lax.dot_general(left, right, (((0,), (0,)), ((), ())), preferred_element_type=F32)


def product_right(left, right):
    return lax.dot_general(left, right, (((1,), (1,)), ((), ())), preferred_element_type=F32)


def normalize(summed):
    center = summed - jnp.mean(summed, axis=-1, keepdims=True)
    inverse = lax.rsqrt(jnp.mean(center * center, axis=-1, keepdims=True) + EPSILON)
    return center * inverse, inverse


def normalize_back(grad_output, normed, inverse, gain_vector):
    scaled = grad_output * gain_vector
    return inverse * (
        scaled
        - jnp.mean(scaled, axis=-1, keepdims=True)
        - normed * jnp.mean(scaled * normed, axis=-1, keepdims=True)
    )


VMEM = pl.BlockSpec(memory_space=pltpu.VMEM)
FAR = pl.BlockSpec(memory_space=pltpu.HBM)
ANYWHERE = pl.BlockSpec(memory_space=pl.ANY)
PARAMS = pltpu.CompilerParams(vmem_limit_bytes=40 * 1024 * 1024)


def after(value, *others):
    zero = jnp.zeros((), F32)
    for other in others:
        first = lax.slice(other, (0,) * other.ndim, (1,) * other.ndim).reshape(())
        zero = zero + jnp.minimum(jnp.abs(first.astype(F32)), 0.0)
    return value + zero.astype(value.dtype)


def softmax_block(keys, queries, same):
    scores = jnp.where(same, product_right(keys, queries) * HD**-0.5, NEG_FILL)
    exponent = jnp.exp(scores - jnp.max(scores, axis=0, keepdims=True))
    total = jnp.sum(exponent, axis=0, keepdims=True)
    return (exponent * (1.0 / total)).astype(BF)


def as_column(row):
    return jnp.broadcast_to(row, (8, row.shape[1])).T[:, :1]


def block_start(number, rows):
    return pl.multiple_of((lax.axis_index("context") ^ number) * rows, rows)


def front_kernel(heads, packs, paired, *refs):
    blocks, refs = refs[: 2 * packs], refs[2 * packs :]
    groups = 2 if paired else 1
    b_ref, weights, refs = refs[0], refs[1 : 1 + groups], refs[1 + groups :]
    q_ref, k_ref, v_ref, c_ref, x_ref, row_ref = refs
    width = heads * HD
    model = x_ref.shape[1]
    rows = c_ref.shape[0]
    half = rows // 2
    step = model // groups
    for number in range(packs):
        for which in range(2):
            block = blocks[2 * number + which]
            at = pl.multiple_of(block_start(number, rows) + which * half, half)
            if paired:
                first = lax.axis_index("weight") == 0
                left, right = block[:half, :step], block[:half, step:]
                x_ref[pl.ds(at, half), :step] = jnp.where(first, left, right)
                x_ref[pl.ds(at, half), step:] = jnp.where(first, right, left)
            else:
                x_ref[pl.ds(at, half)] = block[:half]
            row_ref[:, pl.ds(at, half)] = block[half : half + 1, :half].astype(F32)
    for number, (out_ref, bias) in enumerate(((q_ref, 0), (k_ref, None), (v_ref, 1))):
        total = None
        for group in range(groups):
            part = product(
                x_ref[:, group * step : (group + 1) * step],
                weights[group][:, number * width : (number + 1) * width],
            )
            total = part if total is None else total + part
        if bias is not None:
            total = total + b_ref[bias : bias + 1]
        out_ref[...] = total.astype(BF)
    at = block_start(0, rows)
    same = as_column(row_ref[...]) == row_ref[:, pl.ds(at, rows)]
    for head in range(heads):
        lanes = slice(head * HD, (head + 1) * HD)
        probability = softmax_block(k_ref[:, lanes], q_ref[pl.ds(at, rows), lanes], same)
        c_ref[:, lanes] = product(v_ref[:, lanes].T, probability).T.astype(BF)


def front(blocks, biases, groups):
    packs = len(blocks) // 2
    rows = 2 * (blocks[0].shape[0] - 16)
    model = blocks[0].shape[1]
    width = biases.shape[1]
    whole = jax.ShapeDtypeStruct((packs * rows, width), BF)
    return pl.pallas_call(
        functools.partial(front_kernel, width // HD, packs, len(groups) == 2),
        out_shape=(
            whole,
            whole,
            whole,
            jax.ShapeDtypeStruct((rows, width), BF),
            jax.ShapeDtypeStruct((packs * rows, model), BF),
            jax.ShapeDtypeStruct((1, packs * rows), F32),
        ),
        in_specs=[VMEM] * (2 * packs + 1 + len(groups)),
        out_specs=(VMEM,) * 6,
        compiler_params=PARAMS,
    )(*blocks, biases, *groups)


def probability_kernel(heads, block, q_ref, k_ref, row_ref, *refs):
    a_hbm, a_ref, copy_sems = refs[-3:]
    count = q_ref.shape[0] // block

    def copy(number):
        at = pl.multiple_of(number * block, block)
        return pltpu.make_async_copy(
            a_ref.at[:, :, pl.ds(at, block)],
            a_hbm.at[:, :, pl.ds(at, block)],
            copy_sems.at[number],
        )

    def body(number, carry):
        at = pl.multiple_of(number * block, block)
        same = as_column(row_ref[...]) == row_ref[:, pl.ds(at, block)]
        for head in range(heads):
            lanes = slice(head * HD, (head + 1) * HD)
            a_ref[head, :, pl.ds(at, block)] = softmax_block(
                k_ref[:, lanes], q_ref[pl.ds(at, block), lanes], same
            )
        copy(number).start()
        return carry

    lax.fori_loop(0, count, body, 0)
    for number in range(count):
        copy(number).wait()


def probabilities(queries, keys, segments, gates):
    length, width = queries.shape
    heads = width // HD
    block = 256
    return pl.pallas_call(
        functools.partial(probability_kernel, heads, block),
        out_shape=jax.ShapeDtypeStruct((heads, length, length), BF),
        in_specs=[VMEM] * 3 + [ANYWHERE] * len(gates),
        out_specs=FAR,
        scratch_shapes=[
            pltpu.VMEM((heads, length, length), BF),
            pltpu.SemaphoreType.DMA((length // block,)),
        ],
        compiler_params=PARAMS,
    )(queries, keys, segments, *gates)


def attention_back_kernel(heads, packs, a_hbm, q_ref, k_ref, v_ref, *refs):
    blocks, (p_ref, b_ref, a_ref, c_ref, copy_sems) = refs[:packs], refs[-5:]
    width = heads * HD
    scale = jnp.asarray(HD**-0.5, BF)
    copies = [
        pltpu.make_async_copy(a_hbm.at[head], a_ref.at[head], copy_sems.at[head])
        for head in range(heads)
    ]
    for copy in copies:
        copy.start()
    for number, block in enumerate(blocks):
        rows = block.shape[0]
        c_ref[pl.ds(block_start(number, rows), rows)] = block[...]
    for head in range(heads):
        lanes = slice(head * HD, (head + 1) * HD)
        grad_context = c_ref[:, lanes]
        copies[head].wait()
        low = a_ref[head]
        wide = low.astype(F32)
        weighted = wide * product_right(v_ref[:, lanes], grad_context)
        row_dot = jnp.sum(weighted, axis=0, keepdims=True)
        grad_scores = (weighted - wide * row_dot).astype(BF)
        grad_values = product(low, grad_context)
        grad_keys = product(grad_scores, q_ref[:, lanes] * scale)
        grad_queries = product((k_ref[:, lanes] * scale).T, grad_scores).T
        p_ref[:, lanes] = grad_queries.astype(BF)
        p_ref[:, width + head * HD : width + (head + 1) * HD] = grad_keys.astype(BF)
        p_ref[:, 2 * width + head * HD : 2 * width + (head + 1) * HD] = grad_values.astype(BF)
        b_ref[0:1, lanes] = jnp.sum(grad_queries, axis=0, keepdims=True)
        b_ref[1:2, lanes] = jnp.sum(grad_values, axis=0, keepdims=True)


def attention_back(probability, queries, keys, values, blocks, gates):
    length, width = queries.shape
    heads = width // HD
    return pl.pallas_call(
        functools.partial(attention_back_kernel, heads, len(blocks)),
        out_shape=(
            jax.ShapeDtypeStruct((length, 3 * width), BF),
            jax.ShapeDtypeStruct((2, width), F32),
        ),
        in_specs=[FAR] + [VMEM] * (3 + len(blocks)) + [ANYWHERE] * len(gates),
        out_specs=(VMEM, VMEM),
        scratch_shapes=[
            pltpu.VMEM((heads, length, length), BF),
            pltpu.VMEM((length, width), BF),
            pltpu.SemaphoreType.DMA((heads,)),
        ],
        compiler_params=PARAMS,
        cost_estimate=pl.CostEstimate(
            flops=10_000_000_000, bytes_accessed=10_000_000, transcendentals=0
        ),
    )(probability, queries, keys, values, *blocks, *gates)


def place_bit(bit):
    return (lax.axis_index("context") // bit) % 2 == 0


def halves_out(value, bit, own_ref, other_ref):
    rows = own_ref.shape[0]
    low = place_bit(bit)
    own_ref[...] = jnp.where(low, value[:rows], value[rows:])
    other_ref[...] = jnp.where(low, value[rows:], value[:rows]).astype(BF)


def pair_grad_kernel(left, left_pair, right, right_pair, _, own_ref, other_ref):
    value = product_left(left[...], right[...]) + product_left(left_pair[...], right_pair[...])
    halves_out(value, 1, own_ref, other_ref)


def pair_grad(left, left_pair, right, right_pair, gate):
    shape = (left.shape[1] // 2, right.shape[1])
    return pl.pallas_call(
        pair_grad_kernel,
        out_shape=(jax.ShapeDtypeStruct(shape, F32), jax.ShapeDtypeStruct(shape, BF)),
        in_specs=[VMEM] * 4 + [ANYWHERE],
        out_specs=(VMEM,) * 2,
        compiler_params=PARAMS,
    )(left, left_pair, right, right_pair, gate)


def column_grad_kernel(extra, left, right, *refs):
    mine_ref, sent_ref = refs[-2:]
    rows, step = left.shape[1], mine_ref.shape[1]
    sent_ref[:rows] = product_left(left[...], right[:, step:]).astype(BF)
    mine_ref[:rows] = product_left(left[...], right[:, :step])
    if extra:
        low = refs[0][...].astype(BF)
        sent_ref[rows:] = low
        mine_ref[rows:] = low.astype(F32)


def column_grad(left, right, gate, extra=None):
    rows = left.shape[1] + (0 if extra is None else extra.shape[0])
    shape = (rows, right.shape[1] // 2)
    more = [] if extra is None else [extra]
    return pl.pallas_call(
        functools.partial(column_grad_kernel, len(more)),
        out_shape=(jax.ShapeDtypeStruct(shape, F32), jax.ShapeDtypeStruct(shape, BF)),
        in_specs=[VMEM] * (2 + len(more)) + [ANYWHERE],
        out_specs=(VMEM,) * 2,
        compiler_params=PARAMS,
    )(left, right, *more, gate)


def sent_grad_kernel(left, right, sums, sent_ref):
    step = left.shape[1] // 2
    sent_ref[:step] = product_left(left[:, step:], right[...]).astype(BF)
    sent_ref[step:] = jnp.zeros_like(sent_ref[step:])
    sent_ref[step : step + 2, : sums.shape[1]] = sums[...].astype(BF)


def sent_grad(left, right, sums):
    return pl.pallas_call(
        sent_grad_kernel,
        out_shape=jax.ShapeDtypeStruct((left.shape[1] // 2 + 16, right.shape[1]), BF),
        in_specs=[VMEM] * 3,
        out_specs=VMEM,
        compiler_params=PARAMS,
    )(left, right, sums)


def split_kernel(count, bit, *refs):
    value = refs[0][...].astype(F32)
    for other in refs[1:count]:
        value = value + other[...].astype(F32)
    halves_out(value, bit, *refs[-2:])


def split(values, bit, gates=()):
    shape = (values[0].shape[0] // 2, values[0].shape[1])
    return pl.pallas_call(
        functools.partial(split_kernel, len(values), bit),
        out_shape=(jax.ShapeDtypeStruct(shape, F32), jax.ShapeDtypeStruct(shape, BF)),
        in_specs=[VMEM] * len(values) + [ANYWHERE] * len(gates),
        out_specs=(VMEM,) * 2,
        compiler_params=PARAMS,
    )(*values, *gates)


def add_kernel(own_ref, other_ref, *refs):
    refs[-1][...] = (own_ref[...] + other_ref[...].astype(F32)).astype(BF)


def add_low(own, other, gates=()):
    return pl.pallas_call(
        add_kernel,
        out_shape=jax.ShapeDtypeStruct(own.shape, BF),
        in_specs=[VMEM] * 2 + [ANYWHERE] * len(gates),
        out_specs=VMEM,
        compiler_params=PARAMS,
    )(own, other, *gates)


def join_kernel(bit, own_ref, other_ref, *refs):
    rows = own_ref.shape[0]
    low = place_bit(bit)
    own, other = own_ref[...], other_ref[...]
    refs[-1][:rows] = jnp.where(low, own, other).astype(refs[-1].dtype)
    refs[-1][rows:] = jnp.where(low, other, own).astype(refs[-1].dtype)


def join(own, other, bit, dtype, gates=()):
    return pl.pallas_call(
        functools.partial(join_kernel, bit),
        out_shape=jax.ShapeDtypeStruct((2 * own.shape[0], own.shape[1]), dtype),
        in_specs=[VMEM] * 2 + [ANYWHERE] * len(gates),
        out_specs=VMEM,
        compiler_params=PARAMS,
    )(own, other, *gates)


def sums_kernel(one, two, first, normed_one, top, normed_two, _, out_ref):
    def put(row, value):
        out_ref[row : row + 1] = jnp.sum(value, axis=0, keepdims=True)

    put(0, one[...])
    put(1, two[...])
    put(2, first[...] * normed_one[...])
    put(3, top[...] * normed_two[...])
    put(4, first[...])
    put(5, top[...])


def row_sums(*operands):
    return pl.pallas_call(
        sums_kernel,
        out_shape=jax.ShapeDtypeStruct((6, operands[0].shape[1]), F32),
        in_specs=[VMEM] * 6 + [ANYWHERE],
        out_specs=VMEM,
        compiler_params=PARAMS,
    )(*operands)


def build(mesh):
    count = dict(mesh.shape)
    paired = count["weight"] == 2

    def flip(value, axis, bit):
        return lax.ppermute(value, axis, [(i, i ^ bit) for i in range(count[axis])])

    def bits(axis):
        bit, found = 1, []
        while bit < count[axis]:
            found.append(bit)
            bit *= 2
        return found

    def shards(
        tokens,
        segments,
        query_key_value_weight,
        input_bias,
        output_weight,
        row_bias,
        norm_gain,
        norm_bias,
        up_weight,
        up_bias,
        down_weight,
        cotangent,
    ):
        weight_at = lax.axis_index("weight")
        context_at = lax.axis_index("context")
        core_at = lax.axis_index("tensor") % 2
        rows, width = tokens.shape
        half = rows // 2
        shard_width = input_bias.shape[2]
        heads = shard_width // HD
        packs = count["context"]

        def columns(value):
            if not paired:
                return value
            middle = value.shape[-1] // 2
            swapped = jnp.concatenate([value[..., middle:], value[..., :middle]], axis=-1)
            return jnp.where(weight_at == 0, value, swapped)

        def own_rows(value):
            middle = value.shape[0] // 2
            swapped = jnp.concatenate([value[middle:], value[:middle]], axis=0)
            return jnp.where(core_at == 0, value, swapped)

        def swapped(value):
            return flip(value, "weight", 1)

        def gather_weight(value, axis):
            if paired:
                return [value, flip(value, "weight", 1)]
            return [lax.all_gather(value, "weight", axis=axis, tiled=True)]

        def contract(value, groups):
            step = width // len(groups)
            total = product(value[:, :step], groups[0])
            for number in range(1, len(groups)):
                total = total + product(
                    value[:, number * step : (number + 1) * step], groups[number]
                )
            return total

        def expand(value, groups):
            parts = [product(value, group) for group in groups]
            return parts[0] if len(parts) == 1 else jnp.concatenate(parts, axis=1)

        def contract_right(value, groups):
            step = width // len(groups)
            total = product_right(value[:, :step], groups[0])
            for number in range(1, len(groups)):
                total = total + product_right(
                    value[:, number * step : (number + 1) * step], groups[number]
                )
            return total

        def expand_right(value, groups):
            parts = [product_right(value, group) for group in groups]
            return parts[0] if len(parts) == 1 else jnp.concatenate(parts, axis=1)

        def row_total(partial):
            mine, theirs = partial[:half], partial[half:].astype(BF)
            total = mine + flip(theirs, "tensor", 1).astype(F32)
            for bit in bits("tensor")[1:]:
                low = total.astype(BF)
                total = low.astype(F32) + flip(low, "tensor", bit).astype(F32)
            return total, low

        def both_halves(value):
            return jnp.concatenate([value, flip(value, "tensor", 1)], axis=0)

        def take_half(value, which):
            middle = value.shape[0] // 2
            return lax.dynamic_slice_in_dim(value, which * middle, middle, axis=0)

        def context_total(value):
            return lax.psum(value.astype(BF), "context").astype(F32)

        def finish_total(halves, gates, done=0):
            order = bits("context")
            for number, bit in enumerate(order):
                if number < done:
                    continue
                received = flip(halves[1], "context", bit)
                if number + 1 < len(order):
                    halves = split([halves[0], received], order[number + 1], gates[number])
            summed = low = add_low(halves[0], received, gates[len(order) - 1])
            for number, bit in enumerate(reversed(order)):
                kind = F32 if number + 1 == len(order) else BF
                received = flip(low, "context", bit)
                low = join(low, received, bit, kind, gates[len(order) + number])
            return low, summed

        def context_blocks(value):
            blocks = [value]
            for bit in reversed(bits("context")):
                blocks = blocks + [flip(block, "context", bit) for block in blocks]
            order = [0]
            for bit in reversed(bits("context")):
                order = order + [at ^ bit for at in order]
            return [blocks[order.index(j)] for j in range(packs)]

        def in_order(blocks):
            placed = []
            for at in range(packs):
                chosen = blocks[0]
                for j in range(1, packs):
                    chosen = jnp.where(context_at == (at ^ j), blocks[j], chosen)
                placed.append(chosen)
            return jnp.concatenate(placed, axis=0)

        gains, shifts, row_pair = columns(norm_gain[0]), columns(norm_bias[0]), columns(row_bias[0])
        cotangent_rows = columns(take_half(cotangent, core_at)).astype(F32)

        projection = query_key_value_weight[0].reshape(-1, 3 * shard_width)
        input_groups = gather_weight(projection, 0)

        def with_segments(which):
            numbers = take_half(segments, which).astype(BF)
            numbers = jnp.pad(numbers[None], ((0, 15), (0, width - half)))
            return jnp.concatenate([take_half(tokens, which), numbers], axis=0)

        halves = context_blocks(with_segments(core_at))
        up_groups = gather_weight(after(up_weight[0], halves[1]), 0)
        output_groups = gather_weight(after(output_weight[0], halves[2 % packs]), 1)
        down_groups = gather_weight(after(down_weight[0], halves[3 % packs]), 1)
        others = [with_segments(1 - core_at)] + [flip(block, "tensor", 1) for block in halves[1:]]
        blocks = [block for pair in zip(halves, others) for block in pair]
        pack_queries, pack_keys, pack_values, context, pack_rows, pack_segments = front(
            blocks, input_bias[0], input_groups
        )

        def own_block(value):
            return lax.dynamic_slice_in_dim(value, context_at * rows, rows, 0)

        hidden_half = columns(take_half(tokens, core_at)).astype(F32)
        total, sent = row_total(expand(context, output_groups))
        pack_probability = probabilities(
            pack_queries, pack_keys, pack_segments, (sent, up_groups[-1])
        )
        attended = after(total, pack_probability, down_groups[-1]) + row_pair[0]
        normed_one, inverse_one = normalize(hidden_half + attended)
        first_norm = normed_one * gains[0] + shifts[0]
        first_low = both_halves(first_norm.astype(BF))

        preactivation = contract(first_low, up_groups) + up_bias[0]
        cumulative = 0.5 * (1.0 + lax.erf(preactivation * ROOT_HALF))
        activated = (preactivation * cumulative).astype(BF)
        slope = cumulative + preactivation * DENSITY_FACTOR * jnp.exp(
            -0.5 * preactivation * preactivation
        )
        total, _ = row_total(expand(activated, down_groups))
        step = width // 2
        if paired:
            first_pair = swapped(first_low[:, step:])
            total = after(total, first_pair)
        normed_two, inverse_two = normalize(first_norm + (total + row_pair[1]))
        result = (normed_two * gains[1] + shifts[1]).astype(BF)

        layer_output = columns(own_rows(both_halves(result)))
        grad_two = normalize_back(cotangent_rows, normed_two, inverse_two, gains[1])
        grad_two_low = both_halves(grad_two.astype(BF))

        def shares(left, right, axis):
            step = width // 2
            if axis == 0:
                return (
                    product_left(left[:, :step], right),
                    product_left(left[:, step:], right).astype(BF),
                )
            return (
                product_left(left, right[:, :step]),
                product_left(left, right[:, step:]).astype(BF),
            )

        def scattered(left, right, axis):
            return lax.psum_scatter(
                product_left(left, right).astype(BF), "weight", scatter_dimension=axis, tiled=True
            ).astype(F32)

        grad_pre = contract_right(grad_two_low, down_groups) * slope
        grad_pre_low = grad_pre.astype(BF)
        total, sent = row_total(expand_right(grad_pre_low, up_groups))
        if paired:
            pre_pair = swapped(grad_pre_low)
            down_mine, down_sent = column_grad(activated, grad_two_low, sent)
            down_received = swapped(down_sent)
            total = after(total, down_sent, pre_pair)
        grad_first = grad_two + total
        grad_one = normalize_back(grad_first, normed_one, inverse_one, gains[0])
        grad_one_low = both_halves(grad_one.astype(BF))
        grad_context = contract_right(grad_one_low, output_groups).astype(BF)
        grad_context_blocks = context_blocks(grad_context)

        gates = []
        if paired:
            up_halves = pair_grad(
                first_low[:, :step], first_pair, grad_pre_low, pre_pair, grad_context
            )
            up_halves = split(
                [up_halves[0], flip(up_halves[1], "context", 1)], 2, (grad_context_blocks[-1],)
            )
            down_halves = split([down_mine, down_received], 1, (grad_context_blocks[-1],))
            gates = [down_halves[1], up_halves[1], layer_output]

        pack_projected, bias_grads = attention_back(
            pack_probability, pack_queries, pack_keys, pack_values, grad_context_blocks, gates
        )
        total, final_sent = row_total(expand_right(own_block(pack_projected), input_groups))
        if paired:
            input_sent = sent_grad(pack_rows, pack_projected, bias_grads)
            received = swapped(input_sent)
            grad_input = product_left(pack_rows[:, :step], pack_projected) + received[
                :step
            ].astype(F32)
            bias_grads = bias_grads.astype(BF).astype(F32) + received[
                step : step + 2, :shard_width
            ].astype(F32)
            grad_up, up_low = finish_total(
                up_halves, [(), (pack_projected,), (), ()], 1
            )
            grad_down, down_low = finish_total(down_halves, [(pack_projected,), (), (), ()])
        else:
            grad_input = scattered(pack_rows, pack_projected, 0)
            bias_grads = lax.psum(bias_grads, "weight")
            grad_down = context_total(scattered(activated, grad_two_low, 1))
            grad_up = context_total(scattered(first_low, grad_pre_low, 0))

        small = row_sums(
            grad_one, grad_two, grad_first, normed_one, cotangent_rows, normed_two, grad_context
        )
        small = small + flip(small, "tensor", 1)
        share_width = output_weight.shape[2]
        joined = jnp.concatenate([columns(small).reshape(-1), jnp.sum(grad_pre, axis=0)])
        size = joined.shape[0]
        joined = jnp.pad(joined, (0, -size % (16 * share_width))).reshape(-1, share_width)
        out_rows, joined_rows = context.shape[1], joined.shape[0]
        if paired:
            below = -out_rows % (16 * packs * 4)
            joined = jnp.pad(joined, ((0, (below - joined_rows) % (16 * packs)), (0, 0)))
            out_mine, out_sent = column_grad(context, grad_one_low, grad_context, joined)
            out_halves = split([out_mine, swapped(out_sent)], 1, (down_low,))
            merged, _ = finish_total(out_halves, [(), (), (), ()])
        else:
            merged = jnp.concatenate(
                [
                    context_total(scattered(context, grad_one_low, 1)),
                    context_total(lax.psum(joined, "weight")),
                ],
                axis=0,
            )
        grad_out = merged[:out_rows]
        joined = merged[out_rows : out_rows + joined_rows].reshape(-1)
        small = joined[: 6 * width].reshape(3, 2, width)
        hidden_sum = joined[6 * width : size]
        grad_tokens = columns(own_rows(both_halves(grad_one + total)))
        return (
            layer_output,
            grad_tokens,
            grad_input.reshape(1, -1, 3, shard_width),
            bias_grads[None],
            grad_out[None],
            small[0][None],
            small[1][None],
            small[2][None],
            grad_up[None],
            hidden_sum[None],
            grad_down[None],
        )

    return shards


def solution(mesh):
    token_rows = P(("weight", "context"), None)
    input_spec = P(None, "weight", None, "tensor")
    out_spec = P(None, "tensor", "weight")
    placed = (
        token_rows,
        P(("weight", "context")),
        input_spec,
        P(None, None, "tensor"),
        out_spec,
        P(),
        P(),
        P(),
        P(None, "weight", "tensor"),
        P(None, "tensor"),
        out_spec,
        token_rows,
    )
    return jax.shard_map(
        build(mesh),
        mesh=mesh,
        in_specs=placed,
        out_specs=(
            token_rows,
            token_rows,
            input_spec,
            P(None, None, "tensor"),
            out_spec,
            P(),
            P(),
            P(),
            P(None, "weight", "tensor"),
            P(None, "tensor"),
            out_spec,
        ),
        check_vma=False,
    )
```

time: 245 us -> 186 us (0.76)
  matrix products: 51.4 us -> 13.8 us
  waiting for transfers between devices: 91.6 us -> 58.5 us
  Pallas kernels: 0 us -> 28.1 us
  starting transfers between devices: 60.2 us -> 41.5 us
  other arithmetic: 25.4 us -> 12.7 us
  local copies, waits for them, and re-layouts: 12.1 us -> 21.6 us
  between operations: 1.95 us -> 6.98 us
    ppermute x53 -> x44, waiting for transfers between devices: 91.6 us -> 58.5 us  [flip(): return lax.ppermute(value, axis, [(i, i ^ bit) for i in range(count[axis])])]
    pallas_call x0 -> x22, Pallas kernels: none -> 28.1 us  [the longest x1 8.53 us: attention_back(): pl.pallas_call(functools.partial(attention_back_kernel, heads, len(blocks...]
    dot_general x7 -> x0, matrix products: 25.6 us -> none  [the longest x2 7.21 us: attention_scores(): jnp.einsum('qhe,khe->hqk', queries, key_heads, preferred_element_type=F32)]
    ppermute x53 -> x44, starting transfers between devices: 60.2 us -> 41.5 us  [flip(): return lax.ppermute(value, axis, [(i, i ^ bit) for i in range(count[axis])])]
    dot_general x8 -> x1, matrix products: 13.8 us -> 1.75 us  [product_left(): lax.dot_general(left, right, (((0,), (0,)), ((), ())), preferred_element_...]
    convert_element_type x8 -> x1, other arithmetic: 10.2 us -> 0.8 us  [shards(): cotangent_rows = columns(take_half(cotangent, core_at)).astype(F32)]
    unnamed x87 -> x94, local copies, waits for them, and re-layouts: 1.92 us -> 10.2 us
    slice x8 -> x9, local copies, waits for them, and re-layouts: 0.16 us -> 4.83 us  [the longest x8 4.8 us: after(): first = lax.slice(other, (0,) * other.ndim, (1,) * other.ndim).reshape(())]
  transfers between devices with their start and end apart: 53 -> 44, of which waited for: 25 -> 19; matrix products, arithmetic and copies ran while one was open for 35% -> 16% of each run, Pallas kernels for 0% -> 15%
where the time goes in v2:
time: 186 us; the launch traced here: 183 us
  waiting for transfers between devices  58.5 us (31%)
  starting transfers between devices  41.5 us (22%)
  Pallas kernels  28.1 us (15%)
  local copies, waits for them, and re-layouts  21.6 us (12%)
  matrix products  13.8 us (7%)
  other arithmetic  12.7 us (7%)
  between operations  6.98 us (4%)
    ppermute x44, waiting for transfers between devices, flip(): return lax.ppermute(value, axis, [(i, i ^ bit) for i in range(count[axis])])  58.5 us
    ppermute x44, starting transfers between devices, flip(): return lax.ppermute(value, axis, [(i, i ^ bit) for i in range(count[axis])])  41.5 us
    unnamed x94, local copies, waits for them, and re-layouts  10.2 us
    pallas_call x1, Pallas kernels, attention_back(): pl.pallas_call(functools.partial(attention_back_kernel, heads, len(blocks...  8.53 us
    pallas_call x1, Pallas kernels, probabilities(): pl.pallas_call(functools.partial(probability_kernel, heads, block), out_s...  7.89 us
    dot_general x8, matrix products, product_right(): lax.dot_general(left, right, (((1,), (1,)), ((), ())), preferred_element_...  6.03 us
    dot_general x6, matrix products, product(): return jnp.dot(left, right, preferred_element_type=F32)  6 us
    slice x8, local copies, waits for them, and re-layouts, after(): first = lax.slice(other, (0,) * other.ndim, (1,) * other.ndim).reshape(())  4.8 us
  transfers between devices with their start and end apart: 44, of which 19 were waited for; matrix products, arithmetic and copies ran while one was open for 16% of the time, Pallas kernels for 15%

profile of v2, /device:TPU:4, one launch (start us, length us, event | category | flops | bytes accessed | tf_op | source)
XLA Modules:
  0.0 183.2 jit_solution(8333158049549745989)
XLA Ops:
  2.8 2.7 %collective-permute-start.2 = (bf16[144,768]{1,0:T(8,128)(2,1)S(1)}, bf16[144,768]{1,0:T(8,128)(2,1)S(1)}, u32[]{:S(2)}, u32[]{:S(2)}) collective-permute-start(bf16[144,768]{1,0:T(8,128)(2,1)S(1)} %fusion.30.refs_0_), channel_id=1, source_target_pairs={{0,8},{4,12},{8,0},{12,4},{1,9},{5,13},{9,1},{13,5},{2,10},{6,14},... | collective-permute-start | bytes 663560 | tf_op jit(solution)/shard_map/ppermute | solution.py:383
  5.4 1.6 collective-permute-start
  7.9 7.8 %collective-permute-done.2.refs_4_ = bf16[144,768]{1,0:T(8,128)(2,1)S(1)} collective-permute-done((bf16[144,768]{1,0:T(8,128)(2,1)S(1)}, bf16[144,768]{1,0:T(8,128)(2,1)S(1)}, u32[]{:S(2)}, u32[]{:S(2)}) %collective-permute-start.2) | collective-permute-done | bytes 221216 | tf_op jit(solution)/shard_map/ppermute | solution.py:383
  20.8 4.3 %collective-permute-done.4.refs_6_ = bf16[144,768]{1,0:T(8,128)(2,1)S(1)} collective-permute-done((bf16[144,768]{1,0:T(8,128)(2,1)S(1)}, bf16[144,768]{1,0:T(8,128)(2,1)S(1)}, u32[]{:S(2)}, u32[]{:S(2)}) %collective-permute-start.4) | collective-permute-done | bytes 221216 | tf_op jit(solution)/shard_map/ppermute | solution.py:383
  27.2 1.3 collective-permute-start.10
  31.2 4.7 %shard_map.203 = (bf16[1024,192]{1,0:T(8,128)(2,1)S(1)}, bf16[1024,192]{1,0:T(8,128)(2,1)S(1)}, bf16[1024,192]{1,0:T(8,128)(2,1)S(1)}, bf16[256,192]{1,0:T(8,128...) custom-call(bf16[144,768]{1,0:T(8,128)(2,1)S(1)} %fusion.30.refs_0_, ...), custom_call_target="tpu_custom_call" | custom-call | tf_op jit(solution)/shard_map/pallas_call | solution.py:122
  35.9 1.2 copy-done.1
  39.4 1.5 collective-permute-done.8
  41.8 1.3 collective-permute-start.9
  43.6 7.9 %shard_map.204.a_hbm = bf16[3,1024,1024]{2,1,0:T(8,128)(2,1)S(1)} custom-call(bf16[1024,192]{1,0:T(8,128)(2,1)S(1)} %get-tuple-element.36.q_ref, bf16[1024,192]{1,0:T(8,128)(2,1)S(1)} %get-tuple-element.37.k_ref, f32[1,1024]{1,0:T(1,128)S(1)} %get-tuple-element.38.row_ref, bf16[128,768]{1,0:T(8,128)(2,1)S(1)} %fusion.20.refs_0_, ...), custom_call_target="tpu_custom_call" | custom-call | tf_op jit(solution)/shard_map/pallas_call | solution.py:170
  52.0 2.6 %copy-done = bf16[3,1024,1024]{2,1,0:T(8,128)(2,1)} copy-done((bf16[3,1024,1024]{2,1,0:T(8,128)(2,1)}, bf16[3,1024,1024]{2,1,0:T(8,128)(2,1)S(1)}, u32[]{:S(2)}) %copy-start) | copy-done | bytes 6291480
  58.5 1.4 collective-permute-done.12
  60.3 2.4 %multiply_convert_fusion = (bf16[256,768]{1,0:T(8,128)(2,1)S(1)}, f32[256,768]{1,0:T(8,128)}) fusion(f32[768]{0:T(1024)S(1)} %reduce.3, f32[256,768]{1,0:T(8,128)S(1)} %fusion.66, bf16[256,384]{1,0:T(8,128)(2,1)S(1)} %get-tuple-element.104.left, bf16[384,768]{1,0:T(8,128)(2,1)} %add_bitcast_fusion.1), kind=kOutput, calls=%fused_computation.22 | convolution fusion | flops 152371200 | bytes 2755584 | tf_op jit(solution)/shard_map/dot_general | solution.py:20
  62.6 1.4 fusion.67
  64.1 1.4 fusion.68
  65.7 1.3 collective-permute-start.15
  67.1 1.5 collective-permute-start.14
  69.5 3.5 %collective-permute-done.15.left_pair = bf16[256,384]{1,0:T(8,128)(2,1)S(1)} collective-permute-done((bf16[256,384]{1,0:T(8,128)(2,1)S(1)}, bf16[256,384]{1,0:T(8,128)(2,1)S(1)}, u32[]{:S(2)}, u32[]{:S(2)}) %collective-permute-start.15) | collective-permute-done | bytes 196640 | tf_op jit(solution)/shard_map/ppermute | solution.py:383
  77.0 1.4 fusion.41
  78.4 1.6 fusion.54
  80.0 1.4 fusion.69
  81.5 1.3 collective-permute-start.20
  83.5 1.3 collective-permute-done.18
  84.8 1.6 collective-permute-start.19
  88.2 4.5 %collective-permute-done.20.right_pair = bf16[256,768]{1,0:T(8,128)(2,1)S(1)} collective-permute-done((bf16[256,768]{1,0:T(8,128)(2,1)S(1)}, bf16[256,768]{1,0:T(8,128)(2,1)S(1)}, u32[]{:S(2)}, u32[]{:S(2)}) %collective-permute-start.20) | collective-permute-done | bytes 393248 | tf_op jit(solution)/shard_map/ppermute | solution.py:383
  94.5 1.3 collective-permute-start.25
  96.4 3.4 %collective-permute-start.23 = (bf16[256,192]{1,0:T(8,128)(2,1)S(1)}, bf16[256,192]{1,0:T(8,128)(2,1)S(1)}, u32[]{:S(2)}, u32[]{:S(2)}) collective-permute-start(bf16[256,192]{1,0:T(8,128)(2,1)S(1)} %fusion.2._.refs_0_.refs_1_), channel_id=1, source_target_pairs={{0,8},{4,12},{8,0},{12,4},{1,9},{5,13},{9,1},{13,5},{2,10},{6,14},... | collective-permute-start | bytes 294920 | tf_op jit(solution)/shard_map/ppermute | solution.py:383
  99.7 1.7 collective-permute-start.22
  103.8 2.7 %collective-permute-done.23.refs_2_ = bf16[256,192]{1,0:T(8,128)(2,1)S(1)} collective-permute-done((bf16[256,192]{1,0:T(8,128)(2,1)S(1)}, bf16[256,192]{1,0:T(8,128)(2,1)S(1)}, u32[]{:S(2)}, u32[]{:S(2)}) %collective-permute-start.23) | collective-permute-done | bytes 98336 | tf_op jit(solution)/shard_map/ppermute | solution.py:383
  107.2 3.1 %collective-permute-done.25.refs_1_ = bf16[768,384]{1,0:T(8,128)(2,1)S(1)} collective-permute-done((bf16[768,384]{1,0:T(8,128)(2,1)S(1)}, bf16[768,384]{1,0:T(8,128)(2,1)S(1)}, u32[]{:S(2)}, u32[]{:S(2)}) %collective-permute-start.25) | collective-permute-done | bytes 589856 | tf_op jit(solution)/shard_map/ppermute | solution.py:383
  110.3 5.5 %collective-permute-done.24.refs_2_.refs_3_ = bf16[256,192]{1,0:T(8,128)(2,1)S(1)} collective-permute-done((bf16[256,192]{1,0:T(8,128)(2,1)S(1)}, bf16[256,192]{1,0:T(8,128)(2,1)S(1)}, u32[]{:S(2)}, u32[]{:S(2)}) %collective-permute-start.24) | collective-permute-done | bytes 98336 | tf_op jit(solution)/shard_map/ppermute | solution.py:383
  116.6 1.6 collective-permute-start.33
  118.3 8.5 %shard_map.209 = (bf16[1024,576]{1,0:T(8,128)(2,1)S(1)}, f32[2,192]{1,0:T(2,128)S(1)}) custom-call(bf16[3,1024,1024]{2,1,0:T(8,128)(2,1)S(1)} %bitcast.60, bf16[1024,192]{1,0:T(8,128)(2,1)S(1)} %copy-done.8, bf16[1024,192]{1,0:T(8,128)(2,1)S(1)} %copy-done.10, bf16[1024,192]{1,0:T(8,128)(2,1)S(1)} %copy-done.22, ...), custom_call_target="tpu_custom_call" | custom-call | flops 10000000000 | bytes 10000000 | tf_op jit(solution)/shard_map/pallas_call | solution.py:218
  129.5 1.2 collective-permute-start.32
  130.7 1.8 collective-permute-start.39
  132.5 1.4 copy-done.2
  136.8 1.2 collective-permute-start.34
  138.9 1.5 collective-permute-start.28
  140.5 4.9 %collective-permute-done.39.other_ref = bf16[96,768]{1,0:T(8,128)(2,1)S(1)} collective-permute-done((bf16[96,768]{1,0:T(8,128)(2,1)S(1)}, bf16[96,768]{1,0:T(8,128)(2,1)S(1)}, u32[]{:S(2)}, u32[]{:S(2)}) %collective-permute-start.39) | collective-permute-done | bytes 147488 | tf_op jit(solution)/shard_map/ppermute | solution.py:383
  145.5 4.6 %collective-permute-done.34.other_ref = bf16[192,384]{1,0:T(8,128)(2,1)S(1)} collective-permute-done((bf16[192,384]{1,0:T(8,128)(2,1)S(1)}, bf16[192,384]{1,0:T(8,128)(2,1)S(1)}, u32[]{:S(2)}, u32[]{:S(2)}) %collective-permute-start.34) | collective-permute-done | bytes 147488 | tf_op jit(solution)/shard_map/ppermute | solution.py:383
  150.3 2.9 %collective-permute-done.40.other_ref = bf16[96,768]{1,0:T(8,128)(2,1)S(1)} collective-permute-done((bf16[96,768]{1,0:T(8,128)(2,1)S(1)}, bf16[96,768]{1,0:T(8,128)(2,1)S(1)}, u32[]{:S(2)}, u32[]{:S(2)}) %collective-permute-start.40) | collective-permute-done | bytes 147488 | tf_op jit(solution)/shard_map/ppermute | solution.py:383
  153.4 2.4 %collective-permute-start.42 = (bf16[192,384]{1,0:T(8,128)(2,1)S(1)}, bf16[192,384]{1,0:T(8,128)(2,1)S(1)}, u32[]{:S(2)}, u32[]{:S(2)}) collective-permute-start(bf16[192,384]{1,0:T(8,128)(2,1)S(1)} %shard_map.214.refs_2_.own_ref), channel_id=1, source_target_pairs={{0,8},{4,12},{8,0},{12,4},{1,9},{5,13},{9,1},{13,5},{2,10},{6,14},... | collective-permute-start | bytes 442376 | tf_op jit(solution)/shard_map/ppermute | solution.py:383
  157.3 7.0 %collective-permute-done.36.other_ref = bf16[64,384]{1,0:T(8,128)(2,1)S(1)} collective-permute-done((bf16[64,384]{1,0:T(8,128)(2,1)S(1)}, bf16[64,384]{1,0:T(8,128)(2,1)S(1)}, u32[]{:S(2)}, u32[]{:S(2)}) %collective-permute-start.36) | collective-permute-done | bytes 49184 | tf_op jit(solution)/shard_map/ppermute | solution.py:383
  164.3 3.5 %collective-permute-start.37 = (bf16[64,384]{1,0:T(8,128)(2,1)S(1)}, bf16[64,384]{1,0:T(8,128)(2,1)S(1)}, u32[]{:S(2)}, u32[]{:S(2)}) collective-permute-start(bf16[64,384]{1,0:T(8,128)(2,1)S(1)} %shard_map.217.own_ref), channel_id=1, source_target_pairs={{0,8},{4,12},{8,0},{12,4},{1,9},{5,13},{9,1},{13,5},{2,10},{6,14},... | collective-permute-start | bytes 147464 | tf_op jit(solution)/shard_map/ppermute | solution.py:383
  167.9 1.8 convolution_add_fusion
  170.0 1.2 collective-permute-start.38
  171.8 2.4 %copy.39 = f32[384,576]{0,1:T(8,128)} copy(f32[384,576]{1,0:T(8,128)} %convolution_add_fusion) | data formatting | bytes 1769472 | tf_op jit(solution)/shard_map/add | solution.py:613
  179.6 1.5 maximum_select_fusion
  (249 shorter events, 45.8 us)
Async XLA Ops:
  2.8 13.0 %collective-permute-start.2 = (bf16[144,768]{1,0:T(8,128)(2,1)S(1)}, bf16[144,768]{1,0:T(8,128)(2,1)S(1)}, u32[]{:S(2)}, u32[]{:S(2)}) collective-permute-start(bf16[144,768]{1,0:T(8,128)(2,1)S(1)} %fusion.30.refs_0_), channel_id=1, source_target_pairs={{0,8},{4,12},{8,0},{12,4},{1,9},{5,13},{9,1},{13,5},{2,10},{6,14},... | collective-permute-start | bytes 663560 | tf_op jit(solution)/shard_map/ppermute | solution.py:383
  5.4 12.1 %collective-permute-start = (bf16[144,768]{1,0:T(8,128)(2,1)S(1)}, bf16[144,768]{1,0:T(8,128)(2,1)S(1)}, u32[]{:S(2)}, u32[]{:S(2)}) collective-permute-start(bf16[144,768]{1,0:T(8,128)(2,1)S(1)} %fusion.30.refs_0_), channel_id=1, source_target_pairs={{0,4},{4,0},{8,12},{12,8},{1,5},{5,1},{9,13},{13,9},{2,6},{6,2},{1... | collective-permute-start | bytes 663560 | tf_op jit(solution)/shard_map/ppermute | solution.py:383
  7.0 19.3 %copy-start.35 = (bf16[1,768,384]{2,1,0:T(8,128)(2,1)S(1)}, bf16[1,768,384]{2,1,0:T(8,128)(2,1)}, u32[]{:S(2)}) copy-start(bf16[1,768,384]{2,1,0:T(8,128)(2,1)} %param.22) | copy-start | bytes 1769476
  7.3 22.1 %collective-permute-start.6 = (bf16[384,576]{1,0:T(8,128)(2,1)S(1)}, bf16[384,576]{1,0:T(8,128)(2,1)S(1)}, u32[]{:S(2)}, u32[]{:S(2)}) collective-permute-start(bf16[384,576]{1,0:T(8,128)(2,1)S(1)} %copy.35.refs_9_), channel_id=1, source_target_pairs={{0,16},{16,0},{1,17},{17,1},{2,18},{18,2},{3,19},{19,3},{4,20},{20... | collective-permute-start | bytes 1327112 | tf_op jit(solution)/shard_map/ppermute | solution.py:383
  17.0 21.2 %collective-permute-start.7 = (bf16[192,384]{1,0:T(8,128)(2,1)S(1)}, bf16[192,384]{1,0:T(8,128)(2,1)S(1)}, u32[]{:S(2)}, u32[]{:S(2)}) collective-permute-start(bf16[192,384]{1,0:T(8,128)(2,1)S(1)} %add_bitcast_fusion.2), channel_id=1, source_target_pairs={{0,16},{16,0},{1,17},{17,1},{2,18},{18,2},{3,19},{19,3},{4,20},{20... | collective-permute-start | bytes 442376 | tf_op jit(solution)/shard_map/ppermute | solution.py:383
  18.7 6.3 %collective-permute-start.4 = (bf16[144,768]{1,0:T(8,128)(2,1)S(1)}, bf16[144,768]{1,0:T(8,128)(2,1)S(1)}, u32[]{:S(2)}, u32[]{:S(2)}) collective-permute-start(bf16[144,768]{1,0:T(8,128)(2,1)S(1)} %collective-permute-done.2.refs_4_), channel_id=1, source_target_pairs={{0,4},{4,0},{8,12},{12,8},{1,5},{5,1},{9,13},{13,9},{2,6},{6,2},{1... | collective-permute-start | bytes 663560 | tf_op jit(solution)/shard_map/ppermute | solution.py:383
  19.4 7.8 %collective-permute-start.1 = (bf16[144,768]{1,0:T(8,128)(2,1)S(1)}, bf16[144,768]{1,0:T(8,128)(2,1)S(1)}, u32[]{:S(2)}, u32[]{:S(2)}) collective-permute-start(bf16[144,768]{1,0:T(8,128)(2,1)S(1)} %collective-permute-done.refs_2_), channel_id=1, source_target_pairs={{0,1},{1,0},{2,3},{3,2},{4,5},{5,4},{6,7},{7,6},{8,9},{9,8},{10,11... | collective-permute-start | bytes 663560 | tf_op jit(solution)/shard_map/ppermute | solution.py:383
  19.4 9.1 %collective-permute-start.3 = (bf16[144,768]{1,0:T(8,128)(2,1)S(1)}, bf16[144,768]{1,0:T(8,128)(2,1)S(1)}, u32[]{:S(2)}, u32[]{:S(2)}) collective-permute-start(bf16[144,768]{1,0:T(8,128)(2,1)S(1)} %collective-permute-done.2.refs_4_), channel_id=1, source_target_pairs={{0,1},{1,0},{2,3},{3,2},{4,5},{5,4},{6,7},{7,6},{8,9},{9,8},{10,11... | collective-permute-start | bytes 663560 | tf_op jit(solution)/shard_map/ppermute | solution.py:383
  26.2 3.1 %collective-permute-start.5 = (bf16[144,768]{1,0:T(8,128)(2,1)S(1)}, bf16[144,768]{1,0:T(8,128)(2,1)S(1)}, u32[]{:S(2)}, u32[]{:S(2)}) collective-permute-start(bf16[144,768]{1,0:T(8,128)(2,1)S(1)} %collective-permute-done.4.refs_6_), channel_id=1, source_target_pairs={{0,1},{1,0},{2,3},{3,2},{4,5},{5,4},{6,7},{7,6},{8,9},{9,8},{10,11... | collective-permute-start | bytes 663560 | tf_op jit(solution)/shard_map/ppermute | solution.py:383
  27.2 16.4 %collective-permute-start.10 = (bf16[384,768]{1,0:T(8,128)(2,1)}, bf16[384,768]{1,0:T(8,128)(2,1)S(1)}, u32[]{:S(2)}, u32[]{:S(2)}) collective-permute-start(bf16[384,768]{1,0:T(8,128)(2,1)} %add_bitcast_fusion.1), channel_id=1, source_target_pairs={{0,16},{16,0},{1,17},{17,1},{2,18},{18,2},{3,19},{19,3},{4,20},{20... | collective-permute-start | bytes 1769480 | tf_op jit(solution)/shard_map/ppermute | solution.py:383
  28.5 27.4 %collective-permute-start.11 = (bf16[768,384]{1,0:T(8,128)(2,1)}, bf16[768,384]{1,0:T(8,128)(2,1)}, u32[]{:S(2)}, u32[]{:S(2)}) collective-permute-start(bf16[768,384]{1,0:T(8,128)(2,1)} %add_bitcast_fusion), channel_id=1, source_target_pairs={{0,16},{16,0},{1,17},{17,1},{2,18},{18,2},{3,19},{19,3},{4,20},{20... | collective-permute-start | bytes 1769480 | tf_op jit(solution)/shard_map/ppermute | solution.py:383
  39.2 1.6 collective-permute-start.8
  41.8 15.9 %collective-permute-start.9 = (bf16[128,768]{1,0:T(8,128)(2,1)S(1)}, bf16[128,768]{1,0:T(8,128)(2,1)S(1)}, u32[]{:S(2)}, u32[]{:S(2)}) collective-permute-start(bf16[128,768]{1,0:T(8,128)(2,1)S(1)} %fusion.20.refs_0_), channel_id=1, source_target_pairs={{0,2},{1,3},{2,0},{3,1},{4,6},{5,7},{6,4},{7,5},{8,10},{9,11},{10,... | collective-permute-start | bytes 589832 | tf_op jit(solution)/shard_map/ppermute | solution.py:383
  58.4 1.5 collective-permute-start.12
  65.5 1.5 collective-permute-start.13
  65.7 7.2 %collective-permute-start.15 = (bf16[256,384]{1,0:T(8,128)(2,1)S(1)}, bf16[256,384]{1,0:T(8,128)(2,1)S(1)}, u32[]{:S(2)}, u32[]{:S(2)}) collective-permute-start(bf16[256,384]{1,0:T(8,128)(2,1)S(1)} %get-tuple-element.105), channel_id=1, source_target_pairs={{0,16},{16,0},{1,17},{17,1},{2,18},{18,2},{3,19},{19,3},{4,20},{20... | collective-permute-start | bytes 589832 | tf_op jit(solution)/shard_map/ppermute | solution.py:383
  67.1 7.0 %collective-permute-start.14 = (bf16[128,768]{1,0:T(8,128)(2,1)S(1)}, bf16[128,768]{1,0:T(8,128)(2,1)S(1)}, u32[]{:S(2)}, u32[]{:S(2)}) collective-permute-start(bf16[128,768]{1,0:T(8,128)(2,1)S(1)} %fusion.17), channel_id=1, source_target_pairs={{0,2},{1,3},{2,0},{3,1},{4,6},{5,7},{6,4},{7,5},{8,10},{9,11},{10,... | collective-permute-start | bytes 589832 | tf_op jit(solution)/shard_map/ppermute | solution.py:383
  75.5 1.4 collective-permute-start.17
  75.5 7.8 %collective-permute-start.16 = (bf16[128,768]{1,0:T(8,128)(2,1)}, bf16[128,768]{1,0:T(8,128)(2,1)S(1)}, u32[]{:S(2)}, u32[]{:S(2)}) collective-permute-start(bf16[128,768]{1,0:T(8,128)(2,1)} %get-tuple-element.98), channel_id=1, source_target_pairs={{0,1},{1,0},{2,3},{3,2},{4,5},{5,4},{6,7},{7,6},{8,9},{9,8},{10,11... | collective-permute-start | bytes 589832 | tf_op jit(solution)/shard_map/ppermute | solution.py:383
  81.5 11.2 %collective-permute-start.20 = (bf16[256,768]{1,0:T(8,128)(2,1)S(1)}, bf16[256,768]{1,0:T(8,128)(2,1)S(1)}, u32[]{:S(2)}, u32[]{:S(2)}) collective-permute-start(bf16[256,768]{1,0:T(8,128)(2,1)S(1)} %get-tuple-element.95.right), channel_id=1, source_target_pairs={{0,16},{16,0},{1,17},{17,1},{2,18},{18,2},{3,19},{19,3},{4,20},{20... | collective-permute-start | bytes 1179656 | tf_op jit(solution)/shard_map/ppermute | solution.py:383
  83.3 1.5 collective-permute-start.18
  84.8 9.1 %collective-permute-start.19 = (bf16[128,768]{1,0:T(8,128)(2,1)S(1)}, bf16[128,768]{1,0:T(8,128)(2,1)S(1)}, u32[]{:S(2)}, u32[]{:S(2)}) collective-permute-start(bf16[128,768]{1,0:T(8,128)(2,1)S(1)} %fusion.14.refs_0_), channel_id=1, source_target_pairs={{0,2},{1,3},{2,0},{3,1},{4,6},{5,7},{6,4},{7,5},{8,10},{9,11},{10,... | collective-permute-start | bytes 589832 | tf_op jit(solution)/shard_map/ppermute | solution.py:383
  93.9 24.4 %slice-start = ((s8[6291456]{0:T(1024)(128)(4,1)}), s8[4194304]{0:T(1024)(128)(4,1)S(1)}, s32[]{:S(2)}) async-start(s8[6291456]{0:T(1024)(128)(4,1)} %bitcast.59), calls=%async_computation | async-start | bytes 8388608
  94.3 1.5 collective-permute-start.21
  94.5 23.8 %copy-start.11 = (bf16[256,768]{1,0:T(8,128)(2,1)}, bf16[256,768]{1,0:T(8,128)(2,1)S(1)}, u32[]{:S(2)}) copy-start(bf16[256,768]{1,0:T(8,128)(2,1)S(1)} %maximum_select_fusion.3.refs_6_) | copy-start | bytes 1179652
  94.5 15.8 %collective-permute-start.25 = (bf16[768,384]{1,0:T(8,128)(2,1)S(1)}, bf16[768,384]{1,0:T(8,128)(2,1)S(1)}, u32[]{:S(2)}, u32[]{:S(2)}) collective-permute-start(bf16[768,384]{1,0:T(8,128)(2,1)S(1)} %get-tuple-element.39), channel_id=1, source_target_pairs={{0,16},{16,0},{1,17},{17,1},{2,18},{18,2},{3,19},{19,3},{4,20},{20... | collective-permute-start | bytes 1769480 | tf_op jit(solution)/shard_map/ppermute | solution.py:383
  96.4 21.9 %slice-start.1 = ((s8[6291456]{0:T(1024)(128)(4,1)}), s8[2097152]{0:T(1024)(128)(4,1)S(1)}, s32[]{:S(2)}) async-start(s8[6291456]{0:T(1024)(128)(4,1)} %bitcast.59), calls=%async_computation.1 | async-start | bytes 4194304
  96.4 10.1 %collective-permute-start.23 = (bf16[256,192]{1,0:T(8,128)(2,1)S(1)}, bf16[256,192]{1,0:T(8,128)(2,1)S(1)}, u32[]{:S(2)}, u32[]{:S(2)}) collective-permute-start(bf16[256,192]{1,0:T(8,128)(2,1)S(1)} %fusion.2._.refs_0_.refs_1_), channel_id=1, source_target_pairs={{0,8},{4,12},{8,0},{12,4},{1,9},{5,13},{9,1},{13,5},{2,10},{6,14},... | collective-permute-start | bytes 294920 | tf_op jit(solution)/shard_map/ppermute | solution.py:383
  99.7 18.5 %collective-permute-start.22 = (bf16[256,192]{1,0:T(8,128)(2,1)S(1)}, bf16[256,192]{1,0:T(8,128)(2,1)S(1)}, u32[]{:S(2)}, u32[]{:S(2)}) collective-permute-start(bf16[256,192]{1,0:T(8,128)(2,1)S(1)} %fusion.2._.refs_0_.refs_1_), channel_id=1, source_target_pairs={{0,4},{4,0},{8,12},{12,8},{1,5},{5,1},{9,13},{13,9},{2,6},{6,2},{1... | collective-permute-start | bytes 294920 | tf_op jit(solution)/shard_map/ppermute | solution.py:383
  102.0 16.2 %collective-permute-start.26 = (bf16[192,768]{1,0:T(8,128)(2,1)S(1)}, bf16[192,768]{1,0:T(8,128)(2,1)S(1)}, u32[]{:S(2)}, u32[]{:S(2)}) collective-permute-start(bf16[192,768]{1,0:T(8,128)(2,1)S(1)} %get-tuple-element.44), channel_id=1, source_target_pairs={{0,4},{4,0},{8,12},{12,8},{1,5},{5,1},{9,13},{13,9},{2,6},{6,2},{1... | collective-permute-start | bytes 884744 | tf_op jit(solution)/shard_map/ppermute | solution.py:383
  102.5 1.3 collective-permute-start.31
  106.5 9.2 %collective-permute-start.24 = (bf16[256,192]{1,0:T(8,128)(2,1)S(1)}, bf16[256,192]{1,0:T(8,128)(2,1)S(1)}, u32[]{:S(2)}, u32[]{:S(2)}) collective-permute-start(bf16[256,192]{1,0:T(8,128)(2,1)S(1)} %collective-permute-done.23.refs_2_), channel_id=1, source_target_pairs={{0,4},{4,0},{8,12},{12,8},{1,5},{5,1},{9,13},{13,9},{2,6},{6,2},{1... | collective-permute-start | bytes 294920 | tf_op jit(solution)/shard_map/ppermute | solution.py:383
  116.6 19.1 %collective-permute-start.33 = (bf16[384,384]{1,0:T(8,128)(2,1)}, bf16[384,384]{1,0:T(8,128)(2,1)}, u32[]{:S(2)}, u32[]{:S(2)}) collective-permute-start(bf16[384,384]{1,0:T(8,128)(2,1)} %get-tuple-element.42.refs_4_), channel_id=1, source_target_pairs={{0,4},{4,0},{8,12},{12,8},{1,5},{5,1},{9,13},{13,9},{2,6},{6,2},{1... | collective-permute-start | bytes 884744 | tf_op jit(solution)/shard_map/ppermute | solution.py:383
  129.1 8.9 %collective-permute-start.27 = (bf16[128,768]{1,0:T(8,128)(2,1)}, bf16[128,768]{1,0:T(8,128)(2,1)}, u32[]{:S(2)}, u32[]{:S(2)}) collective-permute-start(bf16[128,768]{1,0:T(8,128)(2,1)} %fusion.21), channel_id=1, source_target_pairs={{0,1},{1,0},{2,3},{3,2},{4,5},{5,4},{6,7},{7,6},{8,9},{9,8},{10,11... | collective-permute-start | bytes 589832 | tf_op jit(solution)/shard_map/ppermute | solution.py:383
  129.5 20.7 %collective-permute-start.32 = (bf16[256,384]{1,0:T(8,128)(2,1)S(1)}, bf16[256,384]{1,0:T(8,128)(2,1)S(1)}, u32[]{:S(2)}, u32[]{:S(2)}) collective-permute-start(bf16[256,384]{1,0:T(8,128)(2,1)S(1)} %get-tuple-element.50), channel_id=1, source_target_pairs={{0,16},{16,0},{1,17},{17,1},{2,18},{18,2},{3,19},{19,3},{4,20},{20... | collective-permute-start | bytes 589832 | tf_op jit(solution)/shard_map/ppermute | solution.py:383
  130.7 14.7 %collective-permute-start.39 = (bf16[96,768]{1,0:T(8,128)(2,1)S(1)}, bf16[96,768]{1,0:T(8,128)(2,1)S(1)}, u32[]{:S(2)}, u32[]{:S(2)}) collective-permute-start(bf16[96,768]{1,0:T(8,128)(2,1)S(1)} %get-tuple-element.45.refs_5_), channel_id=1, source_target_pairs={{0,8},{4,12},{8,0},{12,4},{1,9},{5,13},{9,1},{13,5},{2,10},{6,14},... | collective-permute-start | bytes 442376 | tf_op jit(solution)/shard_map/ppermute | solution.py:383
  134.7 33.2 %collective-permute-start.30 = (bf16[400,576]{1,0:T(8,128)(2,1)S(1)}, bf16[400,576]{1,0:T(8,128)(2,1)S(1)}, u32[]{:S(2)}, u32[]{:S(2)}) collective-permute-start(bf16[400,576]{1,0:T(8,128)(2,1)S(1)} %shard_map.210), channel_id=1, source_target_pairs={{0,16},{16,0},{1,17},{17,1},{2,18},{18,2},{3,19},{19,3},{4,20},{20... | collective-permute-start | bytes 1382408 | tf_op jit(solution)/shard_map/ppermute | solution.py:383
  136.8 13.4 %collective-permute-start.34 = (bf16[192,384]{1,0:T(8,128)(2,1)S(1)}, bf16[192,384]{1,0:T(8,128)(2,1)S(1)}, u32[]{:S(2)}, u32[]{:S(2)}) collective-permute-start(bf16[192,384]{1,0:T(8,128)(2,1)S(1)} %get-tuple-element.53), channel_id=1, source_target_pairs={{0,8},{4,12},{8,0},{12,4},{1,9},{5,13},{9,1},{13,5},{2,10},{6,14},... | collective-permute-start | bytes 442376 | tf_op jit(solution)/shard_map/ppermute | solution.py:383
  138.9 17.6 %collective-permute-start.28 = (bf16[128,768]{1,0:T(8,128)(2,1)S(1)}, bf16[128,768]{1,0:T(8,128)(2,1)S(1)}, u32[]{:S(2)}, u32[]{:S(2)}) collective-permute-start(bf16[128,768]{1,0:T(8,128)(2,1)S(1)} %fusion.11), channel_id=1, source_target_pairs={{0,2},{1,3},{2,0},{3,1},{4,6},{5,7},{6,4},{7,5},{8,10},{9,11},{10,... | collective-permute-start | bytes 589832 | tf_op jit(solution)/shard_map/ppermute | solution.py:383
  145.4 7.8 %collective-permute-start.40 = (bf16[96,768]{1,0:T(8,128)(2,1)S(1)}, bf16[96,768]{1,0:T(8,128)(2,1)S(1)}, u32[]{:S(2)}, u32[]{:S(2)}) collective-permute-start(bf16[96,768]{1,0:T(8,128)(2,1)S(1)} %shard_map.220.own_ref), channel_id=1, source_target_pairs={{0,8},{4,12},{8,0},{12,4},{1,9},{5,13},{9,1},{13,5},{2,10},{6,14},... | collective-permute-start | bytes 442376 | tf_op jit(solution)/shard_map/ppermute | solution.py:383
  150.3 5.5 %collective-permute-start.35 = (bf16[128,384]{1,0:T(8,128)(2,1)S(1)}, bf16[128,384]{1,0:T(8,128)(2,1)S(1)}, u32[]{:S(2)}, u32[]{:S(2)}) collective-permute-start(bf16[128,384]{1,0:T(8,128)(2,1)S(1)} %get-tuple-element.55), channel_id=1, source_target_pairs={{0,4},{4,0},{8,12},{12,8},{1,5},{5,1},{9,13},{13,9},{2,6},{6,2},{1... | collective-permute-start | bytes 294920 | tf_op jit(solution)/shard_map/ppermute | solution.py:383
  153.3 21.9 %collective-permute-start.41 = (bf16[192,768]{1,0:T(8,128)(2,1)S(1)}, bf16[192,768]{1,0:T(8,128)(2,1)S(1)}, u32[]{:S(2)}, u32[]{:S(2)}) collective-permute-start(bf16[192,768]{1,0:T(8,128)(2,1)S(1)} %shard_map.221.own_ref), channel_id=1, source_target_pairs={{0,4},{4,0},{8,12},{12,8},{1,5},{5,1},{9,13},{13,9},{2,6},{6,2},{1... | collective-permute-start | bytes 884744 | tf_op jit(solution)/shard_map/ppermute | solution.py:383
  153.4 20.8 %collective-permute-start.42 = (bf16[192,384]{1,0:T(8,128)(2,1)S(1)}, bf16[192,384]{1,0:T(8,128)(2,1)S(1)}, u32[]{:S(2)}, u32[]{:S(2)}) collective-permute-start(bf16[192,384]{1,0:T(8,128)(2,1)S(1)} %shard_map.214.refs_2_.own_ref), channel_id=1, source_target_pairs={{0,8},{4,12},{8,0},{12,4},{1,9},{5,13},{9,1},{13,5},{2,10},{6,14},... | collective-permute-start | bytes 442376 | tf_op jit(solution)/shard_map/ppermute | solution.py:383
  155.8 8.5 %collective-permute-start.36 = (bf16[64,384]{1,0:T(8,128)(2,1)S(1)}, bf16[64,384]{1,0:T(8,128)(2,1)S(1)}, u32[]{:S(2)}, u32[]{:S(2)}) collective-permute-start(bf16[64,384]{1,0:T(8,128)(2,1)S(1)} %get-tuple-element.57), channel_id=1, source_target_pairs={{0,8},{4,12},{8,0},{12,4},{1,9},{5,13},{9,1},{13,5},{2,10},{6,14},... | collective-permute-start | bytes 147464 | tf_op jit(solution)/shard_map/ppermute | solution.py:383
  157.3 22.3 %collective-permute-start.29 = (f32[128,768]{1,0:T(8,128)}, f32[128,768]{1,0:T(8,128)}, u32[]{:S(2)}, u32[]{:S(2)}) collective-permute-start(f32[128,768]{1,0:T(8,128)} %add_add_fusion), channel_id=1, source_target_pairs={{0,1},{1,0},{2,3},{3,2},{4,5},{5,4},{6,7},{7,6},{8,9},{9,8},{10,11... | collective-permute-start | bytes 1179656 | tf_op jit(solution)/shard_map/ppermute | solution.py:383
  164.3 5.6 %collective-permute-start.37 = (bf16[64,384]{1,0:T(8,128)(2,1)S(1)}, bf16[64,384]{1,0:T(8,128)(2,1)S(1)}, u32[]{:S(2)}, u32[]{:S(2)}) collective-permute-start(bf16[64,384]{1,0:T(8,128)(2,1)S(1)} %shard_map.217.own_ref), channel_id=1, source_target_pairs={{0,8},{4,12},{8,0},{12,4},{1,9},{5,13},{9,1},{13,5},{2,10},{6,14},... | collective-permute-start | bytes 147464 | tf_op jit(solution)/shard_map/ppermute | solution.py:383
  170.0 6.4 %collective-permute-start.38 = (bf16[128,384]{1,0:T(8,128)(2,1)S(1)}, bf16[128,384]{1,0:T(8,128)(2,1)S(1)}, u32[]{:S(2)}, u32[]{:S(2)}) collective-permute-start(bf16[128,384]{1,0:T(8,128)(2,1)S(1)} %shard_map.218.own_ref), channel_id=1, source_target_pairs={{0,4},{4,0},{8,12},{12,8},{1,5},{5,1},{9,13},{13,9},{2,6},{6,2},{1... | collective-permute-start | bytes 294920 | tf_op jit(solution)/shard_map/ppermute | solution.py:383
  174.3 7.8 %collective-permute-start.43 = (bf16[384,384]{1,0:T(8,128)(2,1)S(1)}, bf16[384,384]{1,0:T(8,128)(2,1)S(1)}, u32[]{:S(2)}, u32[]{:S(2)}) collective-permute-start(bf16[384,384]{1,0:T(8,128)(2,1)S(1)} %shard_map.223.own_ref), channel_id=1, source_target_pairs={{0,4},{4,0},{8,12},{12,8},{1,5},{5,1},{9,13},{13,9},{2,6},{6,2},{1... | collective-permute-start | bytes 884744 | tf_op jit(solution)/shard_map/ppermute | solution.py:383
  (42 other events, 246.2 us)

commit v3 on v2

--- a/solution.py
+++ b/solution.py
@@ -136,7 +136,8 @@
 
 
 def probability_kernel(heads, block, q_ref, k_ref, row_ref, *refs):
-    a_hbm, a_ref, copy_sems = refs[-3:]
+    a_hbm, token_ref, a_ref, copy_sems = refs[-4:]
+    token_ref[...] = jnp.minimum(jnp.abs(row_ref[:, : token_ref.shape[1]]), 0.0)
     count = q_ref.shape[0] // block
 
     def copy(number):
@@ -169,9 +170,12 @@
     block = 256
     return pl.pallas_call(
         functools.partial(probability_kernel, heads, block),
-        out_shape=jax.ShapeDtypeStruct((heads, length, length), BF),
+        out_shape=(
+            pltpu.HBM((heads, length, length), BF),
+            jax.ShapeDtypeStruct((1, 128), F32),
+        ),
         in_specs=[VMEM] * 3 + [ANYWHERE] * len(gates),
-        out_specs=FAR,
+        out_specs=(FAR, VMEM),
         scratch_shapes=[
             pltpu.VMEM((heads, length, length), BF),
             pltpu.SemaphoreType.DMA((length // block,)),
@@ -286,21 +290,22 @@
     )(left, right, *more, gate)
 
 
-def sent_grad_kernel(left, right, sums, sent_ref):
+def sent_grad_kernel(left, right, sums, *refs):
+    sent_ref = refs[-1]
     step = left.shape[1] // 2
     sent_ref[:step] = product_left(left[:, step:], right[...]).astype(BF)
     sent_ref[step:] = jnp.zeros_like(sent_ref[step:])
     sent_ref[step : step + 2, : sums.shape[1]] = sums[...].astype(BF)
 
 
-def sent_grad(left, right, sums):
+def sent_grad(left, right, sums, gates):
     return pl.pallas_call(
         sent_grad_kernel,
         out_shape=jax.ShapeDtypeStruct((left.shape[1] // 2 + 16, right.shape[1]), BF),
-        in_specs=[VMEM] * 3,
+        in_specs=[VMEM] * 3 + [ANYWHERE] * len(gates),
         out_specs=VMEM,
         compiler_params=PARAMS,
-    )(left, right, sums)
+    )(left, right, sums, *gates)
 
 
 def split_kernel(count, bit, *refs):
@@ -319,6 +324,108 @@
         out_specs=(VMEM,) * 2,
         compiler_params=PARAMS,
     )(*values, *gates)
+
+
+def split_parts_kernel(parts, merged, bit, *refs):
+    own_ref, other_ref = refs[-2:]
+    low = place_bit(bit)
+    start = 0
+    for number, rows in enumerate(parts):
+        if merged:
+            value = refs[0][start : start + rows] + refs[1][start : start + rows].astype(F32)
+        else:
+            value = refs[2 * number][...] + refs[2 * number + 1][...].astype(F32)
+        first, second = value[: rows // 2], value[rows // 2 :]
+        at = slice(start // 2, (start + rows) // 2)
+        own_ref[at] = jnp.where(low, first, second)
+        other_ref[at] = jnp.where(low, second, first).astype(BF)
+        start += rows
+
+
+def split_parts(values, parts, bit, gates):
+    merged = len(values) == 2
+    shape = (sum(parts) // 2, values[0].shape[1])
+    return pl.pallas_call(
+        functools.partial(split_parts_kernel, parts, merged, bit),
+        out_shape=(jax.ShapeDtypeStruct(shape, F32), jax.ShapeDtypeStruct(shape, BF)),
+        in_specs=[VMEM] * len(values) + [ANYWHERE] * len(gates),
+        out_specs=(VMEM,) * 2,
+        compiler_params=PARAMS,
+    )(*values, *gates)
+
+
+def join_parts_kernel(parts, last, bit, own_ref, other_ref, *refs):
+    low = place_bit(bit)
+    start = 0
+    for number, rows in enumerate(parts):
+        at = slice(start, start + rows)
+        own, other = own_ref[at], other_ref[at]
+        ref, base = (refs[number], 0) if last else (refs[0], 2 * start)
+        ref[base : base + rows] = jnp.where(low, own, other).astype(ref.dtype)
+        ref[base + rows : base + 2 * rows] = jnp.where(low, other, own).astype(ref.dtype)
+        start += rows
+
+
+def join_parts(own, other, parts, bit, last):
+    columns = own.shape[1]
+    if last:
+        shapes = tuple(jax.ShapeDtypeStruct((2 * rows, columns), F32) for rows in parts)
+    else:
+        shapes = (jax.ShapeDtypeStruct((2 * own.shape[0], columns), BF),)
+    return pl.pallas_call(
+        functools.partial(join_parts_kernel, parts, last, bit),
+        out_shape=shapes,
+        in_specs=[VMEM] * 2,
+        out_specs=(VMEM,) * len(shapes),
+        compiler_params=PARAMS,
+    )(own, other)
+
+
+def finish_kernel(parts, own_ref, other_ref, down_ref, out_ref, *small_refs):
+    low = place_bit(1)
+    joined = []
+    start = 0
+    for rows in parts:
+        own, other = own_ref[start : start + rows], other_ref[start : start + rows]
+        joined.append((jnp.where(low, own, other), jnp.where(low, other, own)))
+        start += rows
+    for number in range(2):
+        down_ref[number * parts[0] : (number + 1) * parts[0]] = joined[0][number].astype(F32)
+    value = jnp.concatenate([part.astype(F32) for part in joined[1]], axis=0)
+    at = out_ref.shape[0]
+    out_ref[...] = value[:at]
+    step = value.shape[1]
+    for ref in small_refs:
+        for row in range(ref.shape[0]):
+            for piece in range(ref.shape[1] // step):
+                ref[row : row + 1, piece * step : (piece + 1) * step] = value[at : at + 1]
+                at += 1
+
+
+def finish(own, other, parts, out_rows, width, hidden):
+    columns = own.shape[1]
+    shapes = [(2 * parts[0], columns), (out_rows, columns)] + [(2, width)] * 3 + [(1, hidden)]
+    return pl.pallas_call(
+        functools.partial(finish_kernel, parts),
+        out_shape=tuple(jax.ShapeDtypeStruct(shape, F32) for shape in shapes),
+        in_specs=[VMEM] * 2,
+        out_specs=(VMEM,) * len(shapes),
+        compiler_params=PARAMS,
+    )(own, other)
+
+
+def add_wide_kernel(first_ref, second_ref, *refs):
+    refs[-1][...] = first_ref[...].astype(F32) + second_ref[...].astype(F32)
+
+
+def add_wide(first, second, gates):
+    return pl.pallas_call(
+        add_wide_kernel,
+        out_shape=jax.ShapeDtypeStruct(first.shape, F32),
+        in_specs=[VMEM] * 2 + [ANYWHERE] * len(gates),
+        out_specs=VMEM,
+        compiler_params=PARAMS,
+    )(first, second, *gates)
 
 
 def add_kernel(own_ref, other_ref, *refs):
@@ -458,13 +565,15 @@
             parts = [product_right(value, group) for group in groups]
             return parts[0] if len(parts) == 1 else jnp.concatenate(parts, axis=1)
 
-        def row_total(partial):
+        def row_total(partial, gates=()):
             mine, theirs = partial[:half], partial[half:].astype(BF)
-            total = mine + flip(theirs, "tensor", 1).astype(F32)
-            for bit in bits("tensor")[1:]:
+            received = flip(theirs, "tensor", 1)
+            total = add_wide(mine, received, gates) if gates else mine + received.astype(F32)
+            for bit in bits("tensor")[1:-1]:
                 low = total.astype(BF)
                 total = low.astype(F32) + flip(low, "tensor", bit).astype(F32)
-            return total, low
+            low = total.astype(BF)
+            return low, flip(low, "tensor", bits("tensor")[-1])
 
         def both_halves(value):
             return jnp.concatenate([value, flip(value, "tensor", 1)], axis=0)
@@ -475,21 +584,6 @@
 
         def context_total(value):
             return lax.psum(value.astype(BF), "context").astype(F32)
-
-        def finish_total(halves, gates, done=0):
-            order = bits("context")
-            for number, bit in enumerate(order):
-                if number < done:
-                    continue
-                received = flip(halves[1], "context", bit)
-                if number + 1 < len(order):
-                    halves = split([halves[0], received], order[number + 1], gates[number])
-            summed = low = add_low(halves[0], received, gates[len(order) - 1])
-            for number, bit in enumerate(reversed(order)):
-                kind = F32 if number + 1 == len(order) else BF
-                received = flip(low, "context", bit)
-                low = join(low, received, bit, kind, gates[len(order) + number])
-            return low, summed
 
         def context_blocks(value):
             blocks = [value]
@@ -521,9 +615,9 @@
             return jnp.concatenate([take_half(tokens, which), numbers], axis=0)
 
         halves = context_blocks(with_segments(core_at))
-        up_groups = gather_weight(after(up_weight[0], halves[1]), 0)
+        up_groups = gather_weight(after(up_weight[0], halves[2 % packs]), 0)
         output_groups = gather_weight(after(output_weight[0], halves[2 % packs]), 1)
-        down_groups = gather_weight(after(down_weight[0], halves[3 % packs]), 1)
+        down_groups = gather_weight(after(down_weight[0], halves[2 % packs]), 1)
         others = [with_segments(1 - core_at)] + [flip(block, "tensor", 1) for block in halves[1:]]
         blocks = [block for pair in zip(halves, others) for block in pair]
         pack_queries, pack_keys, pack_values, context, pack_rows, pack_segments = front(
@@ -534,11 +628,11 @@
             return lax.dynamic_slice_in_dim(value, context_at * rows, rows, 0)
 
         hidden_half = columns(take_half(tokens, core_at)).astype(F32)
-        total, sent = row_total(expand(context, output_groups))
-        pack_probability = probabilities(
+        sent, received = row_total(expand(context, output_groups))
+        pack_probability, token = probabilities(
             pack_queries, pack_keys, pack_segments, (sent, up_groups[-1])
         )
-        attended = after(total, pack_probability, down_groups[-1]) + row_pair[0]
+        attended = add_wide(sent, received, (token, down_groups[-1])) + row_pair[0]
         normed_one, inverse_one = normalize(hidden_half + attended)
         first_norm = normed_one * gains[0] + shifts[0]
         first_low = both_halves(first_norm.astype(BF))
@@ -549,11 +643,13 @@
         slope = cumulative + preactivation * DENSITY_FACTOR * jnp.exp(
             -0.5 * preactivation * preactivation
         )
-        total, _ = row_total(expand(activated, down_groups))
+        sent, received = row_total(expand(activated, down_groups))
         step = width // 2
+        gates = ()
         if paired:
             first_pair = swapped(first_low[:, step:])
-            total = after(total, first_pair)
+            gates = (first_pair,)
+        total = add_wide(sent, received, gates)
         normed_two, inverse_two = normalize(first_norm + (total + row_pair[1]))
         result = (normed_two * gains[1] + shifts[1]).astype(BF)
 
@@ -580,51 +676,19 @@
 
         grad_pre = contract_right(grad_two_low, down_groups) * slope
         grad_pre_low = grad_pre.astype(BF)
-        total, sent = row_total(expand_right(grad_pre_low, up_groups))
+        sent, received = row_total(expand_right(grad_pre_low, up_groups))
+        gates = ()
         if paired:
             pre_pair = swapped(grad_pre_low)
             down_mine, down_sent = column_grad(activated, grad_two_low, sent)
             down_received = swapped(down_sent)
-            total = after(total, down_sent, pre_pair)
-        grad_first = grad_two + total
+            gates = (down_sent, pre_pair)
+            up_halves = pair_grad(first_low[:, :step], first_pair, grad_pre_low, pre_pair, sent)
+        grad_first = grad_two + add_wide(sent, received, gates)
         grad_one = normalize_back(grad_first, normed_one, inverse_one, gains[0])
         grad_one_low = both_halves(grad_one.astype(BF))
         grad_context = contract_right(grad_one_low, output_groups).astype(BF)
         grad_context_blocks = context_blocks(grad_context)
-
-        gates = []
-        if paired:
-            up_halves = pair_grad(
-                first_low[:, :step], first_pair, grad_pre_low, pre_pair, grad_context
-            )
-            up_halves = split(
-                [up_halves[0], flip(up_halves[1], "context", 1)], 2, (grad_context_blocks[-1],)
-            )
-            down_halves = split([down_mine, down_received], 1, (grad_context_blocks[-1],))
-            gates = [down_halves[1], up_halves[1], layer_output]
-
-        pack_projected, bias_grads = attention_back(
-            pack_probability, pack_queries, pack_keys, pack_values, grad_context_blocks, gates
-        )
-        total, final_sent = row_total(expand_right(own_block(pack_projected), input_groups))
-        if paired:
-            input_sent = sent_grad(pack_rows, pack_projected, bias_grads)
-            received = swapped(input_sent)
-            grad_input = product_left(pack_rows[:, :step], pack_projected) + received[
-                :step
-            ].astype(F32)
-            bias_grads = bias_grads.astype(BF).astype(F32) + received[
-                step : step + 2, :shard_width
-            ].astype(F32)
-            grad_up, up_low = finish_total(
-                up_halves, [(), (pack_projected,), (), ()], 1
-            )
-            grad_down, down_low = finish_total(down_halves, [(pack_projected,), (), (), ()])
-        else:
-            grad_input = scattered(pack_rows, pack_projected, 0)
-            bias_grads = lax.psum(bias_grads, "weight")
-            grad_down = context_total(scattered(activated, grad_two_low, 1))
-            grad_up = context_total(scattered(first_low, grad_pre_low, 0))
 
         small = row_sums(
             grad_one, grad_two, grad_first, normed_one, cotangent_rows, normed_two, grad_context
@@ -635,24 +699,67 @@
         size = joined.shape[0]
         joined = jnp.pad(joined, (0, -size % (16 * share_width))).reshape(-1, share_width)
         out_rows, joined_rows = context.shape[1], joined.shape[0]
-        if paired:
-            below = -out_rows % (16 * packs * 4)
-            joined = jnp.pad(joined, ((0, (below - joined_rows) % (16 * packs)), (0, 0)))
+        chained = paired and packs == 4
+        gates = []
+        if chained:
+            up_halves = split(
+                [up_halves[0], flip(up_halves[1], "context", 1)], 2, (grad_context_blocks[2],)
+            )
+            last = (grad_context_blocks[-1],)
+            below = -out_rows % 256
+            joined = jnp.pad(joined, ((0, below - joined_rows), (0, 0)))
             out_mine, out_sent = column_grad(context, grad_one_low, grad_context, joined)
-            out_halves = split([out_mine, swapped(out_sent)], 1, (down_low,))
-            merged, _ = finish_total(out_halves, [(), (), (), ()])
+            parts = (down_mine.shape[0], out_mine.shape[0])
+            halves = split_parts(
+                (down_mine, down_received, out_mine, swapped(out_sent)), parts, 1, last
+            )
+            gates = [halves[1], up_halves[1], layer_output]
+
+        pack_projected, bias_grads = attention_back(
+            pltpu.with_memory_space_constraint(pack_probability, pltpu.HBM),
+            pack_queries,
+            pack_keys,
+            pack_values,
+            grad_context_blocks,
+            gates,
+        )
+        ends = ()
+        if chained:
+            parts = tuple(rows // 2 for rows in parts)
+            halves = split_parts(
+                (halves[0], flip(halves[1], "context", 1)), parts, 2, (pack_projected,)
+            )
+            ends = (up_halves[1], halves[1])
+            input_sent = sent_grad(
+                pack_rows, pack_projected, bias_grads, (up_halves[1], halves[1])
+            )
+            low = add_low(up_halves[0], flip(up_halves[1], "context", 2))
+            low = join(low, flip(low, "context", 2), 2, BF)
+            grad_up = join(low, flip(low, "context", 1), 1, F32)
+            low = add_low(halves[0], flip(halves[1], "context", 2))
+            small_parts = tuple(rows // 2 for rows in parts)
+            (low,) = join_parts(low, flip(low, "context", 2), small_parts, 2, False)
+            grad_down, grad_out, *small, hidden_sum = finish(
+                low, flip(low, "context", 1), parts, out_rows, width, up_bias.shape[1]
+            )
+            received = swapped(input_sent)
+            grad_input = product_left(pack_rows[:, :step], pack_projected) + received[
+                :step
+            ].astype(F32)
+            bias_grads = bias_grads.astype(BF).astype(F32) + received[
+                step : step + 2, :shard_width
+            ].astype(F32)
         else:
-            merged = jnp.concatenate(
-                [
-                    context_total(scattered(context, grad_one_low, 1)),
-                    context_total(lax.psum(joined, "weight")),
-                ],
-                axis=0,
-            )
-        grad_out = merged[:out_rows]
-        joined = merged[out_rows : out_rows + joined_rows].reshape(-1)
-        small = joined[: 6 * width].reshape(3, 2, width)
-        hidden_sum = joined[6 * width : size]
+            grad_input = scattered(pack_rows, pack_projected, 0)
+            bias_grads = lax.psum(bias_grads, "weight")
+            grad_down = context_total(scattered(activated, grad_two_low, 1))
+            grad_up = context_total(scattered(first_low, grad_pre_low, 0))
+            grad_out = context_total(scattered(context, grad_one_low, 1))
+            joined = lax.psum(lax.psum(joined, "weight"), "context").reshape(-1)
+            small = joined[: 6 * width].reshape(3, 2, width)
+            hidden_sum = joined[None, 6 * width : size]
+        sent, received = row_total(expand_right(own_block(pack_projected), input_groups), ends)
+        total = sent.astype(F32) + received.astype(F32)
         grad_tokens = columns(own_rows(both_halves(grad_one + total)))
         return (
             layer_output,
@@ -664,7 +771,7 @@
             small[1][None],
             small[2][None],
             grad_up[None],
-            hidden_sum[None],
+            hidden_sum,
             grad_down[None],
         )
 

time: 186 us -> 171 us (0.919); the launches traced: 183 us -> 170 us
  local copies, waits for them, and re-layouts: 21.6 us -> 13.6 us
  starting transfers between devices: 41.5 us -> 36.3 us
  between operations: 6.98 us -> 2.35 us
  Pallas kernels: 28.1 us -> 32.2 us
  matrix products: 13.8 us -> 9.85 us
  waiting for transfers between devices: 58.5 us -> 62.4 us
    ppermute x44 -> x40, starting transfers between devices: 41.5 us -> 36.3 us  [flip(): return lax.ppermute(value, axis, [(i, i ^ bit) for i in range(count[axis])])]
    slice x8 -> x1, local copies, waits for them, and re-layouts: 4.8 us -> 0.51 us  [after(): first = lax.slice(other, (0,) * other.ndim, (1,) * other.ndim).reshape(())]
    ppermute x44 -> x40, waiting for transfers between devices: 58.5 us -> 62.4 us  [flip(): return lax.ppermute(value, axis, [(i, i ^ bit) for i in range(count[axis])])]
    pallas_call x0 -> x8, Pallas kernels: none -> 2.78 us  [the longest x2 1.38 us: split_parts(): pl.pallas_call(functools.partial(split_parts_kernel, parts, merged, bit),...]
    pallas_call x1, Pallas kernels: 8.53 us -> 10.6 us  [attention_back(): pl.pallas_call(functools.partial(attention_back_kernel, heads, len(blocks...]
    dot_general x6, matrix products: 6 us -> 4.08 us  [product(): return jnp.dot(left, right, preferred_element_type=F32)]
    unnamed x94 -> x90, local copies, waits for them, and re-layouts: 10.2 us -> 8.49 us
  transfers between devices with their start and end apart: 44 -> 40, of which waited for: 19 -> 18; matrix products, arithmetic and copies ran while one was open for 16% -> 10% of each run, Pallas kernels for 15% -> 18%
where the time goes in v3:
time: 171 us; the launch traced here: 170 us
  waiting for transfers between devices  62.4 us (36%)
  starting transfers between devices  36.3 us (21%)
  Pallas kernels  32.2 us (19%)
  other arithmetic  13.7 us (8%)
  local copies, waits for them, and re-layouts  13.6 us (8%)
  matrix products  9.85 us (6%)
  between operations  2.35 us (1%)
    ppermute x40, waiting for transfers between devices, flip(): return lax.ppermute(value, axis, [(i, i ^ bit) for i in range(count[axis])])  62.4 us
    ppermute x40, starting transfers between devices, flip(): return lax.ppermute(value, axis, [(i, i ^ bit) for i in range(count[axis])])  36.3 us
    pallas_call x1, Pallas kernels, attention_back(): pl.pallas_call(functools.partial(attention_back_kernel, heads, len(blocks...  10.6 us
    unnamed x90, local copies, waits for them, and re-layouts  8.49 us
    pallas_call x1, Pallas kernels, probabilities(): pl.pallas_call(functools.partial(probability_kernel, heads, block), out_s...  8.15 us
    dot_general x8, matrix products, product_right(): lax.dot_general(left, right, (((1,), (1,)), ((), ())), preferred_element_...  4.97 us
    pallas_call x1, Pallas kernels, front(): pl.pallas_call(functools.partial(front_kernel, width // HD, packs, len(gr...  4.76 us
    dot_general x6, matrix products, product(): return jnp.dot(left, right, preferred_element_type=F32)  4.08 us
  transfers between devices with their start and end apart: 40, of which 18 were waited for; matrix products, arithmetic and copies ran while one was open for 10% of the time, Pallas kernels for 18%

profile of v3, /device:TPU:4, one launch (start us, length us, event | category | flops | bytes accessed | tf_op | source)
XLA Modules:
  0.0 170.4 jit_solution(11224129606433351928)
XLA Ops:
  2.8 2.7 %collective-permute-start.2 = (bf16[144,768]{1,0:T(8,128)(2,1)S(1)}, bf16[144,768]{1,0:T(8,128)(2,1)S(1)}, u32[]{:S(2)}, u32[]{:S(2)}) collective-permute-start(bf16[144,768]{1,0:T(8,128)(2,1)S(1)} %fusion.28.refs_0_), channel_id=1, source_target_pairs={{0,8},{4,12},{8,0},{12,4},{1,9},{5,13},{9,1},{13,5},{2,10},{6,14},... | collective-permute-start | bytes 663560 | tf_op jit(solution)/shard_map/ppermute | solution.py:490
  5.4 1.6 collective-permute-start
  7.9 7.8 %collective-permute-done.2.refs_4_ = bf16[144,768]{1,0:T(8,128)(2,1)S(1)} collective-permute-done((bf16[144,768]{1,0:T(8,128)(2,1)S(1)}, bf16[144,768]{1,0:T(8,128)(2,1)S(1)}, u32[]{:S(2)}, u32[]{:S(2)}) %collective-permute-start.2) | collective-permute-done | bytes 221216 | tf_op jit(solution)/shard_map/ppermute | solution.py:490
  19.5 4.3 %collective-permute-done.4.refs_6_ = bf16[144,768]{1,0:T(8,128)(2,1)S(1)} collective-permute-done((bf16[144,768]{1,0:T(8,128)(2,1)S(1)}, bf16[144,768]{1,0:T(8,128)(2,1)S(1)}, u32[]{:S(2)}, u32[]{:S(2)}) %collective-permute-start.4) | collective-permute-done | bytes 221216 | tf_op jit(solution)/shard_map/ppermute | solution.py:490
  23.8 1.9 %add_bitcast_fusion = bf16[768,384]{1,0:T(8,128)(2,1)} fusion(bf16[1,768,384]{2,1,0:T(8,128)(2,1)} %param.22, bf16[]{:T(256)} %bitcast.4), kind=kLoop, calls=%fused_computation.24 | loop fusion | flops 294912 | bytes 1179650 | tf_op jit(solution)/shard_map/add | solution.py:57
  25.7 1.3 collective-permute-start.10
  27.7 4.8 %shard_map.203 = (bf16[1024,192]{1,0:T(8,128)(2,1)S(1)}, bf16[1024,192]{1,0:T(8,128)(2,1)S(1)}, bf16[1024,192]{1,0:T(8,128)(2,1)S(1)}, bf16[256,192]{1,0:T(8,128...) custom-call(bf16[144,768]{1,0:T(8,128)(2,1)S(1)} %fusion.28.refs_0_, ...), custom_call_target="tpu_custom_call" | custom-call | tf_op jit(solution)/shard_map/pallas_call | solution.py:122
  32.5 1.2 copy-done.1
  35.6 1.5 collective-permute-done.8
  38.1 1.3 collective-permute-start.9
  40.5 1.6 collective-permute-done.10.refs_1_
  42.0 8.1 %shard_map.204 = (bf16[3,1024,1024]{2,1,0:T(8,128)(2,1)}, f32[1,128]{1,0:T(1,128)S(1)}) custom-call(bf16[1024,192]{1,0:T(8,128)(2,1)S(1)} %get-tuple-element.40.q_ref, bf16[1024,192]{1,0:T(8,128)(2,1)S(1)} %copy-done.14, f32[1,1024]{1,0:T(1,128)S(1)} %get-tuple-element.42.row_ref, bf16[128,768]{1,0:T(8,128)(2,1)S(1)} %fusion.18.refs_0_.first_ref, ...), custom_call_target="tpu_custom_call" | custom-call | tf_op jit(solution)/shard_map/pallas_call | solution.py:171
  50.2 4.1 %collective-permute-done.11.refs_1_ = bf16[768,384]{1,0:T(8,128)(2,1)S(1)} collective-permute-done((bf16[768,384]{1,0:T(8,128)(2,1)}, bf16[768,384]{1,0:T(8,128)(2,1)S(1)}, u32[]{:S(2)}, u32[]{:S(2)}) %collective-permute-start.11) | collective-permute-done | bytes 589856 | tf_op jit(solution)/shard_map/ppermute | solution.py:490
  55.1 1.4 collective-permute-done.12
  56.8 1.5 multiply_convert_fusion
  58.3 1.4 fusion.64
  60.4 1.3 collective-permute-start.15
  61.7 1.5 collective-permute-start.14
  64.1 3.5 %collective-permute-done.15.refs_0_.left_pair = bf16[256,384]{1,0:T(8,128)(2,1)S(1)} collective-permute-done((bf16[256,384]{1,0:T(8,128)(2,1)S(1)}, bf16[256,384]{1,0:T(8,128)(2,1)S(1)}, u32[]{:S(2)}, u32[]{:S(2)}) %collective-permute-start.15) | collective-permute-done | bytes 196640 | tf_op jit(solution)/shard_map/ppermute | solution.py:490
  70.1 1.4 collective-permute-done.17
  72.0 1.6 fusion.53
  73.6 1.4 fusion.66
  77.0 1.3 collective-permute-start.20
  79.4 1.6 collective-permute-start.19
  83.1 1.2 shard_map.207
  85.3 2.8 %collective-permute-done.20.refs_1_.right_pair = bf16[256,768]{1,0:T(8,128)(2,1)S(1)} collective-permute-done((bf16[256,768]{1,0:T(8,128)(2,1)S(1)}, bf16[256,768]{1,0:T(8,128)(2,1)S(1)}, u32[]{:S(2)}, u32[]{:S(2)}) %collective-permute-start.20) | collective-permute-done | bytes 393248 | tf_op jit(solution)/shard_map/ppermute | solution.py:490
  89.5 1.3 collective-permute-start.25
  90.7 1.2 shard_map.212
  92.0 1.7 collective-permute-start.28
  94.2 3.4 %collective-permute-start.23 = (bf16[256,192]{1,0:T(8,128)(2,1)S(1)}, bf16[256,192]{1,0:T(8,128)(2,1)S(1)}, u32[]{:S(2)}, u32[]{:S(2)}) collective-permute-start(bf16[256,192]{1,0:T(8,128)(2,1)S(1)} %fusion.2._.refs_1_.refs_0_), channel_id=1, source_target_pairs={{0,8},{4,12},{8,0},{12,4},{1,9},{5,13},{9,1},{13,5},{2,10},{6,14},... | collective-permute-start | bytes 294920 | tf_op jit(solution)/shard_map/ppermute | solution.py:490
  100.5 3.5 %collective-permute-done.23.refs_2_ = bf16[256,192]{1,0:T(8,128)(2,1)S(1)} collective-permute-done((bf16[256,192]{1,0:T(8,128)(2,1)S(1)}, bf16[256,192]{1,0:T(8,128)(2,1)S(1)}, u32[]{:S(2)}, u32[]{:S(2)}) %collective-permute-start.23) | collective-permute-done | bytes 98336 | tf_op jit(solution)/shard_map/ppermute | solution.py:490
  104.0 4.1 %collective-permute-start.24 = (bf16[256,192]{1,0:T(8,128)(2,1)S(1)}, bf16[256,192]{1,0:T(8,128)(2,1)S(1)}, u32[]{:S(2)}, u32[]{:S(2)}) collective-permute-start(bf16[256,192]{1,0:T(8,128)(2,1)S(1)} %collective-permute-done.23.refs_2_), channel_id=1, source_target_pairs={{0,4},{4,0},{8,12},{12,8},{1,5},{5,1},{9,13},{13,9},{2,6},{6,2},{1... | collective-permute-start | bytes 294920 | tf_op jit(solution)/shard_map/ppermute | solution.py:490
  108.3 1.2 copy-done.10
  110.6 1.2 collective-permute-done.24.refs_4_.refs_3_
  111.8 1.3 shard_map.211
  113.1 2.5 %collective-permute-start.30 = (bf16[512,384]{1,0:T(8,128)(2,1)S(1)}, bf16[512,384]{1,0:T(8,128)(2,1)S(1)}, u32[]{:S(2)}, u32[]{:S(2)}) collective-permute-start(bf16[512,384]{1,0:T(8,128)(2,1)S(1)} %get-tuple-element.50.refs_4_), channel_id=1, source_target_pairs={{0,4},{4,0},{8,12},{12,8},{1,5},{5,1},{9,13},{13,9},{2,6},{6,2},{1... | collective-permute-start | bytes 1179656 | tf_op jit(solution)/shard_map/ppermute | solution.py:490
  115.7 10.6 %shard_map.214 = (bf16[1024,576]{1,0:T(8,128)(2,1)S(1)}, f32[2,192]{1,0:T(2,128)S(1)}) custom-call(bf16[3,1024,1024]{2,1,0:T(8,128)(2,1)} %get-tuple-element.45.a_hbm, bf16[1024,192]{1,0:T(8,128)(2,1)S(1)} %copy-done.12, bf16[1024,192]{1,0:T(8,128)(2,1)S(1)} %copy-done.15, bf16[1024,192]{1,0:T(8,128)(2,1)S(1)} %copy-done.19, ...), custom_call_target="tpu_custom_call" | custom-call | flops 10000000000 | bytes 10000000 | tf_op jit(solution)/shard_map/pallas_call | solution.py:222
  128.7 6.2 %collective-permute-done.38.other_ref = bf16[96,768]{1,0:T(8,128)(2,1)S(1)} collective-permute-done((bf16[96,768]{1,0:T(8,128)(2,1)S(1)}, bf16[96,768]{1,0:T(8,128)(2,1)S(1)}, u32[]{:S(2)}, u32[]{:S(2)}) %collective-permute-start.38) | collective-permute-done | bytes 147488 | tf_op jit(solution)/shard_map/ppermute | solution.py:490
  135.2 1.2 copy-done.2
  138.0 2.1 %collective-permute-start.34 = (bf16[256,384]{1,0:T(8,128)(2,1)S(1)}, bf16[256,384]{1,0:T(8,128)(2,1)S(1)}, u32[]{:S(2)}, u32[]{:S(2)}) collective-permute-start(bf16[256,384]{1,0:T(8,128)(2,1)S(1)} %get-tuple-element.56.refs_1_), channel_id=1, source_target_pairs={{0,8},{4,12},{8,0},{12,4},{1,9},{5,13},{9,1},{13,5},{2,10},{6,14},... | collective-permute-start | bytes 589832 | tf_op jit(solution)/shard_map/ppermute | solution.py:490
  140.2 1.6 collective-permute-start.31
  141.7 2.1 %collective-permute-done.39.other_ref = bf16[192,768]{1,0:T(8,128)(2,1)S(1)} collective-permute-done((bf16[192,768]{1,0:T(8,128)(2,1)S(1)}, bf16[192,768]{1,0:T(8,128)(2,1)S(1)}, u32[]{:S(2)}, u32[]{:S(2)}) %collective-permute-start.39) | collective-permute-done | bytes 294944 | tf_op jit(solution)/shard_map/ppermute | solution.py:490
  144.9 3.4 %collective-permute-done.34.other_ref = bf16[256,384]{1,0:T(8,128)(2,1)S(1)} collective-permute-done((bf16[256,384]{1,0:T(8,128)(2,1)S(1)}, bf16[256,384]{1,0:T(8,128)(2,1)S(1)}, u32[]{:S(2)}, u32[]{:S(2)}) %collective-permute-start.34) | collective-permute-done | bytes 196640 | tf_op jit(solution)/shard_map/ppermute | solution.py:490
  148.6 10.3 %collective-permute-done.35.other_ref = bf16[256,384]{1,0:T(8,128)(2,1)S(1)} collective-permute-done((bf16[256,384]{1,0:T(8,128)(2,1)S(1)}, bf16[256,384]{1,0:T(8,128)(2,1)S(1)}, u32[]{:S(2)}, u32[]{:S(2)}) %collective-permute-start.35) | collective-permute-done | bytes 196640 | tf_op jit(solution)/shard_map/ppermute | solution.py:490
  160.7 1.2 copy.39
  161.9 1.3 add_bitcast_fusion.3
  164.2 5.0 %collective-permute-done.36.other_ref = bf16[512,384]{1,0:T(8,128)(2,1)S(1)} collective-permute-done((bf16[512,384]{1,0:T(8,128)(2,1)S(1)}, bf16[512,384]{1,0:T(8,128)(2,1)S(1)}, u32[]{:S(2)}, u32[]{:S(2)}) %collective-permute-start.36) | collective-permute-done | bytes 393248 | tf_op jit(solution)/shard_map/ppermute | solution.py:490
  169.2 1.2 shard_map.220
  (224 shorter events, 36.6 us)
Async XLA Ops:
  0.7 16.2 %copy-start.39 = (bf16[1,192,384]{2,1,0:T(8,128)(2,1)S(1)}, bf16[1,192,384]{2,1,0:T(8,128)(2,1)}, u32[]{:S(2)}) copy-start(bf16[1,192,384]{2,1,0:T(8,128)(2,1)} %param.16) | copy-start | bytes 442372
  0.7 17.9 %copy-start.35 = (bf16[1,384,768]{2,1,0:T(8,128)(2,1)S(1)}, bf16[1,384,768]{2,1,0:T(8,128)(2,1)}, u32[]{:S(2)}) copy-start(bf16[1,384,768]{2,1,0:T(8,128)(2,1)} %param.20) | copy-start | bytes 1769476
  2.8 13.0 %collective-permute-start.2 = (bf16[144,768]{1,0:T(8,128)(2,1)S(1)}, bf16[144,768]{1,0:T(8,128)(2,1)S(1)}, u32[]{:S(2)}, u32[]{:S(2)}) collective-permute-start(bf16[144,768]{1,0:T(8,128)(2,1)S(1)} %fusion.28.refs_0_), channel_id=1, source_target_pairs={{0,8},{4,12},{8,0},{12,4},{1,9},{5,13},{9,1},{13,5},{2,10},{6,14},... | collective-permute-start | bytes 663560 | tf_op jit(solution)/shard_map/ppermute | solution.py:490
  5.4 12.7 %collective-permute-start = (bf16[144,768]{1,0:T(8,128)(2,1)S(1)}, bf16[144,768]{1,0:T(8,128)(2,1)S(1)}, u32[]{:S(2)}, u32[]{:S(2)}) collective-permute-start(bf16[144,768]{1,0:T(8,128)(2,1)S(1)} %fusion.28.refs_0_), channel_id=1, source_target_pairs={{0,4},{4,0},{8,12},{12,8},{1,5},{5,1},{9,13},{13,9},{2,6},{6,2},{1... | collective-permute-start | bytes 663560 | tf_op jit(solution)/shard_map/ppermute | solution.py:490
  7.2 20.5 %collective-permute-start.6 = (bf16[384,576]{1,0:T(8,128)(2,1)S(1)}, bf16[384,576]{1,0:T(8,128)(2,1)S(1)}, u32[]{:S(2)}, u32[]{:S(2)}) collective-permute-start(bf16[384,576]{1,0:T(8,128)(2,1)S(1)} %copy.35.refs_9_), channel_id=1, source_target_pairs={{0,16},{16,0},{1,17},{17,1},{2,18},{18,2},{3,19},{19,3},{4,20},{20... | collective-permute-start | bytes 1327112 | tf_op jit(solution)/shard_map/ppermute | solution.py:490
  16.9 10.8 %copy-start.17 = (f32[1,2,192]{2,1,0:T(2,128)S(1)}, f32[1,2,192]{2,1,0:T(2,128)}, u32[]{:S(2)}) copy-start(f32[1,2,192]{2,1,0:T(2,128)} %param.15) | copy-start | bytes 4612
  17.0 16.8 %copy-start.30 = (bf16[192,384]{1,0:T(8,128)(2,1)}, bf16[192,384]{1,0:T(8,128)(2,1)S(1)}, u32[]{:S(2)}) copy-start(bf16[192,384]{1,0:T(8,128)(2,1)S(1)} %add_bitcast_fusion.2) | copy-start | bytes 442372
  17.0 17.0 %collective-permute-start.7 = (bf16[192,384]{1,0:T(8,128)(2,1)S(1)}, bf16[192,384]{1,0:T(8,128)(2,1)S(1)}, u32[]{:S(2)}, u32[]{:S(2)}) collective-permute-start(bf16[192,384]{1,0:T(8,128)(2,1)S(1)} %add_bitcast_fusion.2), channel_id=1, source_target_pairs={{0,16},{16,0},{1,17},{17,1},{2,18},{18,2},{3,19},{19,3},{4,20},{20... | collective-permute-start | bytes 442376 | tf_op jit(solution)/shard_map/ppermute | solution.py:490
  17.5 6.3 %collective-permute-start.4 = (bf16[144,768]{1,0:T(8,128)(2,1)S(1)}, bf16[144,768]{1,0:T(8,128)(2,1)S(1)}, u32[]{:S(2)}, u32[]{:S(2)}) collective-permute-start(bf16[144,768]{1,0:T(8,128)(2,1)S(1)} %collective-permute-done.2.refs_4_), channel_id=1, source_target_pairs={{0,4},{4,0},{8,12},{12,8},{1,5},{5,1},{9,13},{13,9},{2,6},{6,2},{1... | collective-permute-start | bytes 663560 | tf_op jit(solution)/shard_map/ppermute | solution.py:490
  18.1 8.9 %collective-permute-start.3 = (bf16[144,768]{1,0:T(8,128)(2,1)S(1)}, bf16[144,768]{1,0:T(8,128)(2,1)S(1)}, u32[]{:S(2)}, u32[]{:S(2)}) collective-permute-start(bf16[144,768]{1,0:T(8,128)(2,1)S(1)} %collective-permute-done.2.refs_4_), channel_id=1, source_target_pairs={{0,1},{1,0},{2,3},{3,2},{4,5},{5,4},{6,7},{7,6},{8,9},{9,8},{10,11... | collective-permute-start | bytes 663560 | tf_op jit(solution)/shard_map/ppermute | solution.py:490
  18.1 7.6 %collective-permute-start.1 = (bf16[144,768]{1,0:T(8,128)(2,1)S(1)}, bf16[144,768]{1,0:T(8,128)(2,1)S(1)}, u32[]{:S(2)}, u32[]{:S(2)}) collective-permute-start(bf16[144,768]{1,0:T(8,128)(2,1)S(1)} %collective-permute-done.refs_2_), channel_id=1, source_target_pairs={{0,1},{1,0},{2,3},{3,2},{4,5},{5,4},{6,7},{7,6},{8,9},{9,8},{10,11... | collective-permute-start | bytes 663560 | tf_op jit(solution)/shard_map/ppermute | solution.py:490
  23.8 4.0 %collective-permute-start.5 = (bf16[144,768]{1,0:T(8,128)(2,1)S(1)}, bf16[144,768]{1,0:T(8,128)(2,1)S(1)}, u32[]{:S(2)}, u32[]{:S(2)}) collective-permute-start(bf16[144,768]{1,0:T(8,128)(2,1)S(1)} %collective-permute-done.4.refs_6_), channel_id=1, source_target_pairs={{0,1},{1,0},{2,3},{3,2},{4,5},{5,4},{6,7},{7,6},{8,9},{9,8},{10,11... | collective-permute-start | bytes 663560 | tf_op jit(solution)/shard_map/ppermute | solution.py:490
  25.7 16.3 %collective-permute-start.10 = (bf16[384,768]{1,0:T(8,128)(2,1)}, bf16[384,768]{1,0:T(8,128)(2,1)S(1)}, u32[]{:S(2)}, u32[]{:S(2)}) collective-permute-start(bf16[384,768]{1,0:T(8,128)(2,1)} %add_bitcast_fusion.1), channel_id=1, source_target_pairs={{0,16},{16,0},{1,17},{17,1},{2,18},{18,2},{3,19},{19,3},{4,20},{20... | collective-permute-start | bytes 1769480 | tf_op jit(solution)/shard_map/ppermute | solution.py:490
  27.0 27.3 %collective-permute-start.11 = (bf16[768,384]{1,0:T(8,128)(2,1)}, bf16[768,384]{1,0:T(8,128)(2,1)S(1)}, u32[]{:S(2)}, u32[]{:S(2)}) collective-permute-start(bf16[768,384]{1,0:T(8,128)(2,1)} %add_bitcast_fusion), channel_id=1, source_target_pairs={{0,16},{16,0},{1,17},{17,1},{2,18},{18,2},{3,19},{19,3},{4,20},{20... | collective-permute-start | bytes 1769480 | tf_op jit(solution)/shard_map/ppermute | solution.py:490
  35.4 1.6 collective-permute-start.8
  38.1 16.2 %collective-permute-start.9 = (bf16[128,768]{1,0:T(8,128)(2,1)S(1)}, bf16[128,768]{1,0:T(8,128)(2,1)S(1)}, u32[]{:S(2)}, u32[]{:S(2)}) collective-permute-start(bf16[128,768]{1,0:T(8,128)(2,1)S(1)} %fusion.18.refs_0_.first_ref), channel_id=1, source_target_pairs={{0,2},{1,3},{2,0},{3,1},{4,6},{5,7},{6,4},{7,5},{8,10},{9,11},{10,... | collective-permute-start | bytes 589832 | tf_op jit(solution)/shard_map/ppermute | solution.py:490
  42.0 12.3 %copy-start.29 = (bf16[128,768]{1,0:T(8,128)(2,1)S(1)}, bf16[128,768]{1,0:T(8,128)(2,1)}, u32[]{:S(2)}) copy-start(bf16[128,768]{1,0:T(8,128)(2,1)} %copy-done.28) | copy-start | bytes 589828
  54.9 1.5 collective-permute-start.12
  60.2 1.5 collective-permute-start.13
  60.4 7.2 %collective-permute-start.15 = (bf16[256,384]{1,0:T(8,128)(2,1)S(1)}, bf16[256,384]{1,0:T(8,128)(2,1)S(1)}, u32[]{:S(2)}, u32[]{:S(2)}) collective-permute-start(bf16[256,384]{1,0:T(8,128)(2,1)S(1)} %get-tuple-element.110), channel_id=1, source_target_pairs={{0,16},{16,0},{1,17},{17,1},{2,18},{18,2},{3,19},{19,3},{4,20},{20... | collective-permute-start | bytes 589832 | tf_op jit(solution)/shard_map/ppermute | solution.py:490
  61.7 7.0 %collective-permute-start.14 = (bf16[128,768]{1,0:T(8,128)(2,1)S(1)}, bf16[128,768]{1,0:T(8,128)(2,1)S(1)}, u32[]{:S(2)}, u32[]{:S(2)}) collective-permute-start(bf16[128,768]{1,0:T(8,128)(2,1)S(1)} %fusion.15.first_ref), channel_id=1, source_target_pairs={{0,2},{1,3},{2,0},{3,1},{4,6},{5,7},{6,4},{7,5},{8,10},{9,11},{10,... | collective-permute-start | bytes 589832 | tf_op jit(solution)/shard_map/ppermute | solution.py:490
  70.1 1.4 collective-permute-start.17
  76.5 1.8 %collective-permute-start.18 = (bf16[128,768]{1,0:T(8,128)(2,1)S(1)}, bf16[128,768]{1,0:T(8,128)(2,1)S(1)}, u32[]{:S(2)}, u32[]{:S(2)}) collective-permute-start(bf16[128,768]{1,0:T(8,128)(2,1)S(1)} %fusion.20), channel_id=1, source_target_pairs={{0,1},{1,0},{2,3},{3,2},{4,5},{5,4},{6,7},{7,6},{8,9},{9,8},{10,11... | collective-permute-start | bytes 589832 | tf_op jit(solution)/shard_map/ppermute | solution.py:490
  76.7 5.3 %collective-permute-start.16 = (bf16[128,768]{1,0:T(8,128)(2,1)}, bf16[128,768]{1,0:T(8,128)(2,1)S(1)}, u32[]{:S(2)}, u32[]{:S(2)}) collective-permute-start(bf16[128,768]{1,0:T(8,128)(2,1)} %get-tuple-element.106), channel_id=1, source_target_pairs={{0,1},{1,0},{2,3},{3,2},{4,5},{5,4},{6,7},{7,6},{8,9},{9,8},{10,11... | collective-permute-start | bytes 589832 | tf_op jit(solution)/shard_map/ppermute | solution.py:490
  77.0 11.2 %collective-permute-start.20 = (bf16[256,768]{1,0:T(8,128)(2,1)S(1)}, bf16[256,768]{1,0:T(8,128)(2,1)S(1)}, u32[]{:S(2)}, u32[]{:S(2)}) collective-permute-start(bf16[256,768]{1,0:T(8,128)(2,1)S(1)} %get-tuple-element.105.right), channel_id=1, source_target_pairs={{0,16},{16,0},{1,17},{17,1},{2,18},{18,2},{3,19},{19,3},{4,20},{20... | collective-permute-start | bytes 1179656 | tf_op jit(solution)/shard_map/ppermute | solution.py:490
  79.4 8.8 %collective-permute-start.19 = (bf16[128,768]{1,0:T(8,128)(2,1)S(1)}, bf16[128,768]{1,0:T(8,128)(2,1)S(1)}, u32[]{:S(2)}, u32[]{:S(2)}) collective-permute-start(bf16[128,768]{1,0:T(8,128)(2,1)S(1)} %fusion.12.refs_0_.first_ref._), channel_id=1, source_target_pairs={{0,2},{1,3},{2,0},{3,1},{4,6},{5,7},{6,4},{7,5},{8,10},{9,11},{10,... | collective-permute-start | bytes 589832 | tf_op jit(solution)/shard_map/ppermute | solution.py:490
  88.6 5.0 %collective-permute-start.21 = (bf16[128,768]{1,0:T(8,128)(2,1)S(1)}, bf16[128,768]{1,0:T(8,128)(2,1)S(1)}, u32[]{:S(2)}, u32[]{:S(2)}) collective-permute-start(bf16[128,768]{1,0:T(8,128)(2,1)S(1)} %get-tuple-element.90), channel_id=1, source_target_pairs={{0,1},{1,0},{2,3},{3,2},{4,5},{5,4},{6,7},{7,6},{8,9},{9,8},{10,11... | collective-permute-start | bytes 589832 | tf_op jit(solution)/shard_map/ppermute | solution.py:490
  89.5 21.2 %collective-permute-start.25 = (bf16[768,384]{1,0:T(8,128)(2,1)}, bf16[768,384]{1,0:T(8,128)(2,1)}, u32[]{:S(2)}, u32[]{:S(2)}) collective-permute-start(bf16[768,384]{1,0:T(8,128)(2,1)} %get-tuple-element.44.refs_0_), channel_id=1, source_target_pairs={{0,16},{16,0},{1,17},{17,1},{2,18},{18,2},{3,19},{19,3},{4,20},{20... | collective-permute-start | bytes 1769480 | tf_op jit(solution)/shard_map/ppermute | solution.py:490
  92.0 16.3 %collective-permute-start.28 = (bf16[192,768]{1,0:T(8,128)(2,1)}, bf16[192,768]{1,0:T(8,128)(2,1)}, u32[]{:S(2)}, u32[]{:S(2)}) collective-permute-start(bf16[192,768]{1,0:T(8,128)(2,1)} %get-tuple-element.52), channel_id=1, source_target_pairs={{0,4},{4,0},{8,12},{12,8},{1,5},{5,1},{9,13},{13,9},{2,6},{6,2},{1... | collective-permute-start | bytes 884744 | tf_op jit(solution)/shard_map/ppermute | solution.py:490
  94.2 9.9 %collective-permute-start.23 = (bf16[256,192]{1,0:T(8,128)(2,1)S(1)}, bf16[256,192]{1,0:T(8,128)(2,1)S(1)}, u32[]{:S(2)}, u32[]{:S(2)}) collective-permute-start(bf16[256,192]{1,0:T(8,128)(2,1)S(1)} %fusion.2._.refs_1_.refs_0_), channel_id=1, source_target_pairs={{0,8},{4,12},{8,0},{12,4},{1,9},{5,13},{9,1},{13,5},{2,10},{6,14},... | collective-permute-start | bytes 294920 | tf_op jit(solution)/shard_map/ppermute | solution.py:490
  97.6 18.1 %collective-permute-start.22 = (bf16[256,192]{1,0:T(8,128)(2,1)S(1)}, bf16[256,192]{1,0:T(8,128)(2,1)}, u32[]{:S(2)}, u32[]{:S(2)}) collective-permute-start(bf16[256,192]{1,0:T(8,128)(2,1)S(1)} %fusion.2._.refs_1_.refs_0_), channel_id=1, source_target_pairs={{0,4},{4,0},{8,12},{12,8},{1,5},{5,1},{9,13},{13,9},{2,6},{6,2},{1... | collective-permute-start | bytes 294920 | tf_op jit(solution)/shard_map/ppermute | solution.py:490
  98.1 10.1 %copy-start.21 = (bf16[256,768]{1,0:T(8,128)(2,1)S(1)}, bf16[256,768]{1,0:T(8,128)(2,1)}, u32[]{:S(2)}) copy-start(bf16[256,768]{1,0:T(8,128)(2,1)} %copy-done.20) | copy-start | bytes 1179652
  98.1 10.1 %copy-start.33 = (bf16[256,384]{1,0:T(8,128)(2,1)S(1)}, bf16[256,384]{1,0:T(8,128)(2,1)}, u32[]{:S(2)}) copy-start(bf16[256,384]{1,0:T(8,128)(2,1)} %get-tuple-element.107) | copy-start | bytes 589828
  98.1 1.3 collective-permute-start.26
  99.5 12.4 %copy-start.4 = (f32[768,384]{1,0:T(8,128)S(1)}, f32[768,384]{1,0:T(8,128)}, u32[]{:S(2)}) copy-start(f32[768,384]{1,0:T(8,128)} %copy-done.3) | copy-start | bytes 3538948
  99.8 12.1 %collective-permute-start.27 = (bf16[256,384]{1,0:T(8,128)(2,1)S(1)}, bf16[256,384]{1,0:T(8,128)(2,1)S(1)}, u32[]{:S(2)}, u32[]{:S(2)}) collective-permute-start(bf16[256,384]{1,0:T(8,128)(2,1)S(1)} %get-tuple-element.49), channel_id=1, source_target_pairs={{0,16},{16,0},{1,17},{17,1},{2,18},{18,2},{3,19},{19,3},{4,20},{20... | collective-permute-start | bytes 589832 | tf_op jit(solution)/shard_map/ppermute | solution.py:490
  104.0 7.8 %collective-permute-start.24 = (bf16[256,192]{1,0:T(8,128)(2,1)S(1)}, bf16[256,192]{1,0:T(8,128)(2,1)S(1)}, u32[]{:S(2)}, u32[]{:S(2)}) collective-permute-start(bf16[256,192]{1,0:T(8,128)(2,1)S(1)} %collective-permute-done.23.refs_2_), channel_id=1, source_target_pairs={{0,4},{4,0},{8,12},{12,8},{1,5},{5,1},{9,13},{13,9},{2,6},{6,2},{1... | collective-permute-start | bytes 294920 | tf_op jit(solution)/shard_map/ppermute | solution.py:490
  110.6 17.1 %collective-permute-start.37 = (bf16[96,768]{1,0:T(8,128)(2,1)S(1)}, bf16[96,768]{1,0:T(8,128)(2,1)S(1)}, u32[]{:S(2)}, u32[]{:S(2)}) collective-permute-start(bf16[96,768]{1,0:T(8,128)(2,1)S(1)} %get-tuple-element.53.refs_5_.refs_0_), channel_id=1, source_target_pairs={{0,8},{4,12},{8,0},{12,4},{1,9},{5,13},{9,1},{13,5},{2,10},{6,14},... | collective-permute-start | bytes 442376 | tf_op jit(solution)/shard_map/ppermute | solution.py:490
  113.1 21.9 %collective-permute-start.30 = (bf16[512,384]{1,0:T(8,128)(2,1)S(1)}, bf16[512,384]{1,0:T(8,128)(2,1)S(1)}, u32[]{:S(2)}, u32[]{:S(2)}) collective-permute-start(bf16[512,384]{1,0:T(8,128)(2,1)S(1)} %get-tuple-element.50.refs_4_), channel_id=1, source_target_pairs={{0,4},{4,0},{8,12},{12,8},{1,5},{5,1},{9,13},{13,9},{2,6},{6,2},{1... | collective-permute-start | bytes 1179656 | tf_op jit(solution)/shard_map/ppermute | solution.py:490
  127.7 7.3 %collective-permute-start.38 = (bf16[96,768]{1,0:T(8,128)(2,1)S(1)}, bf16[96,768]{1,0:T(8,128)(2,1)S(1)}, u32[]{:S(2)}, u32[]{:S(2)}) collective-permute-start(bf16[96,768]{1,0:T(8,128)(2,1)S(1)} %shard_map.221.own_ref), channel_id=1, source_target_pairs={{0,8},{4,12},{8,0},{12,4},{1,9},{5,13},{9,1},{13,5},{2,10},{6,14},... | collective-permute-start | bytes 442376 | tf_op jit(solution)/shard_map/ppermute | solution.py:490
  128.6 11.5 %collective-permute-start.29 = (bf16[128,768]{1,0:T(8,128)(2,1)S(1)}, bf16[128,768]{1,0:T(8,128)(2,1)S(1)}, u32[]{:S(2)}, u32[]{:S(2)}) collective-permute-start(bf16[128,768]{1,0:T(8,128)(2,1)S(1)} %fusion.19), channel_id=1, source_target_pairs={{0,1},{1,0},{2,3},{3,2},{4,5},{5,4},{6,7},{7,6},{8,9},{9,8},{10,11... | collective-permute-start | bytes 589832 | tf_op jit(solution)/shard_map/ppermute | solution.py:490
  135.0 8.8 %collective-permute-start.39 = (bf16[192,768]{1,0:T(8,128)(2,1)S(1)}, bf16[192,768]{1,0:T(8,128)(2,1)S(1)}, u32[]{:S(2)}, u32[]{:S(2)}) collective-permute-start(bf16[192,768]{1,0:T(8,128)(2,1)S(1)} %shard_map.222.own_ref), channel_id=1, source_target_pairs={{0,4},{4,0},{8,12},{12,8},{1,5},{5,1},{9,13},{13,9},{2,6},{6,2},{1... | collective-permute-start | bytes 884744 | tf_op jit(solution)/shard_map/ppermute | solution.py:490
  137.2 21.9 %collective-permute-start.33 = (bf16[400,576]{1,0:T(8,128)(2,1)S(1)}, bf16[400,576]{1,0:T(8,128)(2,1)S(1)}, u32[]{:S(2)}, u32[]{:S(2)}) collective-permute-start(bf16[400,576]{1,0:T(8,128)(2,1)S(1)} %shard_map.217), channel_id=1, source_target_pairs={{0,16},{16,0},{1,17},{17,1},{2,18},{18,2},{3,19},{19,3},{4,20},{20... | collective-permute-start | bytes 1382408 | tf_op jit(solution)/shard_map/ppermute | solution.py:490
  138.0 10.3 %collective-permute-start.34 = (bf16[256,384]{1,0:T(8,128)(2,1)S(1)}, bf16[256,384]{1,0:T(8,128)(2,1)S(1)}, u32[]{:S(2)}, u32[]{:S(2)}) collective-permute-start(bf16[256,384]{1,0:T(8,128)(2,1)S(1)} %get-tuple-element.56.refs_1_), channel_id=1, source_target_pairs={{0,8},{4,12},{8,0},{12,4},{1,9},{5,13},{9,1},{13,5},{2,10},{6,14},... | collective-permute-start | bytes 589832 | tf_op jit(solution)/shard_map/ppermute | solution.py:490
  140.2 8.3 %collective-permute-start.31 = (bf16[128,768]{1,0:T(8,128)(2,1)S(1)}, bf16[128,768]{1,0:T(8,128)(2,1)S(1)}, u32[]{:S(2)}, u32[]{:S(2)}) collective-permute-start(bf16[128,768]{1,0:T(8,128)(2,1)S(1)} %convert_element_type.117), channel_id=1, source_target_pairs={{0,2},{1,3},{2,0},{3,1},{4,6},{5,7},{6,4},{7,5},{8,10},{9,11},{10,... | collective-permute-start | bytes 589832 | tf_op jit(solution)/shard_map/ppermute | solution.py:490
  148.4 10.6 %collective-permute-start.35 = (bf16[256,384]{1,0:T(8,128)(2,1)S(1)}, bf16[256,384]{1,0:T(8,128)(2,1)S(1)}, u32[]{:S(2)}, u32[]{:S(2)}) collective-permute-start(bf16[256,384]{1,0:T(8,128)(2,1)S(1)} %shard_map.218.own_ref), channel_id=1, source_target_pairs={{0,8},{4,12},{8,0},{12,4},{1,9},{5,13},{9,1},{13,5},{2,10},{6,14},... | collective-permute-start | bytes 589832 | tf_op jit(solution)/shard_map/ppermute | solution.py:490
  148.5 14.6 %collective-permute-start.32 = (f32[128,768]{1,0:T(8,128)S(1)}, f32[128,768]{1,0:T(8,128)S(1)}, u32[]{:S(2)}, u32[]{:S(2)}) collective-permute-start(f32[128,768]{1,0:T(8,128)S(1)} %add_add_fusion), channel_id=1, source_target_pairs={{0,1},{1,0},{2,3},{3,2},{4,5},{5,4},{6,7},{7,6},{8,9},{9,8},{10,11... | collective-permute-start | bytes 1179656 | tf_op jit(solution)/shard_map/ppermute | solution.py:490
  159.0 10.3 %collective-permute-start.36 = (bf16[512,384]{1,0:T(8,128)(2,1)S(1)}, bf16[512,384]{1,0:T(8,128)(2,1)S(1)}, u32[]{:S(2)}, u32[]{:S(2)}) collective-permute-start(bf16[512,384]{1,0:T(8,128)(2,1)S(1)} %shard_map.219.own_ref), channel_id=1, source_target_pairs={{0,4},{4,0},{8,12},{12,8},{1,5},{5,1},{9,13},{13,9},{2,6},{6,2},{1... | collective-permute-start | bytes 1179656 | tf_op jit(solution)/shard_map/ppermute | solution.py:490
  (37 other events, 139.4 us)

commit v4 on v3

--- a/solution.py
+++ b/solution.py
@@ -618,7 +618,13 @@
         up_groups = gather_weight(after(up_weight[0], halves[2 % packs]), 0)
         output_groups = gather_weight(after(output_weight[0], halves[2 % packs]), 1)
         down_groups = gather_weight(after(down_weight[0], halves[2 % packs]), 1)
-        others = [with_segments(1 - core_at)] + [flip(block, "tensor", 1) for block in halves[1:]]
+        others = [with_segments(1 - core_at)]
+        if packs == 4:
+            tall = halves[1].shape[0]
+            both = flip(jnp.concatenate(halves[1:3], axis=0), "tensor", 1)
+            others += [both[:tall], both[tall:], flip(halves[3], "tensor", 1)]
+        else:
+            others += [flip(block, "tensor", 1) for block in halves[1:]]
         blocks = [block for pair in zip(halves, others) for block in pair]
         pack_queries, pack_keys, pack_values, context, pack_rows, pack_segments = front(
             blocks, input_bias[0], input_groups

time: 171 us -> 167 us (0.977)
  waiting for transfers between devices: 62.4 us -> 68 us
  starting transfers between devices: 36.3 us -> 30.8 us
  other arithmetic: 13.7 us -> 10.9 us
    ppermute x40 -> x39, waiting for transfers between devices: 62.4 us -> 68 us  [flip(): return lax.ppermute(value, axis, [(i, i ^ bit) for i in range(count[axis])])]
    ppermute x40 -> x39, starting transfers between devices: 36.3 us -> 30.8 us  [flip(): return lax.ppermute(value, axis, [(i, i ^ bit) for i in range(count[axis])])]
    unnamed x90 -> x96, local copies, waits for them, and re-layouts: 8.49 us -> 7.54 us
  transfers between devices with their start and end apart: 40 -> 39, of which waited for: 18 -> 18; matrix products, arithmetic and copies ran while one was open for 10% -> 9% of each run, Pallas kernels for 18% -> 19%
where the time goes in v4:
time: 167 us
  waiting for transfers between devices  68 us (41%)
  Pallas kernels  32.2 us (19%)
  starting transfers between devices  30.8 us (18%)
  local copies, waits for them, and re-layouts  12.6 us (8%)
  other arithmetic  10.9 us (7%)
  matrix products  9.84 us (6%)
  between operations  2.35 us (1%)
    ppermute x39, waiting for transfers between devices, flip(): return lax.ppermute(value, axis, [(i, i ^ bit) for i in range(count[axis])])  68 us
    ppermute x39, starting transfers between devices, flip(): return lax.ppermute(value, axis, [(i, i ^ bit) for i in range(count[axis])])  30.8 us
    pallas_call x1, Pallas kernels, attention_back(): pl.pallas_call(functools.partial(attention_back_kernel, heads, len(blocks...  10.6 us
    pallas_call x1, Pallas kernels, probabilities(): pl.pallas_call(functools.partial(probability_kernel, heads, block), out_s...  8.15 us
    unnamed x96, local copies, waits for them, and re-layouts  7.54 us
    dot_general x8, matrix products, product_right(): lax.dot_general(left, right, (((1,), (1,)), ((), ())), preferred_element_...  4.97 us
    pallas_call x1, Pallas kernels, front(): pl.pallas_call(functools.partial(front_kernel, width // HD, packs, len(gr...  4.75 us
    dot_general x6, matrix products, product(): return jnp.dot(left, right, preferred_element_type=F32)  4.07 us
  transfers between devices with their start and end apart: 39, of which 18 were waited for; matrix products, arithmetic and copies ran while one was open for 9% of the time, Pallas kernels for 19%

profile of v4, /device:TPU:4, one launch (start us, length us, event | category | flops | bytes accessed | tf_op | source)
XLA Modules:
  0.0 166.8 jit_solution(12884884742685336393)
XLA Ops:
  0.7 1.1 constant_dynamic-slice_fusion.2
  2.7 1.6 collective-permute-start
  4.3 2.6 %collective-permute-start.1 = (bf16[144,768]{1,0:T(8,128)(2,1)S(1)}, bf16[144,768]{1,0:T(8,128)(2,1)S(1)}, u32[]{:S(2)}, u32[]{:S(2)}) collective-permute-start(bf16[144,768]{1,0:T(8,128)(2,1)S(1)} %fusion.28.refs_0_), channel_id=1, source_target_pairs={{0,8},{4,12},{8,0},{12,4},{1,9},{5,13},{9,1},{13,5},{2,10},{6,14},... | collective-permute-start | bytes 663560 | tf_op jit(solution)/shard_map/ppermute | solution.py:490
  7.9 6.7 %collective-permute-done.refs_2_ = bf16[144,768]{1,0:T(8,128)(2,1)S(1)} collective-permute-done((bf16[144,768]{1,0:T(8,128)(2,1)S(1)}, bf16[144,768]{1,0:T(8,128)(2,1)S(1)}, u32[]{:S(2)}, u32[]{:S(2)}) %collective-permute-start) | collective-permute-done | bytes 221216 | tf_op jit(solution)/shard_map/ppermute | solution.py:490
  14.5 2.4 %collective-permute-done.1.refs_4_ = bf16[144,768]{1,0:T(8,128)(2,1)S(1)} collective-permute-done((bf16[144,768]{1,0:T(8,128)(2,1)S(1)}, bf16[144,768]{1,0:T(8,128)(2,1)S(1)}, u32[]{:S(2)}, u32[]{:S(2)}) %collective-permute-start.1) | collective-permute-done | bytes 221216 | tf_op jit(solution)/shard_map/ppermute | solution.py:490
  19.7 1.5 collective-permute-start.9
  22.5 5.9 %collective-permute-done.3.refs_6_ = bf16[144,768]{1,0:T(8,128)(2,1)S(1)} collective-permute-done((bf16[144,768]{1,0:T(8,128)(2,1)S(1)}, bf16[144,768]{1,0:T(8,128)(2,1)S(1)}, u32[]{:S(2)}, u32[]{:S(2)}) %collective-permute-start.3) | collective-permute-done | bytes 221216 | tf_op jit(solution)/shard_map/ppermute | solution.py:490
  29.0 1.4 collective-permute-done.4.refs_7_
  30.5 4.7 %shard_map.203 = (bf16[1024,192]{1,0:T(8,128)(2,1)S(1)}, bf16[1024,192]{1,0:T(8,128)(2,1)S(1)}, bf16[1024,192]{1,0:T(8,128)(2,1)S(1)}, bf16[256,192]{1,0:T(8,128...) custom-call(bf16[144,768]{1,0:T(8,128)(2,1)S(1)} %fusion.28.refs_0_, ...), custom_call_target="tpu_custom_call" | custom-call | tf_op jit(solution)/shard_map/pallas_call | solution.py:122
  35.2 1.3 copy-done.1
  39.1 1.1 fusion.18.refs_0_.first_ref
  40.1 1.6 collective-permute-start.8
  42.7 8.1 %shard_map.204 = (bf16[3,1024,1024]{2,1,0:T(8,128)(2,1)}, f32[1,128]{1,0:T(1,128)S(1)}) custom-call(bf16[1024,192]{1,0:T(8,128)(2,1)S(1)} %copy-done.12, bf16[1024,192]{1,0:T(8,128)(2,1)S(1)} %copy-done.15, f32[1,1024]{1,0:T(1,128)S(1)} %get-tuple-element.42.row_ref, bf16[128,768]{1,0:T(8,128)(2,1)S(1)} %fusion.18.refs_0_.first_ref, ...), custom_call_target="tpu_custom_call" | custom-call | tf_op jit(solution)/shard_map/pallas_call | solution.py:171
  51.6 1.4 collective-permute-done.11
  53.4 1.5 multiply_convert_fusion
  54.9 1.4 fusion.65
  57.0 1.5 collective-permute-start.14
  60.0 4.2 %collective-permute-done.14.refs_0_.left_pair = bf16[256,384]{1,0:T(8,128)(2,1)S(1)} collective-permute-done((bf16[256,384]{1,0:T(8,128)(2,1)S(1)}, bf16[256,384]{1,0:T(8,128)(2,1)S(1)}, u32[]{:S(2)}, u32[]{:S(2)}) %collective-permute-start.14) | collective-permute-done | bytes 196640 | tf_op jit(solution)/shard_map/ppermute | solution.py:490
  64.2 1.4 collective-permute-done.13.second_ref
  66.9 1.4 collective-permute-done.16
  68.7 1.6 fusion.53
  70.3 1.4 fusion.67
  73.8 1.3 collective-permute-start.19
  75.2 1.1 fusion.12.refs_0_.first_ref._
  76.9 1.1 maximum_select_fusion.2
  78.0 1.2 shard_map.207
  80.2 4.7 %collective-permute-done.19.refs_1_.right_pair = bf16[256,768]{1,0:T(8,128)(2,1)S(1)} collective-permute-done((bf16[256,768]{1,0:T(8,128)(2,1)S(1)}, bf16[256,768]{1,0:T(8,128)(2,1)S(1)}, u32[]{:S(2)}, u32[]{:S(2)}) %collective-permute-start.19) | collective-permute-done | bytes 393248 | tf_op jit(solution)/shard_map/ppermute | solution.py:490
  86.2 1.4 collective-permute-start.24
  87.6 1.2 shard_map.212
  89.8 2.6 %collective-permute-start.22 = (bf16[256,192]{1,0:T(8,128)(2,1)S(1)}, bf16[256,192]{1,0:T(8,128)(2,1)S(1)}, u32[]{:S(2)}, u32[]{:S(2)}) collective-permute-start(bf16[256,192]{1,0:T(8,128)(2,1)S(1)} %fusion.2._.refs_1_.refs_0_), channel_id=1, source_target_pairs={{0,8},{4,12},{8,0},{12,4},{1,9},{5,13},{9,1},{13,5},{2,10},{6,14},... | collective-permute-start | bytes 294920 | tf_op jit(solution)/shard_map/ppermute | solution.py:490
  93.0 1.1 collective-permute-done.25
  95.3 4.3 %collective-permute-done.22.refs_2_ = bf16[256,192]{1,0:T(8,128)(2,1)S(1)} collective-permute-done((bf16[256,192]{1,0:T(8,128)(2,1)S(1)}, bf16[256,192]{1,0:T(8,128)(2,1)S(1)}, u32[]{:S(2)}, u32[]{:S(2)}) %collective-permute-start.22) | collective-permute-done | bytes 98336 | tf_op jit(solution)/shard_map/ppermute | solution.py:490
  99.6 3.3 %collective-permute-start.23 = (bf16[256,192]{1,0:T(8,128)(2,1)S(1)}, bf16[256,192]{1,0:T(8,128)(2,1)S(1)}, u32[]{:S(2)}, u32[]{:S(2)}) collective-permute-start(bf16[256,192]{1,0:T(8,128)(2,1)S(1)} %collective-permute-done.22.refs_2_), channel_id=1, source_target_pairs={{0,4},{4,0},{8,12},{12,8},{1,5},{5,1},{9,13},{13,9},{2,6},{6,2},{1... | collective-permute-start | bytes 294920 | tf_op jit(solution)/shard_map/ppermute | solution.py:490
  103.1 1.2 copy-done.10
  106.6 1.3 shard_map.211
  107.9 2.5 %collective-permute-start.29 = (bf16[512,384]{1,0:T(8,128)(2,1)S(1)}, bf16[512,384]{1,0:T(8,128)(2,1)S(1)}, u32[]{:S(2)}, u32[]{:S(2)}) collective-permute-start(bf16[512,384]{1,0:T(8,128)(2,1)S(1)} %get-tuple-element.50.refs_4_), channel_id=1, source_target_pairs={{0,4},{4,0},{8,12},{12,8},{1,5},{5,1},{9,13},{13,9},{2,6},{6,2},{1... | collective-permute-start | bytes 1179656 | tf_op jit(solution)/shard_map/ppermute | solution.py:490
  110.4 10.6 %shard_map.214 = (bf16[1024,576]{1,0:T(8,128)(2,1)S(1)}, f32[2,192]{1,0:T(2,128)S(1)}) custom-call(bf16[3,1024,1024]{2,1,0:T(8,128)(2,1)} %get-tuple-element.45.a_hbm, bf16[1024,192]{1,0:T(8,128)(2,1)S(1)} %copy-done.13, bf16[1024,192]{1,0:T(8,128)(2,1)S(1)} %copy-done.16, bf16[1024,192]{1,0:T(8,128)(2,1)S(1)} %copy-done.20, ...), custom_call_target="tpu_custom_call" | custom-call | flops 10000000000 | bytes 10000000 | tf_op jit(solution)/shard_map/pallas_call | solution.py:222
  123.3 6.4 %collective-permute-done.37.other_ref = bf16[96,768]{1,0:T(8,128)(2,1)S(1)} collective-permute-done((bf16[96,768]{1,0:T(8,128)(2,1)S(1)}, bf16[96,768]{1,0:T(8,128)(2,1)S(1)}, u32[]{:S(2)}, u32[]{:S(2)}) %collective-permute-start.37) | collective-permute-done | bytes 147488 | tf_op jit(solution)/shard_map/ppermute | solution.py:490
  129.9 1.2 copy-done.2
  131.9 1.3 collective-permute-start.32
  133.2 1.7 %collective-permute-start.33 = (bf16[256,384]{1,0:T(8,128)(2,1)S(1)}, bf16[256,384]{1,0:T(8,128)(2,1)S(1)}, u32[]{:S(2)}, u32[]{:S(2)}) collective-permute-start(bf16[256,384]{1,0:T(8,128)(2,1)S(1)} %get-tuple-element.56.refs_1_), channel_id=1, source_target_pairs={{0,8},{4,12},{8,0},{12,4},{1,9},{5,13},{9,1},{13,5},{2,10},{6,14},... | collective-permute-start | bytes 589832 | tf_op jit(solution)/shard_map/ppermute | solution.py:490
  135.6 2.5 %collective-permute-done.38.other_ref = bf16[192,768]{1,0:T(8,128)(2,1)S(1)} collective-permute-done((bf16[192,768]{1,0:T(8,128)(2,1)S(1)}, bf16[192,768]{1,0:T(8,128)(2,1)S(1)}, u32[]{:S(2)}, u32[]{:S(2)}) %collective-permute-start.38) | collective-permute-done | bytes 294944 | tf_op jit(solution)/shard_map/ppermute | solution.py:490
  138.1 1.1 shard_map.223
  139.2 4.6 %collective-permute-done.33.other_ref = bf16[256,384]{1,0:T(8,128)(2,1)S(1)} collective-permute-done((bf16[256,384]{1,0:T(8,128)(2,1)S(1)}, bf16[256,384]{1,0:T(8,128)(2,1)S(1)}, u32[]{:S(2)}, u32[]{:S(2)}) %collective-permute-start.33) | collective-permute-done | bytes 196640 | tf_op jit(solution)/shard_map/ppermute | solution.py:490
  144.1 10.4 %collective-permute-done.34.other_ref = bf16[256,384]{1,0:T(8,128)(2,1)S(1)} collective-permute-done((bf16[256,384]{1,0:T(8,128)(2,1)S(1)}, bf16[256,384]{1,0:T(8,128)(2,1)S(1)}, u32[]{:S(2)}, u32[]{:S(2)}) %collective-permute-start.34) | collective-permute-done | bytes 196640 | tf_op jit(solution)/shard_map/ppermute | solution.py:490
  155.4 1.2 copy.39
  158.3 7.3 %collective-permute-done.35.other_ref = bf16[512,384]{1,0:T(8,128)(2,1)S(1)} collective-permute-done((bf16[512,384]{1,0:T(8,128)(2,1)S(1)}, bf16[512,384]{1,0:T(8,128)(2,1)S(1)}, u32[]{:S(2)}, u32[]{:S(2)}) %collective-permute-start.35) | collective-permute-done | bytes 393248 | tf_op jit(solution)/shard_map/ppermute | solution.py:490
  165.6 1.2 shard_map.220
  (230 shorter events, 30.8 us)
Async XLA Ops:
  2.7 15.5 %copy-start.43 = (bf16[1,192,384]{2,1,0:T(8,128)(2,1)S(1)}, bf16[1,192,384]{2,1,0:T(8,128)(2,1)}, u32[]{:S(2)}) copy-start(bf16[1,192,384]{2,1,0:T(8,128)(2,1)} %param.16) | copy-start | bytes 442372
  2.7 11.9 %collective-permute-start = (bf16[144,768]{1,0:T(8,128)(2,1)S(1)}, bf16[144,768]{1,0:T(8,128)(2,1)S(1)}, u32[]{:S(2)}, u32[]{:S(2)}) collective-permute-start(bf16[144,768]{1,0:T(8,128)(2,1)S(1)} %fusion.28.refs_0_), channel_id=1, source_target_pairs={{0,4},{4,0},{8,12},{12,8},{1,5},{5,1},{9,13},{13,9},{2,6},{6,2},{1... | collective-permute-start | bytes 663560 | tf_op jit(solution)/shard_map/ppermute | solution.py:490
  4.3 12.6 %collective-permute-start.1 = (bf16[144,768]{1,0:T(8,128)(2,1)S(1)}, bf16[144,768]{1,0:T(8,128)(2,1)S(1)}, u32[]{:S(2)}, u32[]{:S(2)}) collective-permute-start(bf16[144,768]{1,0:T(8,128)(2,1)S(1)} %fusion.28.refs_0_), channel_id=1, source_target_pairs={{0,8},{4,12},{8,0},{12,4},{1,9},{5,13},{9,1},{13,5},{2,10},{6,14},... | collective-permute-start | bytes 663560 | tf_op jit(solution)/shard_map/ppermute | solution.py:490
  6.9 11.9 %copy-start.38 = (bf16[1,384,768]{2,1,0:T(8,128)(2,1)S(1)}, bf16[1,384,768]{2,1,0:T(8,128)(2,1)}, u32[]{:S(2)}) copy-start(bf16[1,384,768]{2,1,0:T(8,128)(2,1)} %param.20) | copy-start | bytes 1769476
  7.2 21.8 %collective-permute-start.5 = (bf16[384,576]{1,0:T(8,128)(2,1)S(1)}, bf16[384,576]{1,0:T(8,128)(2,1)S(1)}, u32[]{:S(2)}, u32[]{:S(2)}) collective-permute-start(bf16[384,576]{1,0:T(8,128)(2,1)S(1)} %copy.35.refs_9_), channel_id=1, source_target_pairs={{0,16},{16,0},{1,17},{17,1},{2,18},{18,2},{3,19},{19,3},{4,20},{20... | collective-permute-start | bytes 1327112 | tf_op jit(solution)/shard_map/ppermute | solution.py:490
  7.8 13.8 %copy-start.39 = (bf16[1,768,384]{2,1,0:T(8,128)(2,1)S(1)}, bf16[1,768,384]{2,1,0:T(8,128)(2,1)}, u32[]{:S(2)}) copy-start(bf16[1,768,384]{2,1,0:T(8,128)(2,1)} %param.22) | copy-start | bytes 1769476
  16.9 12.0 %collective-permute-start.2 = (bf16[288,768]{1,0:T(8,128)(2,1)S(1)}, bf16[288,768]{1,0:T(8,128)(2,1)S(1)}, u32[]{:S(2)}, u32[]{:S(2)}) collective-permute-start(bf16[288,768]{1,0:T(8,128)(2,1)S(1)} %pad_maximum_fusion.2), channel_id=1, source_target_pairs={{0,1},{1,0},{2,3},{3,2},{4,5},{5,4},{6,7},{7,6},{8,9},{9,8},{10,11... | collective-permute-start | bytes 1327112 | tf_op jit(solution)/shard_map/ppermute | solution.py:490
  18.2 18.2 %copy-start.32 = (bf16[192,384]{1,0:T(8,128)(2,1)}, bf16[192,384]{1,0:T(8,128)(2,1)S(1)}, u32[]{:S(2)}) copy-start(bf16[192,384]{1,0:T(8,128)(2,1)S(1)} %add_bitcast_fusion.2) | copy-start | bytes 442372
  18.2 18.5 %collective-permute-start.6 = (bf16[192,384]{1,0:T(8,128)(2,1)S(1)}, bf16[192,384]{1,0:T(8,128)(2,1)S(1)}, u32[]{:S(2)}, u32[]{:S(2)}) collective-permute-start(bf16[192,384]{1,0:T(8,128)(2,1)S(1)} %add_bitcast_fusion.2), channel_id=1, source_target_pairs={{0,16},{16,0},{1,17},{17,1},{2,18},{18,2},{3,19},{19,3},{4,20},{20... | collective-permute-start | bytes 442376 | tf_op jit(solution)/shard_map/ppermute | solution.py:490
  19.7 10.8 %copy-start.18 = (f32[1,2,192]{2,1,0:T(2,128)S(1)}, f32[1,2,192]{2,1,0:T(2,128)}, u32[]{:S(2)}) copy-start(f32[1,2,192]{2,1,0:T(2,128)} %param.15) | copy-start | bytes 4612
  19.7 23.0 %collective-permute-start.9 = (bf16[384,768]{1,0:T(8,128)(2,1)}, bf16[384,768]{1,0:T(8,128)(2,1)S(1)}, u32[]{:S(2)}, u32[]{:S(2)}) collective-permute-start(bf16[384,768]{1,0:T(8,128)(2,1)} %add_bitcast_fusion.1), channel_id=1, source_target_pairs={{0,16},{16,0},{1,17},{17,1},{2,18},{18,2},{3,19},{19,3},{4,20},{20... | collective-permute-start | bytes 1769480 | tf_op jit(solution)/shard_map/ppermute | solution.py:490
  21.2 7.3 %collective-permute-start.3 = (bf16[144,768]{1,0:T(8,128)(2,1)S(1)}, bf16[144,768]{1,0:T(8,128)(2,1)S(1)}, u32[]{:S(2)}, u32[]{:S(2)}) collective-permute-start(bf16[144,768]{1,0:T(8,128)(2,1)S(1)} %collective-permute-done.1.refs_4_), channel_id=1, source_target_pairs={{0,4},{4,0},{8,12},{12,8},{1,5},{5,1},{9,13},{13,9},{2,6},{6,2},{1... | collective-permute-start | bytes 663560 | tf_op jit(solution)/shard_map/ppermute | solution.py:490
  28.5 22.4 %collective-permute-start.10 = (bf16[768,384]{1,0:T(8,128)(2,1)}, bf16[768,384]{1,0:T(8,128)(2,1)S(1)}, u32[]{:S(2)}, u32[]{:S(2)}) collective-permute-start(bf16[768,384]{1,0:T(8,128)(2,1)} %add_bitcast_fusion), channel_id=1, source_target_pairs={{0,16},{16,0},{1,17},{17,1},{2,18},{18,2},{3,19},{19,3},{4,20},{20... | collective-permute-start | bytes 1769480 | tf_op jit(solution)/shard_map/ppermute | solution.py:490
  29.0 1.5 collective-permute-start.4
  37.5 1.6 collective-permute-start.7
  40.1 10.8 %collective-permute-start.8 = (bf16[128,768]{1,0:T(8,128)(2,1)S(1)}, bf16[128,768]{1,0:T(8,128)(2,1)S(1)}, u32[]{:S(2)}, u32[]{:S(2)}) collective-permute-start(bf16[128,768]{1,0:T(8,128)(2,1)S(1)} %fusion.18.refs_0_.first_ref), channel_id=1, source_target_pairs={{0,2},{1,3},{2,0},{3,1},{4,6},{5,7},{6,4},{7,5},{8,10},{9,11},{10,... | collective-permute-start | bytes 589832 | tf_op jit(solution)/shard_map/ppermute | solution.py:490
  51.5 1.5 collective-permute-start.11
  56.8 1.7 %collective-permute-start.12 = (bf16[128,768]{1,0:T(8,128)(2,1)S(1)}, bf16[128,768]{1,0:T(8,128)(2,1)S(1)}, u32[]{:S(2)}, u32[]{:S(2)}) collective-permute-start(bf16[128,768]{1,0:T(8,128)(2,1)S(1)} %fusion.21), channel_id=1, source_target_pairs={{0,1},{1,0},{2,3},{3,2},{4,5},{5,4},{6,7},{7,6},{8,9},{9,8},{10,11... | collective-permute-start | bytes 589832 | tf_op jit(solution)/shard_map/ppermute | solution.py:490
  57.0 7.2 %collective-permute-start.14 = (bf16[256,384]{1,0:T(8,128)(2,1)S(1)}, bf16[256,384]{1,0:T(8,128)(2,1)S(1)}, u32[]{:S(2)}, u32[]{:S(2)}) collective-permute-start(bf16[256,384]{1,0:T(8,128)(2,1)S(1)} %get-tuple-element.112), channel_id=1, source_target_pairs={{0,16},{16,0},{1,17},{17,1},{2,18},{18,2},{3,19},{19,3},{4,20},{20... | collective-permute-start | bytes 589832 | tf_op jit(solution)/shard_map/ppermute | solution.py:490
  58.6 6.9 %collective-permute-start.13 = (bf16[128,768]{1,0:T(8,128)(2,1)S(1)}, bf16[128,768]{1,0:T(8,128)(2,1)S(1)}, u32[]{:S(2)}, u32[]{:S(2)}) collective-permute-start(bf16[128,768]{1,0:T(8,128)(2,1)S(1)} %fusion.15.first_ref), channel_id=1, source_target_pairs={{0,2},{1,3},{2,0},{3,1},{4,6},{5,7},{6,4},{7,5},{8,10},{9,11},{10,... | collective-permute-start | bytes 589832 | tf_op jit(solution)/shard_map/ppermute | solution.py:490
  66.9 1.4 collective-permute-start.16
  73.3 1.9 %collective-permute-start.17 = (bf16[128,768]{1,0:T(8,128)(2,1)S(1)}, bf16[128,768]{1,0:T(8,128)(2,1)S(1)}, u32[]{:S(2)}, u32[]{:S(2)}) collective-permute-start(bf16[128,768]{1,0:T(8,128)(2,1)S(1)} %fusion.20), channel_id=1, source_target_pairs={{0,1},{1,0},{2,3},{3,2},{4,5},{5,4},{6,7},{7,6},{8,9},{9,8},{10,11... | collective-permute-start | bytes 589832 | tf_op jit(solution)/shard_map/ppermute | solution.py:490
  73.4 3.4 %collective-permute-start.15 = (bf16[128,768]{1,0:T(8,128)(2,1)}, bf16[128,768]{1,0:T(8,128)(2,1)S(1)}, u32[]{:S(2)}, u32[]{:S(2)}) collective-permute-start(bf16[128,768]{1,0:T(8,128)(2,1)} %get-tuple-element.108), channel_id=1, source_target_pairs={{0,1},{1,0},{2,3},{3,2},{4,5},{5,4},{6,7},{7,6},{8,9},{9,8},{10,11... | collective-permute-start | bytes 589832 | tf_op jit(solution)/shard_map/ppermute | solution.py:490
  73.8 11.2 %collective-permute-start.19 = (bf16[256,768]{1,0:T(8,128)(2,1)S(1)}, bf16[256,768]{1,0:T(8,128)(2,1)S(1)}, u32[]{:S(2)}, u32[]{:S(2)}) collective-permute-start(bf16[256,768]{1,0:T(8,128)(2,1)S(1)} %get-tuple-element.105.right), channel_id=1, source_target_pairs={{0,16},{16,0},{1,17},{17,1},{2,18},{18,2},{3,19},{19,3},{4,20},{20... | collective-permute-start | bytes 1179656 | tf_op jit(solution)/shard_map/ppermute | solution.py:490
  76.2 8.7 %collective-permute-start.18 = (bf16[128,768]{1,0:T(8,128)(2,1)S(1)}, bf16[128,768]{1,0:T(8,128)(2,1)S(1)}, u32[]{:S(2)}, u32[]{:S(2)}) collective-permute-start(bf16[128,768]{1,0:T(8,128)(2,1)S(1)} %fusion.12.refs_0_.first_ref._), channel_id=1, source_target_pairs={{0,2},{1,3},{2,0},{3,1},{4,6},{5,7},{6,4},{7,5},{8,10},{9,11},{10,... | collective-permute-start | bytes 589832 | tf_op jit(solution)/shard_map/ppermute | solution.py:490
  85.4 3.9 %collective-permute-start.20 = (bf16[128,768]{1,0:T(8,128)(2,1)S(1)}, bf16[128,768]{1,0:T(8,128)(2,1)S(1)}, u32[]{:S(2)}, u32[]{:S(2)}) collective-permute-start(bf16[128,768]{1,0:T(8,128)(2,1)S(1)} %get-tuple-element.90), channel_id=1, source_target_pairs={{0,1},{1,0},{2,3},{3,2},{4,5},{5,4},{6,7},{7,6},{8,9},{9,8},{10,11... | collective-permute-start | bytes 589832 | tf_op jit(solution)/shard_map/ppermute | solution.py:490
  86.2 19.3 %collective-permute-start.24 = (bf16[768,384]{1,0:T(8,128)(2,1)}, bf16[768,384]{1,0:T(8,128)(2,1)}, u32[]{:S(2)}, u32[]{:S(2)}) collective-permute-start(bf16[768,384]{1,0:T(8,128)(2,1)} %get-tuple-element.44.refs_0_), channel_id=1, source_target_pairs={{0,16},{16,0},{1,17},{17,1},{2,18},{18,2},{3,19},{19,3},{4,20},{20... | collective-permute-start | bytes 1769480 | tf_op jit(solution)/shard_map/ppermute | solution.py:490
  88.8 14.3 %collective-permute-start.27 = (bf16[192,768]{1,0:T(8,128)(2,1)}, bf16[192,768]{1,0:T(8,128)(2,1)}, u32[]{:S(2)}, u32[]{:S(2)}) collective-permute-start(bf16[192,768]{1,0:T(8,128)(2,1)} %get-tuple-element.52), channel_id=1, source_target_pairs={{0,4},{4,0},{8,12},{12,8},{1,5},{5,1},{9,13},{13,9},{2,6},{6,2},{1... | collective-permute-start | bytes 884744 | tf_op jit(solution)/shard_map/ppermute | solution.py:490
  89.8 9.9 %collective-permute-start.22 = (bf16[256,192]{1,0:T(8,128)(2,1)S(1)}, bf16[256,192]{1,0:T(8,128)(2,1)S(1)}, u32[]{:S(2)}, u32[]{:S(2)}) collective-permute-start(bf16[256,192]{1,0:T(8,128)(2,1)S(1)} %fusion.2._.refs_1_.refs_0_), channel_id=1, source_target_pairs={{0,8},{4,12},{8,0},{12,4},{1,9},{5,13},{9,1},{13,5},{2,10},{6,14},... | collective-permute-start | bytes 294920 | tf_op jit(solution)/shard_map/ppermute | solution.py:490
  92.4 18.0 %collective-permute-start.21 = (bf16[256,192]{1,0:T(8,128)(2,1)S(1)}, bf16[256,192]{1,0:T(8,128)(2,1)}, u32[]{:S(2)}, u32[]{:S(2)}) collective-permute-start(bf16[256,192]{1,0:T(8,128)(2,1)S(1)} %fusion.2._.refs_1_.refs_0_), channel_id=1, source_target_pairs={{0,4},{4,0},{8,12},{12,8},{1,5},{5,1},{9,13},{13,9},{2,6},{6,2},{1... | collective-permute-start | bytes 294920 | tf_op jit(solution)/shard_map/ppermute | solution.py:490
  92.9 10.1 %copy-start.22 = (bf16[256,768]{1,0:T(8,128)(2,1)S(1)}, bf16[256,768]{1,0:T(8,128)(2,1)}, u32[]{:S(2)}) copy-start(bf16[256,768]{1,0:T(8,128)(2,1)} %copy-done.21) | copy-start | bytes 1179652
  92.9 10.1 %copy-start.36 = (bf16[256,384]{1,0:T(8,128)(2,1)S(1)}, bf16[256,384]{1,0:T(8,128)(2,1)}, u32[]{:S(2)}) copy-start(bf16[256,384]{1,0:T(8,128)(2,1)} %get-tuple-element.109) | copy-start | bytes 589828
  92.9 10.0 %copy-start.37 = (bf16[256,384]{1,0:T(8,128)(2,1)S(1)}, bf16[256,384]{1,0:T(8,128)(2,1)}, u32[]{:S(2)}) copy-start(bf16[256,384]{1,0:T(8,128)(2,1)} %get-tuple-element.110) | copy-start | bytes 589828
  92.9 1.3 collective-permute-start.25
  94.3 12.3 %copy-start.4 = (f32[768,384]{1,0:T(8,128)S(1)}, f32[768,384]{1,0:T(8,128)}, u32[]{:S(2)}) copy-start(f32[768,384]{1,0:T(8,128)} %copy-done.3) | copy-start | bytes 3538948
  94.6 12.0 %collective-permute-start.26 = (bf16[256,384]{1,0:T(8,128)(2,1)S(1)}, bf16[256,384]{1,0:T(8,128)(2,1)S(1)}, u32[]{:S(2)}, u32[]{:S(2)}) collective-permute-start(bf16[256,384]{1,0:T(8,128)(2,1)S(1)} %get-tuple-element.49), channel_id=1, source_target_pairs={{0,16},{16,0},{1,17},{17,1},{2,18},{18,2},{3,19},{19,3},{4,20},{20... | collective-permute-start | bytes 589832 | tf_op jit(solution)/shard_map/ppermute | solution.py:490
  99.6 6.9 %collective-permute-start.23 = (bf16[256,192]{1,0:T(8,128)(2,1)S(1)}, bf16[256,192]{1,0:T(8,128)(2,1)S(1)}, u32[]{:S(2)}, u32[]{:S(2)}) collective-permute-start(bf16[256,192]{1,0:T(8,128)(2,1)S(1)} %collective-permute-done.22.refs_2_), channel_id=1, source_target_pairs={{0,4},{4,0},{8,12},{12,8},{1,5},{5,1},{9,13},{13,9},{2,6},{6,2},{1... | collective-permute-start | bytes 294920 | tf_op jit(solution)/shard_map/ppermute | solution.py:490
  105.4 17.0 %collective-permute-start.36 = (bf16[96,768]{1,0:T(8,128)(2,1)S(1)}, bf16[96,768]{1,0:T(8,128)(2,1)S(1)}, u32[]{:S(2)}, u32[]{:S(2)}) collective-permute-start(bf16[96,768]{1,0:T(8,128)(2,1)S(1)} %get-tuple-element.53.refs_5_.refs_0_), channel_id=1, source_target_pairs={{0,8},{4,12},{8,0},{12,4},{1,9},{5,13},{9,1},{13,5},{2,10},{6,14},... | collective-permute-start | bytes 442376 | tf_op jit(solution)/shard_map/ppermute | solution.py:490
  107.9 21.9 %collective-permute-start.29 = (bf16[512,384]{1,0:T(8,128)(2,1)S(1)}, bf16[512,384]{1,0:T(8,128)(2,1)S(1)}, u32[]{:S(2)}, u32[]{:S(2)}) collective-permute-start(bf16[512,384]{1,0:T(8,128)(2,1)S(1)} %get-tuple-element.50.refs_4_), channel_id=1, source_target_pairs={{0,4},{4,0},{8,12},{12,8},{1,5},{5,1},{9,13},{13,9},{2,6},{6,2},{1... | collective-permute-start | bytes 1179656 | tf_op jit(solution)/shard_map/ppermute | solution.py:490
  122.4 7.2 %collective-permute-start.37 = (bf16[96,768]{1,0:T(8,128)(2,1)S(1)}, bf16[96,768]{1,0:T(8,128)(2,1)S(1)}, u32[]{:S(2)}, u32[]{:S(2)}) collective-permute-start(bf16[96,768]{1,0:T(8,128)(2,1)S(1)} %shard_map.221.own_ref), channel_id=1, source_target_pairs={{0,8},{4,12},{8,0},{12,4},{1,9},{5,13},{9,1},{13,5},{2,10},{6,14},... | collective-permute-start | bytes 442376 | tf_op jit(solution)/shard_map/ppermute | solution.py:490
  123.2 11.8 %collective-permute-start.28 = (bf16[128,768]{1,0:T(8,128)(2,1)S(1)}, bf16[128,768]{1,0:T(8,128)(2,1)S(1)}, u32[]{:S(2)}, u32[]{:S(2)}) collective-permute-start(bf16[128,768]{1,0:T(8,128)(2,1)S(1)} %fusion.19), channel_id=1, source_target_pairs={{0,1},{1,0},{2,3},{3,2},{4,5},{5,4},{6,7},{7,6},{8,9},{9,8},{10,11... | collective-permute-start | bytes 589832 | tf_op jit(solution)/shard_map/ppermute | solution.py:490
  129.7 8.4 %collective-permute-start.38 = (bf16[192,768]{1,0:T(8,128)(2,1)S(1)}, bf16[192,768]{1,0:T(8,128)(2,1)S(1)}, u32[]{:S(2)}, u32[]{:S(2)}) collective-permute-start(bf16[192,768]{1,0:T(8,128)(2,1)S(1)} %shard_map.222.own_ref), channel_id=1, source_target_pairs={{0,4},{4,0},{8,12},{12,8},{1,5},{5,1},{9,13},{13,9},{2,6},{6,2},{1... | collective-permute-start | bytes 884744 | tf_op jit(solution)/shard_map/ppermute | solution.py:490
  131.9 22.7 %collective-permute-start.32 = (bf16[400,576]{1,0:T(8,128)(2,1)S(1)}, bf16[400,576]{1,0:T(8,128)(2,1)S(1)}, u32[]{:S(2)}, u32[]{:S(2)}) collective-permute-start(bf16[400,576]{1,0:T(8,128)(2,1)S(1)} %shard_map.217), channel_id=1, source_target_pairs={{0,16},{16,0},{1,17},{17,1},{2,18},{18,2},{3,19},{19,3},{4,20},{20... | collective-permute-start | bytes 1382408 | tf_op jit(solution)/shard_map/ppermute | solution.py:490
  133.2 10.6 %collective-permute-start.33 = (bf16[256,384]{1,0:T(8,128)(2,1)S(1)}, bf16[256,384]{1,0:T(8,128)(2,1)S(1)}, u32[]{:S(2)}, u32[]{:S(2)}) collective-permute-start(bf16[256,384]{1,0:T(8,128)(2,1)S(1)} %get-tuple-element.56.refs_1_), channel_id=1, source_target_pairs={{0,8},{4,12},{8,0},{12,4},{1,9},{5,13},{9,1},{13,5},{2,10},{6,14},... | collective-permute-start | bytes 589832 | tf_op jit(solution)/shard_map/ppermute | solution.py:490
  135.0 8.9 %collective-permute-start.30 = (bf16[128,768]{1,0:T(8,128)(2,1)S(1)}, bf16[128,768]{1,0:T(8,128)(2,1)S(1)}, u32[]{:S(2)}, u32[]{:S(2)}) collective-permute-start(bf16[128,768]{1,0:T(8,128)(2,1)S(1)} %convert_element_type.117), channel_id=1, source_target_pairs={{0,2},{1,3},{2,0},{3,1},{4,6},{5,7},{6,4},{7,5},{8,10},{9,11},{10,... | collective-permute-start | bytes 589832 | tf_op jit(solution)/shard_map/ppermute | solution.py:490
  143.9 10.6 %collective-permute-start.34 = (bf16[256,384]{1,0:T(8,128)(2,1)S(1)}, bf16[256,384]{1,0:T(8,128)(2,1)S(1)}, u32[]{:S(2)}, u32[]{:S(2)}) collective-permute-start(bf16[256,384]{1,0:T(8,128)(2,1)S(1)} %shard_map.218.own_ref), channel_id=1, source_target_pairs={{0,8},{4,12},{8,0},{12,4},{1,9},{5,13},{9,1},{13,5},{2,10},{6,14},... | collective-permute-start | bytes 589832 | tf_op jit(solution)/shard_map/ppermute | solution.py:490
  144.0 13.2 %collective-permute-start.31 = (f32[128,768]{1,0:T(8,128)S(1)}, f32[128,768]{1,0:T(8,128)S(1)}, u32[]{:S(2)}, u32[]{:S(2)}) collective-permute-start(f32[128,768]{1,0:T(8,128)S(1)} %add_add_fusion), channel_id=1, source_target_pairs={{0,1},{1,0},{2,3},{3,2},{4,5},{5,4},{6,7},{7,6},{8,9},{9,8},{10,11... | collective-permute-start | bytes 1179656 | tf_op jit(solution)/shard_map/ppermute | solution.py:490
  154.5 11.1 %collective-permute-start.35 = (bf16[512,384]{1,0:T(8,128)(2,1)S(1)}, bf16[512,384]{1,0:T(8,128)(2,1)S(1)}, u32[]{:S(2)}, u32[]{:S(2)}) collective-permute-start(bf16[512,384]{1,0:T(8,128)(2,1)S(1)} %shard_map.219.own_ref), channel_id=1, source_target_pairs={{0,4},{4,0},{8,12},{12,8},{1,5},{5,1},{9,13},{13,9},{2,6},{6,2},{1... | collective-permute-start | bytes 1179656 | tf_op jit(solution)/shard_map/ppermute | solution.py:490
  (39 other events, 135.4 us)

commit v5 on v4

--- a/solution.py
+++ b/solution.py
@@ -93,7 +93,7 @@
                 x_ref[pl.ds(at, half), step:] = jnp.where(first, right, left)
             else:
                 x_ref[pl.ds(at, half)] = block[:half]
-            row_ref[:, pl.ds(at, half)] = block[half : half + 1, :half].astype(F32)
+            row_ref[:, pl.ds(at, half)] = block[half : half + 16, :half].astype(F32)[:1]
     for number, (out_ref, bias) in enumerate(((q_ref, 0), (k_ref, None), (v_ref, 1))):
         total = None
         for group in range(groups):
@@ -294,8 +294,9 @@
     sent_ref = refs[-1]
     step = left.shape[1] // 2
     sent_ref[:step] = product_left(left[:, step:], right[...]).astype(BF)
+    below = jnp.concatenate([sums[...], jnp.zeros((14, sums.shape[1]), F32)], axis=0)
     sent_ref[step:] = jnp.zeros_like(sent_ref[step:])
-    sent_ref[step : step + 2, : sums.shape[1]] = sums[...].astype(BF)
+    sent_ref[step:, : sums.shape[1]] = below.astype(BF)
 
 
 def sent_grad(left, right, sums, gates):

time: 167 us -> 167 us (level)
  no operation moved by 1% of the time
where the time goes in v5:
time: 167 us
  waiting for transfers between devices  68 us (41%)
  Pallas kernels  32.2 us (19%)
  starting transfers between devices  30.8 us (18%)
  local copies, waits for them, and re-layouts  12.6 us (8%)
  other arithmetic  10.9 us (7%)
  matrix products  9.84 us (6%)
  between operations  2.35 us (1%)
    ppermute x39, waiting for transfers between devices, flip(): return lax.ppermute(value, axis, [(i, i ^ bit) for i in range(count[axis])])  68 us
    ppermute x39, starting transfers between devices, flip(): return lax.ppermute(value, axis, [(i, i ^ bit) for i in range(count[axis])])  30.8 us
    pallas_call x1, Pallas kernels, attention_back(): pl.pallas_call(functools.partial(attention_back_kernel, heads, len(blocks...  10.6 us
    pallas_call x1, Pallas kernels, probabilities(): pl.pallas_call(functools.partial(probability_kernel, heads, block), out_s...  8.15 us
    unnamed x96, local copies, waits for them, and re-layouts  7.54 us
    dot_general x8, matrix products, product_right(): lax.dot_general(left, right, (((1,), (1,)), ((), ())), preferred_element_...  4.97 us
    pallas_call x1, Pallas kernels, front(): pl.pallas_call(functools.partial(front_kernel, width // HD, packs, len(gr...  4.75 us
    dot_general x6, matrix products, product(): return jnp.dot(left, right, preferred_element_type=F32)  4.07 us
  transfers between devices with their start and end apart: 39, of which 18 were waited for; matrix products, arithmetic and copies ran while one was open for 9% of the time, Pallas kernels for 19%

profile of v5, /device:TPU:4, one launch (start us, length us, event | category | flops | bytes accessed | tf_op | source)
XLA Modules:
  0.0 166.8 jit_solution(6842283109778856257)
XLA Ops:
  0.7 1.1 constant_dynamic-slice_fusion.2
  2.7 1.6 collective-permute-start
  4.3 2.6 %collective-permute-start.1 = (bf16[144,768]{1,0:T(8,128)(2,1)S(1)}, bf16[144,768]{1,0:T(8,128)(2,1)S(1)}, u32[]{:S(2)}, u32[]{:S(2)}) collective-permute-start(bf16[144,768]{1,0:T(8,128)(2,1)S(1)} %fusion.28.refs_0_), channel_id=1, source_target_pairs={{0,8},{4,12},{8,0},{12,4},{1,9},{5,13},{9,1},{13,5},{2,10},{6,14},... | collective-permute-start | bytes 663560 | tf_op jit(solution)/shard_map/ppermute | solution.py:491
  7.9 6.7 %collective-permute-done.refs_2_ = bf16[144,768]{1,0:T(8,128)(2,1)S(1)} collective-permute-done((bf16[144,768]{1,0:T(8,128)(2,1)S(1)}, bf16[144,768]{1,0:T(8,128)(2,1)S(1)}, u32[]{:S(2)}, u32[]{:S(2)}) %collective-permute-start) | collective-permute-done | bytes 221216 | tf_op jit(solution)/shard_map/ppermute | solution.py:491
  14.5 2.4 %collective-permute-done.1.refs_4_ = bf16[144,768]{1,0:T(8,128)(2,1)S(1)} collective-permute-done((bf16[144,768]{1,0:T(8,128)(2,1)S(1)}, bf16[144,768]{1,0:T(8,128)(2,1)S(1)}, u32[]{:S(2)}, u32[]{:S(2)}) %collective-permute-start.1) | collective-permute-done | bytes 221216 | tf_op jit(solution)/shard_map/ppermute | solution.py:491
  19.7 1.5 collective-permute-start.9
  22.5 5.9 %collective-permute-done.3.refs_6_ = bf16[144,768]{1,0:T(8,128)(2,1)S(1)} collective-permute-done((bf16[144,768]{1,0:T(8,128)(2,1)S(1)}, bf16[144,768]{1,0:T(8,128)(2,1)S(1)}, u32[]{:S(2)}, u32[]{:S(2)}) %collective-permute-start.3) | collective-permute-done | bytes 221216 | tf_op jit(solution)/shard_map/ppermute | solution.py:491
  29.0 1.4 collective-permute-done.4.refs_7_
  30.5 4.7 %shard_map.203 = (bf16[1024,192]{1,0:T(8,128)(2,1)S(1)}, bf16[1024,192]{1,0:T(8,128)(2,1)S(1)}, bf16[1024,192]{1,0:T(8,128)(2,1)S(1)}, bf16[256,192]{1,0:T(8,128...) custom-call(bf16[144,768]{1,0:T(8,128)(2,1)S(1)} %fusion.28.refs_0_, ...), custom_call_target="tpu_custom_call" | custom-call | tf_op jit(solution)/shard_map/pallas_call | solution.py:122
  35.2 1.3 copy-done.1
  39.1 1.1 fusion.18.refs_0_.first_ref
  40.1 1.6 collective-permute-start.8
  42.7 8.1 %shard_map.204 = (bf16[3,1024,1024]{2,1,0:T(8,128)(2,1)}, f32[1,128]{1,0:T(1,128)S(1)}) custom-call(bf16[1024,192]{1,0:T(8,128)(2,1)S(1)} %copy-done.12, bf16[1024,192]{1,0:T(8,128)(2,1)S(1)} %copy-done.15, f32[1,1024]{1,0:T(1,128)S(1)} %get-tuple-element.42.row_ref, bf16[128,768]{1,0:T(8,128)(2,1)S(1)} %fusion.18.refs_0_.first_ref, ...), custom_call_target="tpu_custom_call" | custom-call | tf_op jit(solution)/shard_map/pallas_call | solution.py:171
  51.6 1.4 collective-permute-done.11
  53.4 1.5 multiply_convert_fusion
  54.9 1.4 fusion.65
  57.0 1.5 collective-permute-start.14
  60.0 4.2 %collective-permute-done.14.refs_0_.left_pair = bf16[256,384]{1,0:T(8,128)(2,1)S(1)} collective-permute-done((bf16[256,384]{1,0:T(8,128)(2,1)S(1)}, bf16[256,384]{1,0:T(8,128)(2,1)S(1)}, u32[]{:S(2)}, u32[]{:S(2)}) %collective-permute-start.14) | collective-permute-done | bytes 196640 | tf_op jit(solution)/shard_map/ppermute | solution.py:491
  64.2 1.4 collective-permute-done.13.second_ref
  66.9 1.4 collective-permute-done.16
  68.7 1.6 fusion.53
  70.3 1.4 fusion.67
  73.8 1.3 collective-permute-start.19
  75.2 1.1 fusion.12.refs_0_.first_ref._
  76.9 1.1 maximum_select_fusion.2
  78.0 1.2 shard_map.207
  80.2 4.7 %collective-permute-done.19.refs_1_.right_pair = bf16[256,768]{1,0:T(8,128)(2,1)S(1)} collective-permute-done((bf16[256,768]{1,0:T(8,128)(2,1)S(1)}, bf16[256,768]{1,0:T(8,128)(2,1)S(1)}, u32[]{:S(2)}, u32[]{:S(2)}) %collective-permute-start.19) | collective-permute-done | bytes 393248 | tf_op jit(solution)/shard_map/ppermute | solution.py:491
  86.2 1.4 collective-permute-start.24
  87.6 1.2 shard_map.212
  89.8 2.6 %collective-permute-start.22 = (bf16[256,192]{1,0:T(8,128)(2,1)S(1)}, bf16[256,192]{1,0:T(8,128)(2,1)S(1)}, u32[]{:S(2)}, u32[]{:S(2)}) collective-permute-start(bf16[256,192]{1,0:T(8,128)(2,1)S(1)} %fusion.2._.refs_1_.refs_0_), channel_id=1, source_target_pairs={{0,8},{4,12},{8,0},{12,4},{1,9},{5,13},{9,1},{13,5},{2,10},{6,14},... | collective-permute-start | bytes 294920 | tf_op jit(solution)/shard_map/ppermute | solution.py:491
  93.0 1.1 collective-permute-done.25
  95.3 4.3 %collective-permute-done.22.refs_2_ = bf16[256,192]{1,0:T(8,128)(2,1)S(1)} collective-permute-done((bf16[256,192]{1,0:T(8,128)(2,1)S(1)}, bf16[256,192]{1,0:T(8,128)(2,1)S(1)}, u32[]{:S(2)}, u32[]{:S(2)}) %collective-permute-start.22) | collective-permute-done | bytes 98336 | tf_op jit(solution)/shard_map/ppermute | solution.py:491
  99.6 3.3 %collective-permute-start.23 = (bf16[256,192]{1,0:T(8,128)(2,1)S(1)}, bf16[256,192]{1,0:T(8,128)(2,1)S(1)}, u32[]{:S(2)}, u32[]{:S(2)}) collective-permute-start(bf16[256,192]{1,0:T(8,128)(2,1)S(1)} %collective-permute-done.22.refs_2_), channel_id=1, source_target_pairs={{0,4},{4,0},{8,12},{12,8},{1,5},{5,1},{9,13},{13,9},{2,6},{6,2},{1... | collective-permute-start | bytes 294920 | tf_op jit(solution)/shard_map/ppermute | solution.py:491
  103.1 1.2 copy-done.10
  106.6 1.3 shard_map.211
  107.9 2.5 %collective-permute-start.29 = (bf16[512,384]{1,0:T(8,128)(2,1)S(1)}, bf16[512,384]{1,0:T(8,128)(2,1)S(1)}, u32[]{:S(2)}, u32[]{:S(2)}) collective-permute-start(bf16[512,384]{1,0:T(8,128)(2,1)S(1)} %get-tuple-element.50.refs_4_), channel_id=1, source_target_pairs={{0,4},{4,0},{8,12},{12,8},{1,5},{5,1},{9,13},{13,9},{2,6},{6,2},{1... | collective-permute-start | bytes 1179656 | tf_op jit(solution)/shard_map/ppermute | solution.py:491
  110.4 10.6 %shard_map.214 = (bf16[1024,576]{1,0:T(8,128)(2,1)S(1)}, f32[2,192]{1,0:T(2,128)S(1)}) custom-call(bf16[3,1024,1024]{2,1,0:T(8,128)(2,1)} %get-tuple-element.45.a_hbm, bf16[1024,192]{1,0:T(8,128)(2,1)S(1)} %copy-done.13, bf16[1024,192]{1,0:T(8,128)(2,1)S(1)} %copy-done.16, bf16[1024,192]{1,0:T(8,128)(2,1)S(1)} %copy-done.20, ...), custom_call_target="tpu_custom_call" | custom-call | flops 10000000000 | bytes 10000000 | tf_op jit(solution)/shard_map/pallas_call | solution.py:222
  123.3 6.4 %collective-permute-done.37.other_ref = bf16[96,768]{1,0:T(8,128)(2,1)S(1)} collective-permute-done((bf16[96,768]{1,0:T(8,128)(2,1)S(1)}, bf16[96,768]{1,0:T(8,128)(2,1)S(1)}, u32[]{:S(2)}, u32[]{:S(2)}) %collective-permute-start.37) | collective-permute-done | bytes 147488 | tf_op jit(solution)/shard_map/ppermute | solution.py:491
  129.9 1.2 copy-done.2
  131.9 1.3 collective-permute-start.32
  133.2 1.7 %collective-permute-start.33 = (bf16[256,384]{1,0:T(8,128)(2,1)S(1)}, bf16[256,384]{1,0:T(8,128)(2,1)S(1)}, u32[]{:S(2)}, u32[]{:S(2)}) collective-permute-start(bf16[256,384]{1,0:T(8,128)(2,1)S(1)} %get-tuple-element.56.refs_1_), channel_id=1, source_target_pairs={{0,8},{4,12},{8,0},{12,4},{1,9},{5,13},{9,1},{13,5},{2,10},{6,14},... | collective-permute-start | bytes 589832 | tf_op jit(solution)/shard_map/ppermute | solution.py:491
  135.6 2.5 %collective-permute-done.38.other_ref = bf16[192,768]{1,0:T(8,128)(2,1)S(1)} collective-permute-done((bf16[192,768]{1,0:T(8,128)(2,1)S(1)}, bf16[192,768]{1,0:T(8,128)(2,1)S(1)}, u32[]{:S(2)}, u32[]{:S(2)}) %collective-permute-start.38) | collective-permute-done | bytes 294944 | tf_op jit(solution)/shard_map/ppermute | solution.py:491
  138.1 1.1 shard_map.223
  139.2 4.6 %collective-permute-done.33.other_ref = bf16[256,384]{1,0:T(8,128)(2,1)S(1)} collective-permute-done((bf16[256,384]{1,0:T(8,128)(2,1)S(1)}, bf16[256,384]{1,0:T(8,128)(2,1)S(1)}, u32[]{:S(2)}, u32[]{:S(2)}) %collective-permute-start.33) | collective-permute-done | bytes 196640 | tf_op jit(solution)/shard_map/ppermute | solution.py:491
  144.1 10.4 %collective-permute-done.34.other_ref = bf16[256,384]{1,0:T(8,128)(2,1)S(1)} collective-permute-done((bf16[256,384]{1,0:T(8,128)(2,1)S(1)}, bf16[256,384]{1,0:T(8,128)(2,1)S(1)}, u32[]{:S(2)}, u32[]{:S(2)}) %collective-permute-start.34) | collective-permute-done | bytes 196640 | tf_op jit(solution)/shard_map/ppermute | solution.py:491
  155.4 1.2 copy.39
  158.3 7.3 %collective-permute-done.35.other_ref = bf16[512,384]{1,0:T(8,128)(2,1)S(1)} collective-permute-done((bf16[512,384]{1,0:T(8,128)(2,1)S(1)}, bf16[512,384]{1,0:T(8,128)(2,1)S(1)}, u32[]{:S(2)}, u32[]{:S(2)}) %collective-permute-start.35) | collective-permute-done | bytes 393248 | tf_op jit(solution)/shard_map/ppermute | solution.py:491
  165.6 1.2 shard_map.220
  (230 shorter events, 30.8 us)
Async XLA Ops:
  2.7 15.5 %copy-start.43 = (bf16[1,192,384]{2,1,0:T(8,128)(2,1)S(1)}, bf16[1,192,384]{2,1,0:T(8,128)(2,1)}, u32[]{:S(2)}) copy-start(bf16[1,192,384]{2,1,0:T(8,128)(2,1)} %param.16) | copy-start | bytes 442372
  2.7 11.9 %collective-permute-start = (bf16[144,768]{1,0:T(8,128)(2,1)S(1)}, bf16[144,768]{1,0:T(8,128)(2,1)S(1)}, u32[]{:S(2)}, u32[]{:S(2)}) collective-permute-start(bf16[144,768]{1,0:T(8,128)(2,1)S(1)} %fusion.28.refs_0_), channel_id=1, source_target_pairs={{0,4},{4,0},{8,12},{12,8},{1,5},{5,1},{9,13},{13,9},{2,6},{6,2},{1... | collective-permute-start | bytes 663560 | tf_op jit(solution)/shard_map/ppermute | solution.py:491
  4.3 12.6 %collective-permute-start.1 = (bf16[144,768]{1,0:T(8,128)(2,1)S(1)}, bf16[144,768]{1,0:T(8,128)(2,1)S(1)}, u32[]{:S(2)}, u32[]{:S(2)}) collective-permute-start(bf16[144,768]{1,0:T(8,128)(2,1)S(1)} %fusion.28.refs_0_), channel_id=1, source_target_pairs={{0,8},{4,12},{8,0},{12,4},{1,9},{5,13},{9,1},{13,5},{2,10},{6,14},... | collective-permute-start | bytes 663560 | tf_op jit(solution)/shard_map/ppermute | solution.py:491
  6.9 11.9 %copy-start.38 = (bf16[1,384,768]{2,1,0:T(8,128)(2,1)S(1)}, bf16[1,384,768]{2,1,0:T(8,128)(2,1)}, u32[]{:S(2)}) copy-start(bf16[1,384,768]{2,1,0:T(8,128)(2,1)} %param.20) | copy-start | bytes 1769476
  7.2 21.8 %collective-permute-start.5 = (bf16[384,576]{1,0:T(8,128)(2,1)S(1)}, bf16[384,576]{1,0:T(8,128)(2,1)S(1)}, u32[]{:S(2)}, u32[]{:S(2)}) collective-permute-start(bf16[384,576]{1,0:T(8,128)(2,1)S(1)} %copy.35.refs_9_), channel_id=1, source_target_pairs={{0,16},{16,0},{1,17},{17,1},{2,18},{18,2},{3,19},{19,3},{4,20},{20... | collective-permute-start | bytes 1327112 | tf_op jit(solution)/shard_map/ppermute | solution.py:491
  7.8 13.8 %copy-start.39 = (bf16[1,768,384]{2,1,0:T(8,128)(2,1)S(1)}, bf16[1,768,384]{2,1,0:T(8,128)(2,1)}, u32[]{:S(2)}) copy-start(bf16[1,768,384]{2,1,0:T(8,128)(2,1)} %param.22) | copy-start | bytes 1769476
  16.9 12.0 %collective-permute-start.2 = (bf16[288,768]{1,0:T(8,128)(2,1)S(1)}, bf16[288,768]{1,0:T(8,128)(2,1)S(1)}, u32[]{:S(2)}, u32[]{:S(2)}) collective-permute-start(bf16[288,768]{1,0:T(8,128)(2,1)S(1)} %pad_maximum_fusion.2), channel_id=1, source_target_pairs={{0,1},{1,0},{2,3},{3,2},{4,5},{5,4},{6,7},{7,6},{8,9},{9,8},{10,11... | collective-permute-start | bytes 1327112 | tf_op jit(solution)/shard_map/ppermute | solution.py:491
  18.2 18.2 %copy-start.32 = (bf16[192,384]{1,0:T(8,128)(2,1)}, bf16[192,384]{1,0:T(8,128)(2,1)S(1)}, u32[]{:S(2)}) copy-start(bf16[192,384]{1,0:T(8,128)(2,1)S(1)} %add_bitcast_fusion.2) | copy-start | bytes 442372
  18.2 18.5 %collective-permute-start.6 = (bf16[192,384]{1,0:T(8,128)(2,1)S(1)}, bf16[192,384]{1,0:T(8,128)(2,1)S(1)}, u32[]{:S(2)}, u32[]{:S(2)}) collective-permute-start(bf16[192,384]{1,0:T(8,128)(2,1)S(1)} %add_bitcast_fusion.2), channel_id=1, source_target_pairs={{0,16},{16,0},{1,17},{17,1},{2,18},{18,2},{3,19},{19,3},{4,20},{20... | collective-permute-start | bytes 442376 | tf_op jit(solution)/shard_map/ppermute | solution.py:491
  19.7 10.8 %copy-start.18 = (f32[1,2,192]{2,1,0:T(2,128)S(1)}, f32[1,2,192]{2,1,0:T(2,128)}, u32[]{:S(2)}) copy-start(f32[1,2,192]{2,1,0:T(2,128)} %param.15) | copy-start | bytes 4612
  19.7 23.0 %collective-permute-start.9 = (bf16[384,768]{1,0:T(8,128)(2,1)}, bf16[384,768]{1,0:T(8,128)(2,1)S(1)}, u32[]{:S(2)}, u32[]{:S(2)}) collective-permute-start(bf16[384,768]{1,0:T(8,128)(2,1)} %add_bitcast_fusion.1), channel_id=1, source_target_pairs={{0,16},{16,0},{1,17},{17,1},{2,18},{18,2},{3,19},{19,3},{4,20},{20... | collective-permute-start | bytes 1769480 | tf_op jit(solution)/shard_map/ppermute | solution.py:491
  21.2 7.3 %collective-permute-start.3 = (bf16[144,768]{1,0:T(8,128)(2,1)S(1)}, bf16[144,768]{1,0:T(8,128)(2,1)S(1)}, u32[]{:S(2)}, u32[]{:S(2)}) collective-permute-start(bf16[144,768]{1,0:T(8,128)(2,1)S(1)} %collective-permute-done.1.refs_4_), channel_id=1, source_target_pairs={{0,4},{4,0},{8,12},{12,8},{1,5},{5,1},{9,13},{13,9},{2,6},{6,2},{1... | collective-permute-start | bytes 663560 | tf_op jit(solution)/shard_map/ppermute | solution.py:491
  28.5 22.4 %collective-permute-start.10 = (bf16[768,384]{1,0:T(8,128)(2,1)}, bf16[768,384]{1,0:T(8,128)(2,1)S(1)}, u32[]{:S(2)}, u32[]{:S(2)}) collective-permute-start(bf16[768,384]{1,0:T(8,128)(2,1)} %add_bitcast_fusion), channel_id=1, source_target_pairs={{0,16},{16,0},{1,17},{17,1},{2,18},{18,2},{3,19},{19,3},{4,20},{20... | collective-permute-start | bytes 1769480 | tf_op jit(solution)/shard_map/ppermute | solution.py:491
  29.0 1.5 collective-permute-start.4
  37.5 1.6 collective-permute-start.7
  40.1 10.8 %collective-permute-start.8 = (bf16[128,768]{1,0:T(8,128)(2,1)S(1)}, bf16[128,768]{1,0:T(8,128)(2,1)S(1)}, u32[]{:S(2)}, u32[]{:S(2)}) collective-permute-start(bf16[128,768]{1,0:T(8,128)(2,1)S(1)} %fusion.18.refs_0_.first_ref), channel_id=1, source_target_pairs={{0,2},{1,3},{2,0},{3,1},{4,6},{5,7},{6,4},{7,5},{8,10},{9,11},{10,... | collective-permute-start | bytes 589832 | tf_op jit(solution)/shard_map/ppermute | solution.py:491
  51.5 1.5 collective-permute-start.11
  56.8 1.7 %collective-permute-start.12 = (bf16[128,768]{1,0:T(8,128)(2,1)S(1)}, bf16[128,768]{1,0:T(8,128)(2,1)S(1)}, u32[]{:S(2)}, u32[]{:S(2)}) collective-permute-start(bf16[128,768]{1,0:T(8,128)(2,1)S(1)} %fusion.21), channel_id=1, source_target_pairs={{0,1},{1,0},{2,3},{3,2},{4,5},{5,4},{6,7},{7,6},{8,9},{9,8},{10,11... | collective-permute-start | bytes 589832 | tf_op jit(solution)/shard_map/ppermute | solution.py:491
  57.0 7.2 %collective-permute-start.14 = (bf16[256,384]{1,0:T(8,128)(2,1)S(1)}, bf16[256,384]{1,0:T(8,128)(2,1)S(1)}, u32[]{:S(2)}, u32[]{:S(2)}) collective-permute-start(bf16[256,384]{1,0:T(8,128)(2,1)S(1)} %get-tuple-element.112), channel_id=1, source_target_pairs={{0,16},{16,0},{1,17},{17,1},{2,18},{18,2},{3,19},{19,3},{4,20},{20... | collective-permute-start | bytes 589832 | tf_op jit(solution)/shard_map/ppermute | solution.py:491
  58.6 6.9 %collective-permute-start.13 = (bf16[128,768]{1,0:T(8,128)(2,1)S(1)}, bf16[128,768]{1,0:T(8,128)(2,1)S(1)}, u32[]{:S(2)}, u32[]{:S(2)}) collective-permute-start(bf16[128,768]{1,0:T(8,128)(2,1)S(1)} %fusion.15.first_ref), channel_id=1, source_target_pairs={{0,2},{1,3},{2,0},{3,1},{4,6},{5,7},{6,4},{7,5},{8,10},{9,11},{10,... | collective-permute-start | bytes 589832 | tf_op jit(solution)/shard_map/ppermute | solution.py:491
  66.9 1.4 collective-permute-start.16
  73.3 1.9 %collective-permute-start.17 = (bf16[128,768]{1,0:T(8,128)(2,1)S(1)}, bf16[128,768]{1,0:T(8,128)(2,1)S(1)}, u32[]{:S(2)}, u32[]{:S(2)}) collective-permute-start(bf16[128,768]{1,0:T(8,128)(2,1)S(1)} %fusion.20), channel_id=1, source_target_pairs={{0,1},{1,0},{2,3},{3,2},{4,5},{5,4},{6,7},{7,6},{8,9},{9,8},{10,11... | collective-permute-start | bytes 589832 | tf_op jit(solution)/shard_map/ppermute | solution.py:491
  73.4 3.4 %collective-permute-start.15 = (bf16[128,768]{1,0:T(8,128)(2,1)}, bf16[128,768]{1,0:T(8,128)(2,1)S(1)}, u32[]{:S(2)}, u32[]{:S(2)}) collective-permute-start(bf16[128,768]{1,0:T(8,128)(2,1)} %get-tuple-element.108), channel_id=1, source_target_pairs={{0,1},{1,0},{2,3},{3,2},{4,5},{5,4},{6,7},{7,6},{8,9},{9,8},{10,11... | collective-permute-start | bytes 589832 | tf_op jit(solution)/shard_map/ppermute | solution.py:491
  73.8 11.2 %collective-permute-start.19 = (bf16[256,768]{1,0:T(8,128)(2,1)S(1)}, bf16[256,768]{1,0:T(8,128)(2,1)S(1)}, u32[]{:S(2)}, u32[]{:S(2)}) collective-permute-start(bf16[256,768]{1,0:T(8,128)(2,1)S(1)} %get-tuple-element.105.right), channel_id=1, source_target_pairs={{0,16},{16,0},{1,17},{17,1},{2,18},{18,2},{3,19},{19,3},{4,20},{20... | collective-permute-start | bytes 1179656 | tf_op jit(solution)/shard_map/ppermute | solution.py:491
  76.2 8.7 %collective-permute-start.18 = (bf16[128,768]{1,0:T(8,128)(2,1)S(1)}, bf16[128,768]{1,0:T(8,128)(2,1)S(1)}, u32[]{:S(2)}, u32[]{:S(2)}) collective-permute-start(bf16[128,768]{1,0:T(8,128)(2,1)S(1)} %fusion.12.refs_0_.first_ref._), channel_id=1, source_target_pairs={{0,2},{1,3},{2,0},{3,1},{4,6},{5,7},{6,4},{7,5},{8,10},{9,11},{10,... | collective-permute-start | bytes 589832 | tf_op jit(solution)/shard_map/ppermute | solution.py:491
  85.4 3.9 %collective-permute-start.20 = (bf16[128,768]{1,0:T(8,128)(2,1)S(1)}, bf16[128,768]{1,0:T(8,128)(2,1)S(1)}, u32[]{:S(2)}, u32[]{:S(2)}) collective-permute-start(bf16[128,768]{1,0:T(8,128)(2,1)S(1)} %get-tuple-element.90), channel_id=1, source_target_pairs={{0,1},{1,0},{2,3},{3,2},{4,5},{5,4},{6,7},{7,6},{8,9},{9,8},{10,11... | collective-permute-start | bytes 589832 | tf_op jit(solution)/shard_map/ppermute | solution.py:491
  86.2 19.3 %collective-permute-start.24 = (bf16[768,384]{1,0:T(8,128)(2,1)}, bf16[768,384]{1,0:T(8,128)(2,1)}, u32[]{:S(2)}, u32[]{:S(2)}) collective-permute-start(bf16[768,384]{1,0:T(8,128)(2,1)} %get-tuple-element.44.refs_0_), channel_id=1, source_target_pairs={{0,16},{16,0},{1,17},{17,1},{2,18},{18,2},{3,19},{19,3},{4,20},{20... | collective-permute-start | bytes 1769480 | tf_op jit(solution)/shard_map/ppermute | solution.py:491
  88.8 14.3 %collective-permute-start.27 = (bf16[192,768]{1,0:T(8,128)(2,1)}, bf16[192,768]{1,0:T(8,128)(2,1)}, u32[]{:S(2)}, u32[]{:S(2)}) collective-permute-start(bf16[192,768]{1,0:T(8,128)(2,1)} %get-tuple-element.52), channel_id=1, source_target_pairs={{0,4},{4,0},{8,12},{12,8},{1,5},{5,1},{9,13},{13,9},{2,6},{6,2},{1... | collective-permute-start | bytes 884744 | tf_op jit(solution)/shard_map/ppermute | solution.py:491
  89.8 9.9 %collective-permute-start.22 = (bf16[256,192]{1,0:T(8,128)(2,1)S(1)}, bf16[256,192]{1,0:T(8,128)(2,1)S(1)}, u32[]{:S(2)}, u32[]{:S(2)}) collective-permute-start(bf16[256,192]{1,0:T(8,128)(2,1)S(1)} %fusion.2._.refs_1_.refs_0_), channel_id=1, source_target_pairs={{0,8},{4,12},{8,0},{12,4},{1,9},{5,13},{9,1},{13,5},{2,10},{6,14},... | collective-permute-start | bytes 294920 | tf_op jit(solution)/shard_map/ppermute | solution.py:491
  92.4 18.0 %collective-permute-start.21 = (bf16[256,192]{1,0:T(8,128)(2,1)S(1)}, bf16[256,192]{1,0:T(8,128)(2,1)}, u32[]{:S(2)}, u32[]{:S(2)}) collective-permute-start(bf16[256,192]{1,0:T(8,128)(2,1)S(1)} %fusion.2._.refs_1_.refs_0_), channel_id=1, source_target_pairs={{0,4},{4,0},{8,12},{12,8},{1,5},{5,1},{9,13},{13,9},{2,6},{6,2},{1... | collective-permute-start | bytes 294920 | tf_op jit(solution)/shard_map/ppermute | solution.py:491
  92.9 10.1 %copy-start.22 = (bf16[256,768]{1,0:T(8,128)(2,1)S(1)}, bf16[256,768]{1,0:T(8,128)(2,1)}, u32[]{:S(2)}) copy-start(bf16[256,768]{1,0:T(8,128)(2,1)} %copy-done.21) | copy-start | bytes 1179652
  92.9 10.1 %copy-start.36 = (bf16[256,384]{1,0:T(8,128)(2,1)S(1)}, bf16[256,384]{1,0:T(8,128)(2,1)}, u32[]{:S(2)}) copy-start(bf16[256,384]{1,0:T(8,128)(2,1)} %get-tuple-element.109) | copy-start | bytes 589828
  92.9 10.0 %copy-start.37 = (bf16[256,384]{1,0:T(8,128)(2,1)S(1)}, bf16[256,384]{1,0:T(8,128)(2,1)}, u32[]{:S(2)}) copy-start(bf16[256,384]{1,0:T(8,128)(2,1)} %get-tuple-element.110) | copy-start | bytes 589828
  92.9 1.3 collective-permute-start.25
  94.3 12.3 %copy-start.4 = (f32[768,384]{1,0:T(8,128)S(1)}, f32[768,384]{1,0:T(8,128)}, u32[]{:S(2)}) copy-start(f32[768,384]{1,0:T(8,128)} %copy-done.3) | copy-start | bytes 3538948
  94.6 12.0 %collective-permute-start.26 = (bf16[256,384]{1,0:T(8,128)(2,1)S(1)}, bf16[256,384]{1,0:T(8,128)(2,1)S(1)}, u32[]{:S(2)}, u32[]{:S(2)}) collective-permute-start(bf16[256,384]{1,0:T(8,128)(2,1)S(1)} %get-tuple-element.49), channel_id=1, source_target_pairs={{0,16},{16,0},{1,17},{17,1},{2,18},{18,2},{3,19},{19,3},{4,20},{20... | collective-permute-start | bytes 589832 | tf_op jit(solution)/shard_map/ppermute | solution.py:491
  99.6 6.9 %collective-permute-start.23 = (bf16[256,192]{1,0:T(8,128)(2,1)S(1)}, bf16[256,192]{1,0:T(8,128)(2,1)S(1)}, u32[]{:S(2)}, u32[]{:S(2)}) collective-permute-start(bf16[256,192]{1,0:T(8,128)(2,1)S(1)} %collective-permute-done.22.refs_2_), channel_id=1, source_target_pairs={{0,4},{4,0},{8,12},{12,8},{1,5},{5,1},{9,13},{13,9},{2,6},{6,2},{1... | collective-permute-start | bytes 294920 | tf_op jit(solution)/shard_map/ppermute | solution.py:491
  105.4 17.0 %collective-permute-start.36 = (bf16[96,768]{1,0:T(8,128)(2,1)S(1)}, bf16[96,768]{1,0:T(8,128)(2,1)S(1)}, u32[]{:S(2)}, u32[]{:S(2)}) collective-permute-start(bf16[96,768]{1,0:T(8,128)(2,1)S(1)} %get-tuple-element.53.refs_5_.refs_0_), channel_id=1, source_target_pairs={{0,8},{4,12},{8,0},{12,4},{1,9},{5,13},{9,1},{13,5},{2,10},{6,14},... | collective-permute-start | bytes 442376 | tf_op jit(solution)/shard_map/ppermute | solution.py:491
  107.9 21.9 %collective-permute-start.29 = (bf16[512,384]{1,0:T(8,128)(2,1)S(1)}, bf16[512,384]{1,0:T(8,128)(2,1)S(1)}, u32[]{:S(2)}, u32[]{:S(2)}) collective-permute-start(bf16[512,384]{1,0:T(8,128)(2,1)S(1)} %get-tuple-element.50.refs_4_), channel_id=1, source_target_pairs={{0,4},{4,0},{8,12},{12,8},{1,5},{5,1},{9,13},{13,9},{2,6},{6,2},{1... | collective-permute-start | bytes 1179656 | tf_op jit(solution)/shard_map/ppermute | solution.py:491
  122.4 7.2 %collective-permute-start.37 = (bf16[96,768]{1,0:T(8,128)(2,1)S(1)}, bf16[96,768]{1,0:T(8,128)(2,1)S(1)}, u32[]{:S(2)}, u32[]{:S(2)}) collective-permute-start(bf16[96,768]{1,0:T(8,128)(2,1)S(1)} %shard_map.221.own_ref), channel_id=1, source_target_pairs={{0,8},{4,12},{8,0},{12,4},{1,9},{5,13},{9,1},{13,5},{2,10},{6,14},... | collective-permute-start | bytes 442376 | tf_op jit(solution)/shard_map/ppermute | solution.py:491
  123.2 11.8 %collective-permute-start.28 = (bf16[128,768]{1,0:T(8,128)(2,1)S(1)}, bf16[128,768]{1,0:T(8,128)(2,1)S(1)}, u32[]{:S(2)}, u32[]{:S(2)}) collective-permute-start(bf16[128,768]{1,0:T(8,128)(2,1)S(1)} %fusion.19), channel_id=1, source_target_pairs={{0,1},{1,0},{2,3},{3,2},{4,5},{5,4},{6,7},{7,6},{8,9},{9,8},{10,11... | collective-permute-start | bytes 589832 | tf_op jit(solution)/shard_map/ppermute | solution.py:491
  129.7 8.4 %collective-permute-start.38 = (bf16[192,768]{1,0:T(8,128)(2,1)S(1)}, bf16[192,768]{1,0:T(8,128)(2,1)S(1)}, u32[]{:S(2)}, u32[]{:S(2)}) collective-permute-start(bf16[192,768]{1,0:T(8,128)(2,1)S(1)} %shard_map.222.own_ref), channel_id=1, source_target_pairs={{0,4},{4,0},{8,12},{12,8},{1,5},{5,1},{9,13},{13,9},{2,6},{6,2},{1... | collective-permute-start | bytes 884744 | tf_op jit(solution)/shard_map/ppermute | solution.py:491
  131.9 22.7 %collective-permute-start.32 = (bf16[400,576]{1,0:T(8,128)(2,1)S(1)}, bf16[400,576]{1,0:T(8,128)(2,1)S(1)}, u32[]{:S(2)}, u32[]{:S(2)}) collective-permute-start(bf16[400,576]{1,0:T(8,128)(2,1)S(1)} %shard_map.217), channel_id=1, source_target_pairs={{0,16},{16,0},{1,17},{17,1},{2,18},{18,2},{3,19},{19,3},{4,20},{20... | collective-permute-start | bytes 1382408 | tf_op jit(solution)/shard_map/ppermute | solution.py:491
  133.2 10.6 %collective-permute-start.33 = (bf16[256,384]{1,0:T(8,128)(2,1)S(1)}, bf16[256,384]{1,0:T(8,128)(2,1)S(1)}, u32[]{:S(2)}, u32[]{:S(2)}) collective-permute-start(bf16[256,384]{1,0:T(8,128)(2,1)S(1)} %get-tuple-element.56.refs_1_), channel_id=1, source_target_pairs={{0,8},{4,12},{8,0},{12,4},{1,9},{5,13},{9,1},{13,5},{2,10},{6,14},... | collective-permute-start | bytes 589832 | tf_op jit(solution)/shard_map/ppermute | solution.py:491
  135.0 8.9 %collective-permute-start.30 = (bf16[128,768]{1,0:T(8,128)(2,1)S(1)}, bf16[128,768]{1,0:T(8,128)(2,1)S(1)}, u32[]{:S(2)}, u32[]{:S(2)}) collective-permute-start(bf16[128,768]{1,0:T(8,128)(2,1)S(1)} %convert_element_type.117), channel_id=1, source_target_pairs={{0,2},{1,3},{2,0},{3,1},{4,6},{5,7},{6,4},{7,5},{8,10},{9,11},{10,... | collective-permute-start | bytes 589832 | tf_op jit(solution)/shard_map/ppermute | solution.py:491
  143.9 10.6 %collective-permute-start.34 = (bf16[256,384]{1,0:T(8,128)(2,1)S(1)}, bf16[256,384]{1,0:T(8,128)(2,1)S(1)}, u32[]{:S(2)}, u32[]{:S(2)}) collective-permute-start(bf16[256,384]{1,0:T(8,128)(2,1)S(1)} %shard_map.218.own_ref), channel_id=1, source_target_pairs={{0,8},{4,12},{8,0},{12,4},{1,9},{5,13},{9,1},{13,5},{2,10},{6,14},... | collective-permute-start | bytes 589832 | tf_op jit(solution)/shard_map/ppermute | solution.py:491
  144.0 13.2 %collective-permute-start.31 = (f32[128,768]{1,0:T(8,128)S(1)}, f32[128,768]{1,0:T(8,128)S(1)}, u32[]{:S(2)}, u32[]{:S(2)}) collective-permute-start(f32[128,768]{1,0:T(8,128)S(1)} %add_add_fusion), channel_id=1, source_target_pairs={{0,1},{1,0},{2,3},{3,2},{4,5},{5,4},{6,7},{7,6},{8,9},{9,8},{10,11... | collective-permute-start | bytes 1179656 | tf_op jit(solution)/shard_map/ppermute | solution.py:491
  154.5 11.1 %collective-permute-start.35 = (bf16[512,384]{1,0:T(8,128)(2,1)S(1)}, bf16[512,384]{1,0:T(8,128)(2,1)S(1)}, u32[]{:S(2)}, u32[]{:S(2)}) collective-permute-start(bf16[512,384]{1,0:T(8,128)(2,1)S(1)} %shard_map.219.own_ref), channel_id=1, source_target_pairs={{0,4},{4,0},{8,12},{12,8},{1,5},{5,1},{9,13},{13,9},{2,6},{6,2},{1... | collective-permute-start | bytes 1179656 | tf_op jit(solution)/shard_map/ppermute | solution.py:491
  (39 other events, 135.4 us)
